TPU v7x, 256 devices: a whole 4x4x8 slice. The times are simulated.
256 devices in a mesh: section: 8 (over y_lo, x), dp: 8 (over z), tensor: 4 (over y_hi, core).
Axes of the slice: x: 4, y: 4 (y_hi: 2, y_lo: 2; y = y_hi * 2 + y_lo), z: 8, core: 2. Of those that a mesh axis runs over, the one named last changes fastest.
Arguments:
- vision_rows: bfloat16 [8192, 12800], P(('section', 'dp')), may hold values from -100 to 100
- vision_gain: float32 [12800], replicated, may hold values from 0.1 to 1.9
- vision_bias: float32 [12800], replicated, may hold values from -4 to 4
- proj_weight: bfloat16 [12800, 4096], P(('section', 'dp'), 'tensor'), may hold values from -0.0546875 to 0.0546875
- text_rows: bfloat16 [8192, 4096], P(('section', 'dp'), 'tensor'), may hold values from -100 to 100
- text_gain: float32 [4096], P('tensor'), may hold values from 0.1 to 1.9
- slot_of_row: int32 [8192], P(('section', 'dp')), may hold values from -1 to 8191, as said below
- out_cotangent: bfloat16 [8192, 4096], P(('section', 'dp'), 'tensor'), may hold values from -6 to 6
Outputs:
- normed: bfloat16 [8192, 4096], P(('section', 'dp'), 'tensor')
- vision_grad: bfloat16 [8192, 12800], P(('section', 'dp', 'tensor'))
Inputs may be any that keep to these rules, and one draw needn't show every extreme that they name: `slot_of_row`: language device g (index g of section+dp) owns slots g * 128 to (g + 1) * 128 - 1. Rows come in aligned runs of 16: a run is all -1 or goes to 16 consecutive slots that start at a multiple of 16. A vision device sends only to language devices with the same dp index, at most 8 // 8 runs to each. No slot receives two rows. In every draw some vision device has all its runs live and some language device receives a row in every slot.
All inputs are finite; a program needn't handle non-finite values.
Results may differ from a plain program's by a relative error of at most 0.0064.
Values may be sent and summed in bfloat16 or wider, within the bound.
No kernel may reach another device: no remote copies, remote signals or barrier semaphores. Data moves between devices by JAX's collectives and lax.ppermute only.
A program may use at most 128 MiB of HBM per device.

v0:
```python
import jax
import jax.numpy as jnp
from jax import lax
from jax.sharding import PartitionSpec as P

D = 4096
UNIT = 16


VISION_EPS = 1e-05
EPSILON = 1e-06
HALF_ROOT = 0.7071067811865476
INV_ROOT_TWO_PI = 0.3989422804014327


def gelu_value(values):
    return 0.5 * values * (1.0 + lax.erf(values * HALF_ROOT))


def gelu_slope(values):
    return (
        0.5 * (1.0 + lax.erf(values * HALF_ROOT))
        + values * jnp.exp(-0.5 * values * values) * INV_ROOT_TWO_PI
    )


def shards(
    vision_rows,
    vision_gain,
    vision_bias,
    proj_weight,
    text_rows,
    text_gain,
    slot_of_row,
    out_cotangent,
):
    sections = lax.axis_size("section")
    groups = lax.axis_size("dp")
    tensor_count = lax.axis_size("tensor")
    row_total = vision_rows.shape[0]
    lang_total = text_rows.shape[0]
    column_count = text_rows.shape[1]
    unit_total = row_total // UNIT
    lang_units = lang_total // UNIT
    capacity = unit_total // sections
    bucket_count = sections * capacity
    vision_wide = vision_rows.astype(jnp.float32)
    centered = vision_wide - jnp.mean(vision_wide, axis=1, keepdims=True)
    vision_inv = lax.rsqrt(jnp.mean(centered * centered, axis=1, keepdims=True) + VISION_EPS)
    vision_hat = centered * vision_inv
    normed_vision = (vision_hat * vision_gain + vision_bias).astype(jnp.bfloat16)
    weight_all = lax.all_gather(proj_weight, ("section", "dp"), axis=0, tiled=True)
    projected = jnp.dot(normed_vision, weight_all, preferred_element_type=jnp.float32)
    features = gelu_value(projected).astype(jnp.bfloat16)
    unit_slot = slot_of_row.reshape(unit_total, UNIT)[:, 0]
    unit_live = unit_slot >= 0
    target_device = jnp.where(unit_live, unit_slot // lang_total, 0) // groups
    same_target = (
        (target_device[:, None] == target_device[None, :]) & unit_live[:, None] & unit_live[None, :]
    )
    unit_order = jnp.arange(unit_total)
    earlier = unit_order[None, :] < unit_order[:, None]
    unit_rank = jnp.sum((same_target & earlier).astype(jnp.int32), axis=1)
    bucket = jnp.clip(target_device * capacity + unit_rank, 0, bucket_count - 1)
    chosen = (jnp.arange(bucket_count)[:, None] == bucket[None, :]) & unit_live[None, :]
    chosen_int = chosen.astype(jnp.int32)
    bucket_used = jnp.sum(chosen_int, axis=1) > 0
    bucket_source = jnp.sum(chosen_int * unit_order[None, :], axis=1)
    feature_units = features.reshape(unit_total, UNIT * column_count)
    send_rows = jnp.where(
        bucket_used[:, None], feature_units[bucket_source], jnp.zeros((), jnp.bfloat16)
    )
    send_slots = jnp.where(bucket_used, jnp.sum(chosen_int * unit_slot[None, :], axis=1), -1)
    arrived, arrived_slots = (
        lax.all_to_all(
            send_rows.reshape(sections, capacity * UNIT, column_count),
            "section",
            split_axis=0,
            concat_axis=0,
            tiled=True,
        ),
        lax.all_to_all(
            send_slots.reshape(sections, capacity),
            "section",
            split_axis=0,
            concat_axis=0,
            tiled=True,
        ),
    )
    lang_index = lax.axis_index("section") * groups + lax.axis_index("dp")
    arrived_slots = arrived_slots.reshape(bucket_count)
    arrived_live = arrived_slots >= 0
    arrived_position = jnp.clip(
        (arrived_slots - lang_index * lang_total) // UNIT, 0, lang_units - 1
    )
    placement = (jnp.arange(lang_units)[:, None] == arrived_position[None, :]) & arrived_live[
        None, :
    ]
    placement_int = placement.astype(jnp.int32)
    slot_is_image = jnp.sum(placement_int, axis=1) > 0
    slot_source = jnp.sum(placement_int * jnp.arange(bucket_count)[None, :], axis=1)
    arrived_units = arrived.reshape(bucket_count, UNIT * column_count)
    hidden_units = jnp.where(
        slot_is_image[:, None],
        arrived_units[slot_source],
        text_rows.reshape(lang_units, UNIT * column_count),
    )
    hidden_wide = hidden_units.reshape(lang_total, column_count).astype(jnp.float32)
    square_total = lax.psum(jnp.sum(hidden_wide * hidden_wide, axis=1), "tensor")
    hidden_inv = lax.rsqrt(square_total / D + EPSILON)[:, None]
    normed = (hidden_wide * hidden_inv * text_gain).astype(jnp.bfloat16)
    upstream = out_cotangent.astype(jnp.float32) * text_gain
    cross_total = lax.psum(jnp.sum(upstream * hidden_wide, axis=1), "tensor")
    cross_mean = (cross_total / D)[:, None]
    hidden_grad = (
        hidden_inv * (upstream - hidden_wide * hidden_inv * hidden_inv * cross_mean)
    ).astype(jnp.bfloat16)
    grad_units = hidden_grad.reshape(lang_units, UNIT * column_count)
    reply_rows = jnp.where(
        arrived_live[:, None], grad_units[arrived_position], jnp.zeros((), jnp.bfloat16)
    )
    returned = lax.all_to_all(
        reply_rows.reshape(sections, capacity * UNIT, column_count),
        "section",
        split_axis=0,
        concat_axis=0,
        tiled=True,
    )
    returned_units = returned.reshape(bucket_count, UNIT * column_count)
    feature_grad = jnp.where(
        unit_live[:, None], returned_units[bucket], jnp.zeros((), jnp.bfloat16)
    )
    feature_grad = feature_grad.reshape(row_total, column_count)
    projected_grad = (feature_grad.astype(jnp.float32) * gelu_slope(projected)).astype(jnp.bfloat16)
    share = row_total // tensor_count
    share_start = lax.axis_index("tensor") * share
    contract_dims = (((1,), (1,)), ((), ()))
    partial_grad = lax.dot_general(
        projected_grad, weight_all, contract_dims, preferred_element_type=jnp.float32
    )
    normed_grad = lax.psum_scatter(partial_grad, "tensor", scatter_dimension=0, tiled=True)
    own_hat = lax.dynamic_slice_in_dim(vision_hat, share_start, share, 0)
    own_inv = lax.dynamic_slice_in_dim(vision_inv, share_start, share, 0)
    weighted = normed_grad * vision_gain
    weighted_mean = jnp.mean(weighted, axis=1, keepdims=True)
    vision_cross = jnp.mean(weighted * own_hat, axis=1, keepdims=True)
    vision_grad = own_inv * (weighted - weighted_mean - own_hat * vision_cross)
    return (normed, vision_grad.astype(jnp.bfloat16))


def solution(mesh):
    in_specs = (
        P(("section", "dp"), None),
        P(),
        P(),
        P(("section", "dp"), "tensor"),
        P(("section", "dp"), "tensor"),
        P("tensor"),
        P(("section", "dp")),
        P(("section", "dp"), "tensor"),
    )
    out_specs = (P(("section", "dp"), "tensor"), P(("section", "dp", "tensor"), None))
    return jax.shard_map(shards, mesh=mesh, in_specs=in_specs, out_specs=out_specs, check_vma=False)
```

profile of v0, /device:TPU:8, one launch (start us, length us, event | category | flops | bytes accessed | tf_op | source)
XLA Modules:
  0.0 523.2 jit_solution(17789614030766908372)
XLA Ops:
  7.2 0.0 copy-start
  7.2 0.0 copy-start.3
  7.2 0.0 all-gather.2.cloned.1.call-start
  7.2 0.7 all-gather.2.cloned.1.call-update
  7.9 1.0 reshape.308
  8.9 0.1 fusion.51
  9.0 0.2 fusion.52
  9.2 0.2 convert_reduce_fusion.3
  9.4 0.2 select_reduce_fusion.2
  9.6 0.7 copy.60
  10.3 5.8 %all-to-all-start = ((s32[8,1,1]{2,1,0:T(1,128)}), s32[8,1,1]{2,1,0:T(1,128)S(1)}, u32[]{:S(2)}, u32[]{:S(2)}) async-start(s32[8,1,1]{2,1,0:T(1,128)} %copy.60), calls=%async_computation | async-start | bytes 8192 | tf_op jit(solution)/shard_map/all_to_all | solution.py:82
  16.0 0.1 copy.61
  16.1 0.1 fusion.34
  16.3 0.6 broadcast_compare_fusion.1
  16.8 2.4 convert_reduce_fusion
  19.3 3.0 fusion.2
  22.3 0.2 compare_reduce_fusion
  22.5 0.2 fusion.50
  22.8 0.1 convert_reduce_fusion.1
  22.9 0.1 copy.65
  23.0 0.7 fusion.35
  23.7 0.5 broadcast_compare_fusion
  24.3 338.3 %all-gather.2.cloned.1.call-done = bf16[12800,1024]{1,0:T(8,128)(2,1)} async-done(((bf16[200,1024]{1,0:T(8,128)(2,1)}), bf16[12800,1024]{1,0:T(8,128)(2,1)}) %all-gather.2.cloned.1.call-update) | async-done | bytes 26214416 | tf_op jit(solution)/shard_map/all_gather | solution.py:52
  362.6 13.1 %multiply_convert_fusion.1 = (bf16[128,1024]{1,0:T(8,128)(2,1)}, f32[128,1024]{1,0:T(8,128)}) fusion(bf16[12800,1024]{1,0:T(8,128)(2,1)} %all-gather.2.cloned.1.call-done, f32[12800]{0:T(1024)S(1)} %copy-done.14, f32[12800]{0:T(1024)S(1)} %copy-done.3, f32[128]{0:T(128)S(1)} %add_rsqrt_fusion.1, f32[128]{0:T(128)S(1)} %broadcast_multiply_fusion.3, ...), kind=kOutput, calls=%fused_computation.36 | convolution fusion | flops 3365928960 | bytes 30381056 | tf_op jit(solution)/shard_map/dot_general | solution.py:53
  375.7 0.0 copy-start.5
  375.7 1.1 reshape.309
  376.8 1.4 gather_fusion
  378.2 1.8 copy_select_fusion.1
  380.0 4.8 all-to-all-start.1
  384.8 0.7 pad_clamp_fusion.2
  385.5 1.3 broadcast_in_dim.45
  386.8 1.3 broadcast_in_dim.46
  388.1 0.1 fusion.36
  388.2 2.4 all-to-all-done.1
  390.7 0.7 copy-done.2
  391.4 1.1 copy.74
  392.5 1.4 gather_fusion.1
  393.9 1.8 gather.23
  395.7 2.0 fusion.14
  397.7 7.8 %all-reduce = (f32[128]{0:T(128)}, f32[128]{0:T(128)}) all-reduce(f32[128]{0:T(128)} %get-tuple-element.5, f32[128]{0:T(128)} %get-tuple-element.4), channel_id=1, replica_groups=mesh['section'=8,'dp'=8,'tensor'=4] {'tensor'}, use_global_device_ids=true, to_apply=%region_9.10 | all-reduce | flops 256 | bytes 2048 | tf_op jit(solution)/shard_map/psum | solution.py:109
  405.5 0.7 add_rsqrt_fusion
  406.1 2.0 fusion.12
  408.1 1.1 reshape.311
  409.2 1.4 gather_fusion.2
  410.6 1.8 copy_select_fusion
  412.4 4.8 all-to-all-start.2
  417.3 0.1 copy.73
  417.3 0.7 broadcast_in_dim.83
  418.0 0.1 broadcast_in_dim.84
  418.1 0.1 fusion.37
  418.2 5.1 all-to-all-done.2
  423.4 0.7 copy-done.1
  424.1 1.1 copy.75
  425.2 1.4 gather_fusion.3
  426.6 1.1 gather.27
  427.7 15.9 %fusion.21 = f32[128,12800]{1,0:T(8,128)} fusion(bf16[12800,1024]{1,0:T(8,128)(2,1)} %all-gather.2.cloned.1.call-done, f32[128,1024]{1,0:T(8,128)} %get-tuple-element.24, bf16[128,1024]{1,0:T(8,128)(2,1)S(1)} %gather.27, pred[128]{0:T(512)(128)(4,1)S(1)} %broadcast_in_dim.84), kind=kOutput, calls=%fused_computation.38 | convolution fusion | flops 3357016064 | bytes 33554560 | tf_op jit(solution)/shard_map/dot_general | solution.py:138
  443.5 0.0 reduce-scatter.2.cloned.1.call-update
  443.6 0.0 copy-start.4
  443.6 0.6 copy-done.13
  444.1 0.1 dynamic-slice.3
  444.2 3.7 fusion
  447.9 63.0 %reduce-scatter.2.cloned.1.call-done = f32[32,12800]{1,0:T(8,128)} async-done(((f32[128,12800]{1,0:T(8,128)}), f32[32,12800]{1,0:T(8,128)}) %reduce-scatter.2.cloned.1.call-update) | async-done | bytes 1638416 | tf_op jit(solution)/shard_map/reduce_scatter | solution.py:141
  511.0 2.2 multiply_reduce_fusion.1
  513.2 3.2 multiply_convert_fusion
  (37 shorter events, 0.2 us)
Async XLA Ops:
  7.2 355.4 %copy-start = (bf16[128,12800]{1,0:T(8,128)(2,1)S(1)}, bf16[128,12800]{1,0:T(8,128)(2,1)}, u32[]{:S(2)}) copy-start(bf16[128,12800]{1,0:T(8,128)(2,1)} %param.8) | copy-start | bytes 9830404
  7.2 355.4 %copy-start.14 = (f32[12800]{0:T(1024)S(1)}, f32[12800]{0:T(1024)}, u32[]{:S(2)}) copy-start(f32[12800]{0:T(1024)} %param.10) | copy-start | bytes 153604
  7.2 355.4 %copy-start.3 = (f32[12800]{0:T(1024)S(1)}, f32[12800]{0:T(1024)}, u32[]{:S(2)}) copy-start(f32[12800]{0:T(1024)} %param.9) | copy-start | bytes 153604
  7.2 355.4 %all-gather.2.cloned.1.call-start = ((), (), s32[]{:S(2)}) async-start(), calls=%async_computation.4 | async-start | bytes 26624000 | tf_op jit(solution)/shard_map/all_gather | solution.py:52
  9.0 366.6 %copy-start.11 = (pred[8]{0:T(512)(128)(4,1)}, pred[8]{0:T(512)(128)(4,1)S(1)}, u32[]{:S(2)}) copy-start(pred[8]{0:T(512)(128)(4,1)S(1)} %get-tuple-element.16) | copy-start | bytes 28
  9.4 0.9 copy-start.9
  10.3 12.0 %all-to-all-start = ((s32[8,1,1]{2,1,0:T(1,128)}), s32[8,1,1]{2,1,0:T(1,128)S(1)}, u32[]{:S(2)}, u32[]{:S(2)}) async-start(s32[8,1,1]{2,1,0:T(1,128)} %copy.60), calls=%async_computation | async-start | bytes 8192 | tf_op jit(solution)/shard_map/all_to_all | solution.py:82
  19.3 356.4 %copy-start.7 = (f32[128]{0:T(128)}, f32[128]{0:T(128)S(1)}, u32[]{:S(2)}) copy-start(f32[128]{0:T(128)S(1)} %broadcast_multiply_fusion.3) | copy-start | bytes 1540
  22.2 353.4 %copy-start.12 = (f32[128]{0:T(128)}, f32[128]{0:T(128)S(1)}, u32[]{:S(2)}) copy-start(f32[128]{0:T(128)S(1)} %add_rsqrt_fusion.1) | copy-start | bytes 1540
  22.5 353.2 %copy-start.6 = (pred[8]{0:T(512)(128)(4,1)}, pred[8]{0:T(512)(128)(4,1)S(1)}, u32[]{:S(2)}) copy-start(pred[8]{0:T(512)(128)(4,1)S(1)} %compare_reduce_fusion) | copy-start | bytes 28
  375.7 20.0 %copy-start.5 = (f32[1024]{0:T(1024)S(1)}, f32[1024]{0:T(1024)}, u32[]{:S(2)}) copy-start(f32[1024]{0:T(1024)} %param.13) | copy-start | bytes 12292
  380.0 10.6 %all-to-all-start.1 = ((bf16[8,16,1024]{2,1,0:T(8,128)(2,1)}), bf16[8,16,1024]{2,1,0:T(8,128)(2,1)S(1)}, u32[]{:S(2)}, u32[]{:S(2)}) async-start(bf16[8,16,1024]{2,1,0:T(8,128)(2,1)} %copy_select_fusion.1), calls=%async_computation.1 | async-start | bytes 524288 | tf_op jit(solution)/shard_map/all_to_all | solution.py:75
  390.7 0.7 copy-start.2
  393.9 23.4 %copy-start.10 = (s32[8]{0:T(128)S(1)}, s32[8]{0:T(128)}, u32[]{:S(2)}) copy-start(s32[8]{0:T(128)} %copy-done.9) | copy-start | bytes 100
  412.4 10.9 %all-to-all-start.2 = ((bf16[8,16,1024]{2,1,0:T(8,128)(2,1)}), bf16[8,16,1024]{2,1,0:T(8,128)(2,1)S(1)}, u32[]{:S(2)}, u32[]{:S(2)}) async-start(bf16[8,16,1024]{2,1,0:T(8,128)(2,1)} %copy_select_fusion), calls=%async_computation.2 | async-start | bytes 524288 | tf_op jit(solution)/shard_map/all_to_all | solution.py:122
  417.2 93.7 %reduce-scatter.2.cloned.1.call-start = ((), (), s32[]{:S(2)}) async-start(), calls=%async_computation.5 | async-start | bytes 8192000 | tf_op jit(solution)/shard_map/reduce_scatter | solution.py:141
  423.4 0.7 copy-start.1
  443.5 0.6 copy-start.13
  443.5 0.7 copy-start.8
  443.6 67.4 %copy-start.4 = (f32[12800]{0:T(1024)S(1)}, f32[12800]{0:T(1024)}, u32[]{:S(2)}) copy-start(f32[12800]{0:T(1024)} %param.9) | copy-start | bytes 153604
Sparse Core Ops, SparseCore 0:
  9.8 352.7 all-gather.1
  443.7 67.2 reduce-scatter.1
where the time goes:
time: 526 us; the launch traced here: 523 us
  waiting for transfers between devices  410 us (78%)
  matrix products  28.9 us (5%)
  other arithmetic  27 us (5%)
  local copies, waits for them, and re-layouts  20.3 us (4%)
  starting transfers between devices  15.4 us (3%)
  between operations  14.2 us (3%)
  blocking collectives  7.8 us (1%)
    all_gather x1, waiting for transfers between devices, shards(): lax.all_gather(proj_weight, ('section', 'dp'), axis=0, tiled=True)  338 us
    reduce_scatter x1, waiting for transfers between devices, shards(): lax.psum_scatter(partial_grad, 'tensor', scatter_dimension=0, tiled=True)  63 us
    dot_general x1, matrix products, shards(): lax.dot_general(projected_grad, weight_all, contract_dims, preferred_elem...  15.9 us
    dot_general x1, matrix products, shards(): jnp.dot(normed_vision, weight_all, preferred_element_type=jnp.float32)  13.1 us
  transfers between devices with their start and end apart: 5, of which 4 were waited for; matrix products, arithmetic and copies ran while one was open for 4% of the time, Pallas kernels for 0%

commit v1 on v0

v1 whole, which is shorter than its diff:
```python
import functools

import jax
import jax.numpy as jnp
from jax import lax
from jax.experimental import pallas as pl
from jax.experimental.pallas import tpu as pltpu
from jax.sharding import PartitionSpec as P

UNIT = 16
VISION_EPS = 1e-05
EPSILON = 1e-06
HALF_ROOT = 0.7071067811865476
INV_ROOT_TWO_PI = 0.3989422804014327
BF = jnp.bfloat16
F32 = jnp.float32


def norm_kernel(parts, order_ref, rows_ref, gain_ref, bias_ref, out_ref):
    wide = rows_ref[...].astype(F32)
    centered = wide - jnp.mean(wide, axis=1, keepdims=True)
    inv = lax.rsqrt(jnp.mean(centered * centered, axis=1, keepdims=True) + VISION_EPS)
    normed = (centered * inv * gain_ref[...] + bias_ref[...]).astype(BF)
    chunk = normed.shape[1] // parts
    for k in range(parts):
        out_ref[k] = normed[:, k * chunk : (k + 1) * chunk]


def slots_kernel(
    source_ref, live_ref, parts_ref, text_ref, cot_ref, gain_ref, hidden_ref, slope_ref, stat_ref
):
    live = live_ref[pl.program_id(0)] > 0
    projected = parts_ref[0, 0].astype(F32)
    for k in range(1, parts_ref.shape[0]):
        projected = projected + parts_ref[k, 0].astype(F32)
    gate = 0.5 * (1.0 + lax.erf(projected * HALF_ROOT))
    feature = (projected * gate).astype(BF)
    hidden = jnp.where(live, feature, text_ref[...])
    hidden_ref[...] = hidden
    slope_ref[...] = (
        gate + projected * jnp.exp(-0.5 * projected * projected) * INV_ROOT_TWO_PI
    )
    wide = hidden.astype(F32)
    upstream = cot_ref[...].astype(F32) * gain_ref[...]
    square = jnp.sum(wide * wide, axis=1, keepdims=True)
    cross = jnp.sum(upstream * wide, axis=1, keepdims=True)
    lane = lax.broadcasted_iota(jnp.int32, stat_ref.shape, 1)
    stat_ref[...] = jnp.where(lane == 0, square, cross)


def grad_kernel(
    width, source_ref, live_ref, hidden_ref, slope_ref, cot_ref, gain_ref, stat_ref, normed_ref, grad_ref
):
    live = live_ref[pl.program_id(0)] > 0
    stat = stat_ref[...] / width
    inv = lax.rsqrt(stat[:, 0:1] + EPSILON)
    wide = hidden_ref[...].astype(F32)
    normed_ref[...] = (wide * inv * gain_ref[...]).astype(BF)
    upstream = cot_ref[...].astype(F32) * gain_ref[...]
    hidden_grad = (inv * (upstream - wide * inv * inv * stat[:, 1:2])).astype(BF)
    grad = (hidden_grad.astype(F32) * slope_ref[...]).astype(BF)
    grad_ref[0] = jnp.where(live, grad, jnp.zeros_like(grad))


def final_kernel(parts, share_ref, parts_ref, rows_ref, gain_ref, out_ref):
    wide = rows_ref[...].astype(F32)
    centered = wide - jnp.mean(wide, axis=1, keepdims=True)
    inv = lax.rsqrt(jnp.mean(centered * centered, axis=1, keepdims=True) + VISION_EPS)
    hat = centered * inv
    grad = jnp.concatenate([parts_ref[k] for k in range(parts)], axis=1).astype(F32)
    weighted = grad * gain_ref[...]
    weighted_mean = jnp.mean(weighted, axis=1, keepdims=True)
    cross = jnp.mean(weighted * hat, axis=1, keepdims=True)
    out_ref[...] = (inv * (weighted - weighted_mean - hat * cross)).astype(BF)


def shards(
    width, vision_rows, vision_gain, vision_bias, proj_weight, text_rows, text_gain, slot_of_row, out_cotangent
):
    sections = lax.axis_size("section")
    groups = lax.axis_size("dp")
    tensors = lax.axis_size("tensor")
    rows, depth = vision_rows.shape
    slots, columns = text_rows.shape
    units = rows // UNIT
    chunk = depth // sections
    section = lax.axis_index("section")
    tensor = lax.axis_index("tensor")
    lang = section * groups + lax.axis_index("dp")

    gain_row = vision_gain.reshape(1, depth)
    text_gain_row = text_gain.reshape(1, columns)

    unit_slot = slot_of_row.reshape(units, UNIT)[:, 0]
    table = lax.all_to_all(
        jnp.broadcast_to(unit_slot, (sections, units)), "section", 0, 0, tiled=True
    )
    alive = table >= 0
    target = jnp.where(alive, table // (slots * groups), -1)
    places = jnp.arange(units)
    taken = jnp.any(target[:, :, None] == places, axis=1)
    free_rank = jnp.cumsum(~taken, axis=1) - 1
    dead_rank = jnp.cumsum(~alive, axis=1) - 1
    fits = (~taken)[:, None, :] & (free_rank[:, None, :] == dead_rank[:, :, None])
    filler = jnp.sum(jnp.where(fits, places, 0), axis=2)
    place = jnp.where(alive, target, filler).astype(jnp.int32)

    own_alive = unit_slot >= 0
    own_target = jnp.where(own_alive, unit_slot // (slots * groups), -1)
    own_taken = jnp.any(own_target[:, None] == places, axis=0)
    own_fits = (~own_taken)[None, :] & (
        (jnp.cumsum(~own_taken) - 1)[None, :] == (jnp.cumsum(~own_alive) - 1)[:, None]
    )
    own_place = jnp.where(own_alive, own_target, jnp.sum(jnp.where(own_fits, places, 0), axis=1))
    own_order = jnp.sum(
        jnp.where(own_place[:, None] == places, jnp.arange(units)[:, None], 0), axis=0
    ).astype(jnp.int32)

    normed_vision = pl.pallas_call(
        functools.partial(norm_kernel, sections),
        out_shape=jax.ShapeDtypeStruct((sections, rows, chunk), BF),
        grid_spec=pltpu.PrefetchScalarGridSpec(
            num_scalar_prefetch=1,
            grid=(units,),
            in_specs=[
                pl.BlockSpec((UNIT, depth), lambda i, order: (order[i], 0)),
                pl.BlockSpec((1, depth), lambda i, order: (0, 0)),
                pl.BlockSpec((1, depth), lambda i, order: (0, 0)),
            ],
            out_specs=pl.BlockSpec((sections, UNIT, chunk), lambda i, order: (0, i, 0)),
        ),
        compiler_params=pltpu.CompilerParams(vmem_limit_bytes=32 * 2**20),
        name="vision_norm",
    )(own_order, vision_rows, gain_row, vision_bias.reshape(1, depth))
    weight = lax.all_gather(proj_weight, "dp", axis=0, tiled=True)
    arrived = lax.all_to_all(normed_vision, "section", 0, 0, tiled=True)
    partial = jnp.dot(
        arrived.reshape(sections * rows, chunk), weight, preferred_element_type=F32
    ).astype(BF)
    partial = jnp.swapaxes(partial.reshape(sections, units, UNIT, columns), 0, 1)
    partial = lax.all_to_all(
        partial.reshape(units, sections * UNIT, columns), "section", 0, 0, tiled=True
    ).reshape(sections, sections, UNIT, columns)

    mine = alive & (table // slots == lang)
    mine_slot = jnp.sum(jnp.where(mine, table, 0), axis=1)
    has = jnp.any(mine, axis=1)
    local = jnp.where(has, (mine_slot - lang * slots) // UNIT, -1)
    filled = jnp.any(local[:, None] == places, axis=0)
    spare = (~filled)[None, :] & (
        (jnp.cumsum(~filled) - 1)[None, :] == (jnp.cumsum(~has) - 1)[:, None]
    )
    where = jnp.where(has, local, jnp.sum(jnp.where(spare, places, 0), axis=1))
    source = jnp.sum(
        jnp.where(where[:, None] == places, jnp.arange(sections)[:, None], 0), axis=0
    ).astype(jnp.int32)
    filled = filled.astype(jnp.int32)

    row_block = pl.BlockSpec((UNIT, columns), lambda i, source, live: (i, 0))
    gain_block = pl.BlockSpec((1, columns), lambda i, source, live: (0, 0))
    stat_block = pl.BlockSpec((UNIT, 2), lambda i, source, live: (i, 0))
    hidden, slope, stat = pl.pallas_call(
        slots_kernel,
        out_shape=(
            jax.ShapeDtypeStruct((slots, columns), BF),
            jax.ShapeDtypeStruct((slots, columns), F32),
            jax.ShapeDtypeStruct((slots, 2), F32),
        ),
        grid_spec=pltpu.PrefetchScalarGridSpec(
            num_scalar_prefetch=2,
            grid=(slots // UNIT,),
            in_specs=[
                pl.BlockSpec(
                    (sections, 1, UNIT, columns), lambda i, source, live: (0, source[i], 0, 0)
                ),
                row_block,
                row_block,
                gain_block,
            ],
            out_specs=[row_block, row_block, stat_block],
        ),
        name="slots",
    )(source, filled, partial, text_rows, out_cotangent, text_gain_row)
    stat = lax.psum(stat, "tensor")
    normed, grad = pl.pallas_call(
        functools.partial(grad_kernel, width),
        out_shape=(
            jax.ShapeDtypeStruct((slots, columns), BF),
            jax.ShapeDtypeStruct((sections, UNIT, columns), BF),
        ),
        grid_spec=pltpu.PrefetchScalarGridSpec(
            num_scalar_prefetch=2,
            grid=(slots // UNIT,),
            in_specs=[row_block, row_block, row_block, gain_block, stat_block],
            out_specs=[
                row_block,
                pl.BlockSpec((1, UNIT, columns), lambda i, source, live: (source[i], 0, 0)),
            ],
        ),
        name="grads",
    )(source, filled, hidden, slope, out_cotangent, text_gain_row, stat)

    grads = lax.all_to_all(
        jnp.broadcast_to(grad, (sections, sections, UNIT, columns)), "section", 0, 0, tiled=True
    ).reshape(sections * sections, UNIT * columns)
    share = units // tensors
    relative = jnp.array([3, 1, 2, 0]) ^ tensor
    pick = place.reshape(sections, tensors, share)[:, relative]
    pick = pick * sections + jnp.arange(sections)[:, None, None]
    pick = jnp.swapaxes(pick, 0, 1)
    half = sections * rows // 2

    def product(index):
        picked = grads[index.reshape(-1)].reshape(half, columns)
        return lax.dot_general(
            picked, weight, (((1,), (1,)), ((), ())), preferred_element_type=F32
        )

    other_core = [(i, i ^ 1) for i in range(tensors)]
    other_y = [(i, i ^ 2) for i in range(tensors)]
    given = product(pick[:2]).astype(BF)
    got = lax.ppermute(given, "tensor", other_core)
    total = product(pick[2:]) + got.astype(F32)
    quarter = half // 2
    far = lax.ppermute(total[:quarter].astype(BF), "tensor", other_y)
    total = (total[quarter:] + far.astype(F32)).astype(BF)
    back = lax.all_to_all(
        total.reshape(sections, share * UNIT, chunk), "section", 0, 0, tiled=True
    )
    own_rows = rows // tensors
    vision_grad = pl.pallas_call(
        functools.partial(final_kernel, sections),
        out_shape=jax.ShapeDtypeStruct((own_rows, depth), BF),
        grid_spec=pltpu.PrefetchScalarGridSpec(
            num_scalar_prefetch=1,
            grid=(share,),
            in_specs=[
                pl.BlockSpec((sections, UNIT, chunk), lambda i, first: (0, i, 0)),
                pl.BlockSpec((UNIT, depth), lambda i, first: (first[0] + i, 0)),
                pl.BlockSpec((1, depth), lambda i, first: (0, 0)),
            ],
            out_specs=pl.BlockSpec((UNIT, depth), lambda i, first: (i, 0)),
        ),
        compiler_params=pltpu.CompilerParams(vmem_limit_bytes=32 * 2**20),
        name="vision_back",
    )((tensor * share).reshape(1).astype(jnp.int32), back, vision_rows, gain_row)
    return normed, vision_grad


def solution(mesh):
    in_specs = (
        P(("section", "dp"), None),
        P(),
        P(),
        P(("section", "dp"), "tensor"),
        P(("section", "dp"), "tensor"),
        P("tensor"),
        P(("section", "dp")),
        P(("section", "dp"), "tensor"),
    )
    out_specs = (P(("section", "dp"), "tensor"), P(("section", "dp", "tensor"), None))

    def program(*args):
        body = functools.partial(shards, args[4].shape[1])
        return jax.shard_map(
            body, mesh=mesh, in_specs=in_specs, out_specs=out_specs, check_vma=False
        )(*args)

    return program
```

time: 526 us -> 253 us (0.48)
  waiting for transfers between devices: 410 us -> 116 us
  starting transfers between devices: 15.4 us -> 39.4 us
  other arithmetic: 27 us -> 4.82 us
  Pallas kernels: 0 us -> 21 us
  matrix products: 28.9 us -> 15.9 us
  blocking collectives: 7.8 us -> 16.6 us
    all_gather x1, waiting for transfers between devices: 338 us -> 0.01 us  [shards(): weight = lax.all_gather(proj_weight, 'dp', axis=0, tiled=True)]
    all_to_all x3 -> x5, waiting for transfers between devices: 7.53 us -> 93.6 us  [the longest x1 38.1 us: shards(): arrived = lax.all_to_all(normed_vision, 'section', 0, 0, tiled=True)]
    reduce_scatter x1 -> x0, waiting for transfers between devices: 63 us -> none  [shards(): lax.psum_scatter(partial_grad, 'tensor', scatter_dimension=0, tiled=True)]
    all_to_all x3 -> x5, starting transfers between devices: 15.4 us -> 37.2 us  [the longest x1 14.1 us: shards(): lax.all_to_all(jnp.broadcast_to(unit_slot, (sections, units)), 'section',...]
    ppermute x0 -> x2, waiting for transfers between devices: none -> 21.6 us  [the longest x1 19.7 us: shards(): far = lax.ppermute(total[:quarter].astype(BF), 'tensor', other_y)]
    pallas_call x0 -> x4, Pallas kernels: none -> 21 us  [the longest x1 6.42 us: shards(): pl.pallas_call(slots_kernel, out_shape=(jax.ShapeDtypeStruct((slots, colu...]
    dot_general x2 -> x3, matrix products: 28.9 us -> 15.9 us  [the longest x2 9.7 us: product(): lax.dot_general(picked, weight, (((1,), (1,)), ((), ())), preferred_eleme...]
    psum x1, blocking collectives: 7.8 us -> 16.6 us  [shards(): stat = lax.psum(stat, 'tensor')]
  transfers between devices with their start and end apart: 5 -> 8, of which waited for: 4 -> 6; matrix products, arithmetic and copies ran while one was open for 4% -> 8% of each run, Pallas kernels for 0% -> 2%
where the time goes in v1:
time: 253 us; the launch traced here: 250 us
  waiting for transfers between devices  116 us (46%)
  starting transfers between devices  39.4 us (16%)
  local copies, waits for them, and re-layouts  22.3 us (9%)
  Pallas kernels  21 us (8%)
  blocking collectives  16.6 us (7%)
  matrix products  15.9 us (6%)
  between operations  14.2 us (6%)
  other arithmetic  4.82 us (2%)
    all_to_all x1, waiting for transfers between devices, shards(): arrived = lax.all_to_all(normed_vision, 'section', 0, 0, tiled=True)  38.1 us
    all_to_all x1, waiting for transfers between devices, shards(): lax.all_to_all(jnp.broadcast_to(grad, (sections, sections, UNIT, columns)...  22.1 us
    all_to_all x1, waiting for transfers between devices, shards(): lax.all_to_all(partial.reshape(units, sections * UNIT, columns), 'section...  21.4 us
    ppermute x1, waiting for transfers between devices, shards(): far = lax.ppermute(total[:quarter].astype(BF), 'tensor', other_y)  19.7 us
    psum x1, blocking collectives, shards(): stat = lax.psum(stat, 'tensor')  16.6 us
    all_to_all x1, starting transfers between devices, shards(): lax.all_to_all(jnp.broadcast_to(unit_slot, (sections, units)), 'section',...  14.1 us
    all_to_all x1, waiting for transfers between devices, shards(): lax.all_to_all(total.reshape(sections, share * UNIT, chunk), 'section', 0...  12 us
    dot_general x2, matrix products, product(): lax.dot_general(picked, weight, (((1,), (1,)), ((), ())), preferred_eleme...  9.7 us
  transfers between devices with their start and end apart: 8, of which 6 were waited for; matrix products, arithmetic and copies ran while one was open for 8% of the time, Pallas kernels for 2%

profile of v1, /device:TPU:8, one launch (start us, length us, event | category | flops | bytes accessed | tf_op | source)
XLA Modules:
  0.0 250.1 jit_solution(10175001080952312676)
XLA Ops:
  7.2 0.7 all-gather.2.cloned.1.call-update
  7.9 0.7 reshape.332
  8.6 0.1 fusion.24
  8.8 0.1 fusion.16
  8.9 0.1 copy.56
  9.0 0.2 add_reduce_fusion
  9.1 0.2 select_reduce_fusion.3
  9.3 0.1 copy.57
  9.4 0.9 reshape.333.gain_ref
  10.3 0.8 reshape.334.bias_ref
  11.1 0.2 select_reduce_fusion.2
  11.3 0.1 select_reduce_fusion.1.order_ref
  11.4 1.9 copy-done
  13.3 5.3 %vision_norm.1 = bf16[8,128,1600]{2,1,0:T(8,128)(2,1)S(1)} custom-call(s32[8]{0:T(128)S(1)} %select_reduce_fusion.1.order_ref, bf16[128,12800]{1,0:T(8,128)(2,1)S(1)} %copy-done, f32[1,12800]{1,0:T(1,128)S(1)} %reshape.333.gain_ref, f32[1,12800]{1,0:T(1,128)S(1)} %reshape.334.bias_ref), custom_call_target="tpu_custom_call" | custom-call | tf_op jit(solution)/shard_map/vision_norm/pallas_call | solution.py:119
  18.6 3.7 %copy.58 = bf16[8,128,1600]{1,2,0:T(8,128)(2,1)} copy(bf16[8,128,1600]{2,1,0:T(8,128)(2,1)S(1)} %vision_norm.1) | data formatting | bytes 6553600 | tf_op jit(solution)/shard_map/vision_norm/pallas_call | solution.py:119
  22.3 5.8 %all-to-all-start.1 = ((bf16[8,128,1600]{1,2,0:T(8,128)(2,1)}), bf16[8,128,1600]{1,2,0:T(8,128)(2,1)S(1)}, u32[]{:S(2)}, u32[]{:S(2)}) async-start(bf16[8,128,1600]{1,2,0:T(8,128)(2,1)} %copy.58), calls=%async_computation.1 | async-start | bytes 6553600 | tf_op jit(solution)/shard_map/all_to_all | solution.py:136
  28.1 38.1 %all-to-all-done.1 = bf16[8,128,1600]{1,2,0:T(8,128)(2,1)S(1)} async-done(((bf16[8,128,1600]{1,2,0:T(8,128)(2,1)}), bf16[8,128,1600]{1,2,0:T(8,128)(2,1)S(1)}, u32[]{:S(2)}, u32[]{:S(2)}) %all-to-all-start.1) | async-done | bytes 3276832 | tf_op jit(solution)/shard_map/all_to_all | solution.py:136
  66.2 0.6 broadcast_in_dim.76
  66.8 14.1 %all-to-all-start = ((s32[8,1,8]{2,1,0:T(1,128)}), s32[8,1,8]{2,1,0:T(1,128)S(1)}, u32[]{:S(2)}, u32[]{:S(2)}) async-start(s32[8,1,8]{2,1,0:T(1,128)} %broadcast_in_dim.76), calls=%async_computation | async-start | bytes 8192 | tf_op jit(solution)/shard_map/all_to_all | solution.py:95
  80.9 6.2 %fusion.3 = bf16[1024,1024]{1,0:T(8,128)(2,1)S(1)} fusion(bf16[1600,1024]{1,0:T(8,128)(2,1)} %all-gather.2.cloned.1.call-done, bf16[8,128,1600]{1,2,0:T(8,128)(2,1)S(1)} %all-to-all-done.1), kind=kOutput, calls=%fused_computation.8 | convolution fusion | flops 3356491776 | bytes 8650752 | tf_op jit(solution)/shard_map/dot_general | solution.py:137
  87.1 1.5 copy.60
  88.6 5.7 %all-to-all-start.2 = ((bf16[8,128,1024]{2,1,0:T(8,128)(2,1)}), bf16[8,128,1024]{2,1,0:T(8,128)(2,1)S(1)}, u32[]{:S(2)}, u32[]{:S(2)}) async-start(bf16[8,128,1024]{2,1,0:T(8,128)(2,1)} %bitcast.40), calls=%async_computation.2 | async-start | bytes 4194304 | tf_op jit(solution)/shard_map/all_to_all | solution.py:141
  94.4 0.1 select_reduce_fusion.6
  94.5 0.1 reduce_or.36
  94.6 0.1 fusion.14
  94.7 0.6 fusion.28
  95.4 0.1 copy.55
  95.5 0.1 add_reduce_fusion.3
  95.6 0.1 add_reduce_fusion.2
  95.7 0.2 select_reduce_fusion.5
  95.9 0.6 select_reduce_fusion.4.source_ref
  96.5 0.1 fusion.7
  96.6 21.4 %all-to-all-done.2 = bf16[8,128,1024]{2,1,0:T(8,128)(2,1)S(1)} async-done(((bf16[8,128,1024]{2,1,0:T(8,128)(2,1)}), bf16[8,128,1024]{2,1,0:T(8,128)(2,1)S(1)}, u32[]{:S(2)}, u32[]{:S(2)}) %all-to-all-start.2) | async-done | bytes 2097184 | tf_op jit(solution)/shard_map/all_to_all | solution.py:141
  118.0 1.3 copy-done.2
  119.3 6.4 %slots.1 = (bf16[128,1024]{1,0:T(8,128)(2,1)}, f32[128,1024]{1,0:T(8,128)}, f32[128,2]{1,0:T(8,128)}) custom-call(s32[8]{0:T(128)} %select_reduce_fusion.4.source_ref, s32[8]{0:T(128)} %get-tuple-element.23.live_ref, bf16[8,8,16,1024]{3,2,1,0:T(8,128)(2,1)} %bitcast.39, bf16[128,1024]{1,0:T(8,128)(2,1)} %text_ref.1, bf16[128,1024]{1,0:T(8,128)(2,1)} %cot_ref.3, ...), custom_call_target="tpu_custom_call" | custom-call | tf_op jit(solution)/shard_map/slots/pallas_call | solution.py:162
  125.8 16.6 %psum.7.stat_ref = f32[128,2]{1,0:T(8,128)} all-reduce(f32[128,2]{1,0:T(8,128)} %get-tuple-element.9), channel_id=1, replica_groups=mesh['section'=8,'dp'=8,'tensor'=4] {'tensor'}, use_global_device_ids=true, to_apply=%region_12.13 | all-reduce | flops 256 | bytes 2048 | tf_op jit(solution)/shard_map/psum | solution.py:184
  142.4 5.7 %grads.1 = (bf16[128,1024]{1,0:T(8,128)(2,1)}, bf16[8,16,1024]{2,1,0:T(8,128)(2,1)}) custom-call(s32[8]{0:T(128)} %select_reduce_fusion.4.source_ref, s32[8]{0:T(128)} %get-tuple-element.23.live_ref, bf16[128,1024]{1,0:T(8,128)(2,1)} %get-tuple-element.7.hidden_ref, f32[128,1024]{1,0:T(8,128)} %get-tuple-element.8.slope_ref, bf16[128,1024]{1,0:T(8,128)(2,1)} %cot_ref.3, ...), custom_call_target="tpu_custom_call" | custom-call | tf_op jit(solution)/shard_map/grads/pallas_call | solution.py:185
  148.1 1.1 copy.61
  149.2 1.6 broadcast_in_dim.81
  150.8 5.6 %all-to-all-start.3 = ((bf16[8,8,16,1024]{3,1,2,0:T(8,128)(2,1)}), bf16[8,8,16,1024]{3,1,2,0:T(8,128)(2,1)S(1)}, u32[]{:S(2)}, u32[]{:S(2)}) async-start(bf16[8,8,16,1024]{3,1,2,0:T(8,128)(2,1)} %broadcast_in_dim.81), calls=%async_computation.3 | async-start | bytes 4194304 | tf_op jit(solution)/shard_map/all_to_all | solution.py:203
  156.4 0.2 reduce_window_sum.30
  156.6 0.2 reduce_window_sum.31
  156.8 0.3 select_reduce_fusion
  157.2 0.6 gather_fusion
  157.8 0.1 copy.65
  157.9 0.1 reshape.344
  158.0 22.1 %all-to-all-done.3 = bf16[8,8,16,1024]{3,1,2,0:T(8,128)(2,1)S(1)} async-done(((bf16[8,8,16,1024]{3,1,2,0:T(8,128)(2,1)}), bf16[8,8,16,1024]{3,1,2,0:T(8,128)(2,1)S(1)}, u32[]{:S(2)}, u32[]{:S(2)}) %all-to-all-start.3) | async-done | bytes 2097184 | tf_op jit(solution)/shard_map/all_to_all | solution.py:203
  180.1 1.2 gather_fusion.2
  181.3 1.3 reshape.345
  182.7 5.3 %convolution_convert_fusion = bf16[512,1600]{0,1:T(8,128)(2,1)} fusion(bf16[512,1024]{1,0:T(8,128)(2,1)} %reshape.345, bf16[1600,1024]{1,0:T(8,128)(2,1)} %all-gather.2.cloned.1.call-done), kind=kOutput, calls=%fused_computation.7 | convolution fusion | flops 1678540800 | bytes 5963776 | tf_op jit(solution)/shard_map/dot_general | solution.py:215
  188.0 0.1 copy.64
  188.1 0.1 reshape.342
  188.2 1.2 gather_fusion.1
  189.4 0.5 reshape.343
  190.0 1.9 collective-permute-done
  191.8 4.4 %convert_add_fusion = f32[512,1600]{0,1:T(8,128)S(1)} fusion(bf16[512,1600]{0,1:T(8,128)(2,1)} %collective-permute-done, bf16[512,1024]{1,0:T(8,128)(2,1)S(1)} %reshape.343, bf16[1600,1024]{1,0:T(8,128)(2,1)} %all-gather.2.cloned.1.call-done), kind=kOutput, calls=%fused_computation.6 | convolution fusion | flops 1679360000 | bytes 9240576 | tf_op jit(solution)/shard_map/dot_general | solution.py:215
  196.2 0.1 slice.42
  196.4 2.1 collective-permute-start.1
  198.5 19.7 %collective-permute-done.1 = bf16[256,1600]{0,1:T(8,128)(2,1)S(1)} collective-permute-done((bf16[256,1600]{0,1:T(8,128)(2,1)S(1)}, bf16[256,1600]{0,1:T(8,128)(2,1)S(1)}, u32[]{:S(2)}, u32[]{:S(2)}) %collective-permute-start.1) | collective-permute-done | bytes 819232 | tf_op jit(solution)/shard_map/ppermute | solution.py:225
  218.2 1.2 fusion.6
  219.4 2.2 copy.66
  221.6 6.1 %all-to-all-start.4 = ((bf16[8,32,1600]{2,1,0:T(8,128)(2,1)}), bf16[8,32,1600]{2,1,0:T(8,128)(2,1)}, u32[]{:S(2)}, u32[]{:S(2)}) async-start(bf16[8,32,1600]{2,1,0:T(8,128)(2,1)} %bitcast.41), calls=%async_computation.4 | async-start | bytes 1703936 | tf_op jit(solution)/shard_map/all_to_all | solution.py:227
  227.7 12.0 %all-to-all-done.4.parts_ref = bf16[8,32,1600]{2,1,0:T(8,128)(2,1)} async-done(((bf16[8,32,1600]{2,1,0:T(8,128)(2,1)}), bf16[8,32,1600]{2,1,0:T(8,128)(2,1)}, u32[]{:S(2)}, u32[]{:S(2)}) %all-to-all-start.4) | async-done | bytes 819232 | tf_op jit(solution)/shard_map/all_to_all | solution.py:227
  239.7 3.5 %vision_back.1 = bf16[32,12800]{1,0:T(8,128)(2,1)} custom-call(s32[1]{0:T(128)} %bitcast.10.share_ref, bf16[8,32,1600]{2,1,0:T(8,128)(2,1)} %all-to-all-done.4.parts_ref, bf16[128,12800]{1,0:T(8,128)(2,1)S(1)} %copy-done.1, f32[1,12800]{1,0:T(1,128)S(1)} %reshape.333.gain_ref), custom_call_target="tpu_custom_call" | custom-call | tf_op jit(solution)/shard_map/vision_back/pallas_call | solution.py:231
  (35 shorter events, 0.5 us)
Async XLA Ops:
  7.2 73.7 %all-gather.2.cloned.1.call-start = ((), (), s32[]{:S(2)}) async-start(), calls=%async_computation.5 | async-start | bytes 3686400 | tf_op jit(solution)/shard_map/all_gather | solution.py:135
  11.4 1.9 copy-start
  22.3 43.9 %all-to-all-start.1 = ((bf16[8,128,1600]{1,2,0:T(8,128)(2,1)}), bf16[8,128,1600]{1,2,0:T(8,128)(2,1)S(1)}, u32[]{:S(2)}, u32[]{:S(2)}) async-start(bf16[8,128,1600]{1,2,0:T(8,128)(2,1)} %copy.58), calls=%async_computation.1 | async-start | bytes 6553600 | tf_op jit(solution)/shard_map/all_to_all | solution.py:136
  66.8 21.8 %all-to-all-start = ((s32[8,1,8]{2,1,0:T(1,128)}), s32[8,1,8]{2,1,0:T(1,128)S(1)}, u32[]{:S(2)}, u32[]{:S(2)}) async-start(s32[8,1,8]{2,1,0:T(1,128)} %broadcast_in_dim.76), calls=%async_computation | async-start | bytes 8192 | tf_op jit(solution)/shard_map/all_to_all | solution.py:95
  87.1 7.3 %copy-start.3 = (s32[4]{0:T(128)S(1)}, s32[4]{0:T(128)}, u32[]{:S(2)}) copy-start(s32[4]{0:T(128)} %constant.97.clone) | copy-start | bytes 52
  88.6 29.4 %all-to-all-start.2 = ((bf16[8,128,1024]{2,1,0:T(8,128)(2,1)}), bf16[8,128,1024]{2,1,0:T(8,128)(2,1)S(1)}, u32[]{:S(2)}, u32[]{:S(2)}) async-start(bf16[8,128,1024]{2,1,0:T(8,128)(2,1)} %bitcast.40), calls=%async_computation.2 | async-start | bytes 4194304 | tf_op jit(solution)/shard_map/all_to_all | solution.py:141
  118.0 1.4 copy-start.2
  150.8 29.3 %all-to-all-start.3 = ((bf16[8,8,16,1024]{3,1,2,0:T(8,128)(2,1)}), bf16[8,8,16,1024]{3,1,2,0:T(8,128)(2,1)S(1)}, u32[]{:S(2)}, u32[]{:S(2)}) async-start(bf16[8,8,16,1024]{3,1,2,0:T(8,128)(2,1)} %broadcast_in_dim.81), calls=%async_computation.3 | async-start | bytes 4194304 | tf_op jit(solution)/shard_map/all_to_all | solution.py:203
  188.0 3.8 %collective-permute-start = (bf16[512,1600]{0,1:T(8,128)(2,1)}, bf16[512,1600]{0,1:T(8,128)(2,1)}, u32[]{:S(2)}, u32[]{:S(2)}) collective-permute-start(bf16[512,1600]{0,1:T(8,128)(2,1)} %convolution_convert_fusion), channel_id=1, source_target_pairs={{0,1},{1,0},{2,3},{3,2},{4,5},{5,4},{6,7},{7,6},{8,9},{9,8},{10,11... | collective-permute-start | bytes 4915208 | tf_op jit(solution)/shard_map/ppermute | solution.py:222
  196.4 43.4 %copy-start.1 = (bf16[128,12800]{1,0:T(8,128)(2,1)S(1)}, bf16[128,12800]{1,0:T(8,128)(2,1)}, u32[]{:S(2)}) copy-start(bf16[128,12800]{1,0:T(8,128)(2,1)} %rows_ref.3) | copy-start | bytes 9830404
  196.4 21.9 %collective-permute-start.1 = (bf16[256,1600]{0,1:T(8,128)(2,1)S(1)}, bf16[256,1600]{0,1:T(8,128)(2,1)S(1)}, u32[]{:S(2)}, u32[]{:S(2)}) collective-permute-start(bf16[256,1600]{0,1:T(8,128)(2,1)S(1)} %slice.42), channel_id=1, source_target_pairs={{0,2},{1,3},{2,0},{3,1},{4,6},{5,7},{6,4},{7,5},{8,10},{9,11},{10,... | collective-permute-start | bytes 2457608 | tf_op jit(solution)/shard_map/ppermute | solution.py:225
  221.6 18.1 %all-to-all-start.4 = ((bf16[8,32,1600]{2,1,0:T(8,128)(2,1)}), bf16[8,32,1600]{2,1,0:T(8,128)(2,1)}, u32[]{:S(2)}, u32[]{:S(2)}) async-start(bf16[8,32,1600]{2,1,0:T(8,128)(2,1)} %bitcast.41), calls=%async_computation.4 | async-start | bytes 1703936 | tf_op jit(solution)/shard_map/all_to_all | solution.py:227
Sparse Core Ops, SparseCore 0:
  9.8 49.0 all-gather.1

commit v2 on v1

v2 whole, which is shorter than its diff:
```python
import functools

import jax
import jax.numpy as jnp
from jax import lax
from jax.experimental import pallas as pl
from jax.experimental.pallas import tpu as pltpu
from jax.sharding import PartitionSpec as P

UNIT = 16
LANES = 128
VISION_EPS = 1e-05
EPSILON = 1e-06
HALF_ROOT = 0.7071067811865476
INV_ROOT_TWO_PI = 0.3989422804014327
BF = jnp.bfloat16
F32 = jnp.float32
VMEM = pl.BlockSpec(memory_space=pltpu.VMEM)
SMEM = pl.BlockSpec(memory_space=pltpu.SMEM)
PARAMS = pltpu.CompilerParams(vmem_limit_bytes=40 * 2**20)
NT = (((1,), (1,)), ((), ()))


def shape(dims, dtype):
    return jax.ShapeDtypeStruct(dims, dtype)


def norm_kernel(chunk, order_ref, live_ref, spot_ref, rows_ref, gain_ref, bias_ref, out_ref):
    step = pl.program_id(0)
    wide = rows_ref[...].astype(F32)
    centered = wide - jnp.mean(wide, axis=1, keepdims=True)
    inv = lax.rsqrt(jnp.mean(centered * centered, axis=1, keepdims=True) + VISION_EPS)
    normed = (centered * inv * gain_ref[...] + bias_ref[...]).astype(BF)
    parts, _, padded = out_ref.shape
    lane = lax.broadcasted_iota(jnp.int32, (UNIT, padded - chunk), 1)
    note = jnp.where(lane == 0, order_ref[step], jnp.where(lane == 1, live_ref[step], spot_ref[step]))
    note = note.astype(F32).astype(BF)
    for k in range(parts):
        out_ref[k] = jnp.concatenate([normed[:, k * chunk : (k + 1) * chunk], note], axis=1)


def forward_kernel(core_ref, own_ref, other_ref, weight_ref, out_ref):
    step = pl.program_id(0)
    steps = pl.num_programs(0)

    def work(ref):
        sections, pair, depth = ref.shape
        product = jnp.dot(
            ref[...].reshape(sections * pair, depth), weight_ref[...], preferred_element_type=F32
        ).astype(BF)
        product = product.reshape(sections, pair, product.shape[1])
        for j in range(pair // UNIT):
            out_ref[j] = product[:, j * UNIT : (j + 1) * UNIT].reshape(sections * UNIT, -1)

    @pl.when(step < steps // 2)
    def _():
        work(own_ref)

    @pl.when(step >= steps // 2)
    def _():
        work(other_ref)


def slots_kernel(
    source_ref, live_ref, parts_ref, text_ref, cot_ref, gain_ref, hidden_ref, slope_ref, stat_ref
):
    stats = []
    for q in range(text_ref.shape[0] // UNIT):
        rows = pl.ds(q * UNIT, UNIT)
        from_rows = pl.ds(pl.multiple_of(source_ref[q] * UNIT, UNIT), UNIT)
        projected = parts_ref[0, from_rows].astype(F32)
        for k in range(1, parts_ref.shape[0]):
            projected = projected + parts_ref[k, from_rows].astype(F32)
        gate = 0.5 * (1.0 + lax.erf(projected * HALF_ROOT))
        hidden = jnp.where(live_ref[q] > 0, (projected * gate).astype(BF), text_ref[rows])
        hidden_ref[rows] = hidden
        slope_ref[rows] = gate + projected * jnp.exp(-0.5 * projected * projected) * INV_ROOT_TWO_PI
        wide = hidden.astype(F32)
        upstream = cot_ref[rows].astype(F32) * gain_ref[...]
        square = jnp.sum(wide * wide, axis=1, keepdims=True)
        cross = jnp.sum(upstream * wide, axis=1, keepdims=True)
        lane = lax.broadcasted_iota(jnp.int32, (UNIT, LANES), 1)
        stats.append(jnp.where(lane == 0, square, cross))
    stat_ref[...] = jnp.transpose(jnp.concatenate(stats, axis=0))[: stat_ref.shape[0]]


def row_scales(stat_ref, width):
    stat = stat_ref[...] / width
    pad = jnp.zeros((LANES - stat.shape[0], LANES), F32)
    stat = jnp.transpose(jnp.concatenate([stat, pad], axis=0))
    return lax.rsqrt(stat[:, 0:1] + EPSILON), stat[:, 1:2]


def grad_kernel(
    width, source_ref, live_ref, hidden_ref, slope_ref, cot_ref, gain_ref, stat_ref, grad_ref
):
    inv_all, cross_all = row_scales(stat_ref, width)
    for q in range(hidden_ref.shape[0] // UNIT):
        rows = slice(q * UNIT, (q + 1) * UNIT)
        inv, cross = inv_all[rows], cross_all[rows]
        wide = hidden_ref[rows].astype(F32)
        upstream = cot_ref[rows].astype(F32) * gain_ref[...]
        hidden_grad = (inv * (upstream - wide * inv * inv * cross)).astype(BF)
        grad = (hidden_grad.astype(F32) * slope_ref[rows]).astype(BF)
        grad = jnp.where(live_ref[q] > 0, grad, jnp.zeros_like(grad))
        to_rows = pl.ds(pl.multiple_of(source_ref[q] * UNIT, UNIT), UNIT)
        for k in range(grad_ref.shape[0]):
            grad_ref[k, to_rows] = grad


def normed_kernel(width, hidden_ref, gain_ref, stat_ref, normed_ref):
    inv, _ = row_scales(stat_ref, width)
    normed_ref[...] = (hidden_ref[...].astype(F32) * inv * gain_ref[...]).astype(BF)


def picked(pick_ref, grads_ref, first, count):
    return jnp.concatenate([grads_ref[pick_ref[first + m]] for m in range(count)], axis=0)


def give_kernel(pick_ref, grads_ref, weight_ref, out_ref):
    rows = out_ref.shape[0]
    count = rows // UNIT
    grad = picked(pick_ref, grads_ref, pl.program_id(0) * count, count)
    out_ref[...] = lax.dot_general(grad, weight_ref[...], NT, preferred_element_type=F32).astype(BF)


def far_kernel(first, pick_ref, grads_ref, weight_ref, got_ref, *out_refs):
    grad = picked(pick_ref, grads_ref, first, got_ref.shape[0] // UNIT)
    total = lax.dot_general(grad, weight_ref[...], NT, preferred_element_type=F32)
    total = (total + got_ref[...].astype(F32)).astype(BF)
    rows = out_refs[0].shape[0]
    for j, ref in enumerate(out_refs):
        ref[...] = total[j * rows : (j + 1) * rows]


def near_kernel(first, pick_ref, grads_ref, weight_ref, got_ref, out_ref):
    grad = picked(pick_ref, grads_ref, first, got_ref.shape[0] // UNIT)
    total = lax.dot_general(grad, weight_ref[...], NT, preferred_element_type=F32)
    out_ref[...] = total + got_ref[...].astype(F32)


def sum_kernel(near_ref, *refs):
    out_ref = refs[-1]
    sections, share, _ = out_ref.shape
    rows = refs[0].shape[0]
    for s in range(sections):
        j, at = divmod(s * share, rows)
        far = refs[j][at : at + share].astype(F32)
        out_ref[s] = (near_ref[s * share : (s + 1) * share] + far).astype(BF)


def final_kernel(chunk, first_ref, parts_ref, rows_ref, gain_ref, out_ref):
    wide = rows_ref[...].astype(F32)
    centered = wide - jnp.mean(wide, axis=1, keepdims=True)
    inv = lax.rsqrt(jnp.mean(centered * centered, axis=1, keepdims=True) + VISION_EPS)
    hat = centered * inv
    grad = jnp.concatenate([parts_ref[k][:, :chunk] for k in range(parts_ref.shape[0])], axis=1)
    weighted = grad.astype(F32) * gain_ref[...]
    weighted_mean = jnp.mean(weighted, axis=1, keepdims=True)
    cross = jnp.mean(weighted * hat, axis=1, keepdims=True)
    out_ref[...] = (inv * (weighted - weighted_mean - hat * cross)).astype(BF)


def ring_gather(block, rows):
    groups = lax.axis_size("dp")
    me = lax.axis_index("dp")
    height = block.shape[0]
    up = [(i, (i + 1) % groups) for i in range(groups)]
    down = [(i, (i - 1) % groups) for i in range(groups)]
    out = jnp.zeros((rows, block.shape[1]), block.dtype)

    def put(out, piece, owner, start=0):
        return lax.dynamic_update_slice_in_dim(out, piece, (owner % groups) * height + start, 0)

    out = put(out, block, me)
    rising = falling = block
    full = (groups - 1) // 2
    for hop in range(1, full + 1):
        rising = lax.ppermute(rising, "dp", up)
        falling = lax.ppermute(falling, "dp", down)
        out = put(out, rising, me - hop + groups)
        out = put(out, falling, me + hop)
    if groups % 2 == 0:
        if groups > 1:
            cut = height // 16 * 8
            opposite = me + groups // 2
            out = put(out, lax.ppermute(rising[:cut], "dp", up), opposite)
            out = put(out, lax.ppermute(falling[cut:], "dp", down), opposite, cut)
    return out


def fill_places(wanted, alive, places):
    taken = jnp.any((wanted[..., :, None] == places) & alive[..., :, None], axis=-2)
    free_rank = jnp.cumsum(~taken, axis=-1) - 1
    dead_rank = jnp.cumsum(~alive, axis=-1) - 1
    fits = (~taken)[..., None, :] & (free_rank[..., None, :] == dead_rank[..., :, None])
    filler = jnp.sum(jnp.where(fits, places, 0), axis=-1)
    return jnp.where(alive, wanted, filler).astype(jnp.int32)


def inverse(place, places):
    return jnp.sum(
        jnp.where(place[..., :, None] == places, places[:, None], 0), axis=-2
    ).astype(jnp.int32)


def shards(
    width, vision_rows, vision_gain, vision_bias, proj_weight, text_rows, text_gain, slot_of_row, out_cotangent
):
    sections = lax.axis_size("section")
    groups = lax.axis_size("dp")
    tensors = lax.axis_size("tensor")
    rows, depth = vision_rows.shape
    slots, columns = text_rows.shape
    units = rows // UNIT
    chunk = depth // sections
    padded = -(-(chunk + 3) // LANES) * LANES
    section = lax.axis_index("section")
    tensor = lax.axis_index("tensor")
    core = tensor % 2
    places = jnp.arange(units)
    other_core = [(i, i ^ 1) for i in range(tensors)]
    other_y = [(i, i ^ 2) for i in range(tensors)]

    gain_row = vision_gain.reshape(1, depth)
    text_gain_row = text_gain.reshape(1, columns)
    weight = ring_gather(proj_weight, padded)

    unit_slot = slot_of_row.reshape(units, UNIT)[:, 0]
    alive = unit_slot >= 0
    safe = jnp.where(alive, unit_slot, 0)
    order = inverse(fill_places(safe // (slots * groups), alive, places), places)
    half = units // 2
    own = lax.dynamic_slice_in_dim(order, core * half, half)
    chosen = own[:, None] == places
    live = jnp.sum(jnp.where(chosen, alive, 0), axis=1).astype(jnp.int32)
    spot = jnp.sum(jnp.where(chosen, safe // UNIT % (slots // UNIT), 0), axis=1).astype(jnp.int32)
    sent = pl.pallas_call(
        functools.partial(norm_kernel, chunk),
        out_shape=shape((sections, half * UNIT, padded), BF),
        grid_spec=pltpu.PrefetchScalarGridSpec(
            num_scalar_prefetch=3,
            grid=(half,),
            in_specs=[
                pl.BlockSpec((UNIT, depth), lambda i, order, live, spot: (order[i], 0)),
                pl.BlockSpec((1, depth), lambda i, order, live, spot: (0, 0)),
                pl.BlockSpec((1, depth), lambda i, order, live, spot: (0, 0)),
            ],
            out_specs=pl.BlockSpec(
                (sections, UNIT, padded), lambda i, order, live, spot: (0, i, 0)
            ),
        ),
        compiler_params=PARAMS,
        name="vision_norm",
    )(own, live, spot, vision_rows, gain_row, vision_bias.reshape(1, depth))
    from_own = lax.all_to_all(sent, "section", 0, 0, tiled=True)
    from_other = lax.ppermute(from_own, "tensor", other_core)

    pair = 2 * UNIT
    partial = pl.pallas_call(
        forward_kernel,
        out_shape=shape((units, sections * UNIT, columns), BF),
        grid_spec=pltpu.PrefetchScalarGridSpec(
            num_scalar_prefetch=1,
            grid=(half,),
            in_specs=[
                pl.BlockSpec(
                    (sections, pair, padded), lambda i, core: (0, jnp.minimum(i, half // 2 - 1), 0)
                ),
                pl.BlockSpec(
                    (sections, pair, padded), lambda i, core: (0, jnp.maximum(i - half // 2, 0), 0)
                ),
                pl.BlockSpec((padded, columns), lambda i, core: (0, 0)),
            ],
            out_specs=pl.BlockSpec(
                (2, sections * UNIT, columns),
                lambda i, core: ((i + core[0] * (half // 2)) % half, 0, 0),
            ),
        ),
        compiler_params=PARAMS,
        name="forward",
    )(core.reshape(1).astype(jnp.int32), from_own, from_other, weight)
    partial = lax.all_to_all(partial, "section", 0, 0, tiled=True)

    def notes(array):
        return array[:, ::UNIT, chunk : chunk + 3].astype(jnp.int32)

    first, second = notes(from_own), notes(from_other)
    table = jnp.where(
        core == 0,
        jnp.concatenate([first, second], axis=1),
        jnp.concatenate([second, first], axis=1),
    )
    here = lax.dynamic_slice_in_dim(table, section, 1, 1)[:, 0]
    has = here[:, 1] > 0
    spots = jnp.arange(sections)
    source = inverse(fill_places(here[:, 2], has, spots), spots)
    filled = jnp.sum(jnp.where(source[:, None] == spots, has, 0), axis=1).astype(jnp.int32)
    place = inverse(table[:, :, 0], places)

    hidden, slope, stat = pl.pallas_call(
        slots_kernel,
        out_shape=(
            shape((slots, columns), BF),
            shape((slots, columns), F32),
            shape((8, slots), F32),
        ),
        in_specs=[SMEM, SMEM, VMEM, VMEM, VMEM, VMEM],
        out_specs=(VMEM, VMEM, VMEM),
        compiler_params=PARAMS,
        name="slots",
    )(source, filled, partial, text_rows, out_cotangent, text_gain_row)
    stat = stat + lax.ppermute(stat, "tensor", other_core)
    stat = stat + lax.ppermute(stat, "tensor", other_y)
    grads = pl.pallas_call(
        functools.partial(grad_kernel, width),
        out_shape=shape((sections, sections * UNIT, columns), BF),
        in_specs=[SMEM, SMEM, VMEM, VMEM, VMEM, VMEM, VMEM],
        out_specs=VMEM,
        compiler_params=PARAMS,
        name="grads",
    )(source, filled, hidden, slope, out_cotangent, text_gain_row, stat)
    grads = lax.all_to_all(grads, "section", 0, 0, tiled=True)
    grads = grads.reshape(sections * sections, UNIT, columns)
    normed = pl.pallas_call(
        functools.partial(normed_kernel, width),
        out_shape=shape((slots, columns), BF),
        in_specs=[VMEM, VMEM, VMEM],
        out_specs=VMEM,
        compiler_params=PARAMS,
        name="normed",
    )(hidden, text_gain_row, stat)

    share = units // tensors
    relative = jnp.array([3, 1, 2, 0]) ^ tensor
    runs = relative[:, None] * share + jnp.arange(share)
    hit = runs[:, None, :, None] == places
    pick = jnp.sum(jnp.where(hit, place[None, :, None, :], 0), axis=3)
    pick = (pick * sections + spots[None, :, None]).reshape(-1).astype(jnp.int32)
    quarter = sections * share * UNIT
    runs_quarter = sections * share
    whole = [SMEM, VMEM, VMEM]
    given = pl.pallas_call(
        give_kernel,
        out_shape=shape((2 * quarter, padded), BF),
        grid_spec=pltpu.PrefetchScalarGridSpec(
            num_scalar_prefetch=1,
            grid=(2,),
            in_specs=[
                pl.BlockSpec((sections * sections, UNIT, columns), lambda i, pick: (0, 0, 0)),
                pl.BlockSpec((padded, columns), lambda i, pick: (0, 0)),
            ],
            out_specs=pl.BlockSpec((quarter, padded), lambda i, pick: (i, 0)),
        ),
        compiler_params=PARAMS,
        name="give",
    )(pick, grads, weight)
    got = lax.ppermute(given, "tensor", other_core)
    pieces = 4
    far = pl.pallas_call(
        functools.partial(far_kernel, 2 * runs_quarter),
        out_shape=tuple(shape((quarter // pieces, padded), BF) for _ in range(pieces)),
        grid=(1,),
        in_specs=[
            SMEM,
            pl.BlockSpec((sections * sections, UNIT, columns), lambda i: (0, 0, 0)),
            pl.BlockSpec((padded, columns), lambda i: (0, 0)),
            pl.BlockSpec((quarter, padded), lambda i: (0, 0)),
        ],
        out_specs=tuple(
            pl.BlockSpec((quarter // pieces, padded), lambda i: (0, 0)) for _ in range(pieces)
        ),
        compiler_params=PARAMS,
        name="far",
    )(pick, grads, weight, got)
    far = [lax.ppermute(piece, "tensor", other_y) for piece in far]
    near = pl.pallas_call(
        functools.partial(near_kernel, 3 * runs_quarter),
        out_shape=shape((quarter, padded), F32),
        grid=(1,),
        in_specs=[
            SMEM,
            pl.BlockSpec((sections * sections, UNIT, columns), lambda i: (0, 0, 0)),
            pl.BlockSpec((padded, columns), lambda i: (0, 0)),
            pl.BlockSpec((quarter, padded), lambda i: (1, 0)),
        ],
        out_specs=pl.BlockSpec((quarter, padded), lambda i: (0, 0)),
        compiler_params=PARAMS,
        name="near",
    )(pick, grads, weight, got)
    total = pl.pallas_call(
        sum_kernel,
        out_shape=shape((sections, share * UNIT, padded), BF),
        in_specs=[VMEM] * (1 + pieces),
        out_specs=VMEM,
        compiler_params=PARAMS,
        name="total",
    )(near, *far)
    back = lax.all_to_all(total, "section", 0, 0, tiled=True)
    vision_grad = pl.pallas_call(
        functools.partial(final_kernel, chunk),
        out_shape=shape((share * UNIT, depth), BF),
        grid_spec=pltpu.PrefetchScalarGridSpec(
            num_scalar_prefetch=1,
            grid=(share,),
            in_specs=[
                pl.BlockSpec((sections, UNIT, padded), lambda i, first: (0, i, 0)),
                pl.BlockSpec((UNIT, depth), lambda i, first: (first[0] + i, 0)),
                pl.BlockSpec((1, depth), lambda i, first: (0, 0)),
            ],
            out_specs=pl.BlockSpec((UNIT, depth), lambda i, first: (i, 0)),
        ),
        compiler_params=PARAMS,
        name="vision_back",
    )((tensor * share).reshape(1).astype(jnp.int32), back, vision_rows, gain_row)
    return normed, vision_grad


def solution(mesh):
    in_specs = (
        P(("section", "dp"), None),
        P(),
        P(),
        P(("section", "dp"), "tensor"),
        P(("section", "dp"), "tensor"),
        P("tensor"),
        P(("section", "dp")),
        P(("section", "dp"), "tensor"),
    )
    out_specs = (P(("section", "dp"), "tensor"), P(("section", "dp", "tensor"), None))

    def program(*args):
        body = functools.partial(shards, args[4].shape[1])
        return jax.shard_map(
            body, mesh=mesh, in_specs=in_specs, out_specs=out_specs, check_vma=False
        )(*args)

    return program
```

time: 253 us -> 216 us (0.85)
  blocking collectives: 16.6 us -> 0 us
  matrix products: 15.9 us -> 0 us
  between operations: 14.2 us -> 0.98 us
  starting transfers between devices: 39.4 us -> 51 us
  waiting for transfers between devices: 116 us -> 109 us
  Pallas kernels: 21 us -> 27.7 us
    ppermute x1 -> x15, starting transfers between devices: 2.14 us -> 27.4 us  [the longest x3 11.3 us: ring_gather(): falling = lax.ppermute(falling, 'dp', down)]
    all_to_all x5 -> x4, waiting for transfers between devices: 93.6 us -> 70.8 us  [the longest x1 24.3 us: shards(): grads = lax.all_to_all(grads, 'section', 0, 0, tiled=True)]
    psum x1 -> x0, blocking collectives: 16.6 us -> none  [shards(): stat = lax.psum(stat, 'tensor')]
    dot_general x3 -> x0, matrix products: 15.9 us -> none  [the longest x2 9.7 us: product(): lax.dot_general(picked, weight, (((1,), (1,)), ((), ())), preferred_eleme...]
    ppermute x1 -> x15, waiting for transfers between devices: 19.7 us -> 34.5 us  [the longest x3 14.2 us: ring_gather(): rising = lax.ppermute(rising, 'dp', up)]
    all_to_all x5 -> x4, starting transfers between devices: 37.2 us -> 23.5 us  [the longest x1 6.38 us: shards(): from_own = lax.all_to_all(sent, 'section', 0, 0, tiled=True)]
    pallas_call x4 -> x10, Pallas kernels: 21 us -> 27.7 us  [the longest x1 6.04 us: shards(): pl.pallas_call(forward_kernel, out_shape=shape((units, sections * UNIT, c...]
    unnamed x8 -> x30, local copies, waits for them, and re-layouts: 3.3 us -> 9.8 us
  transfers between devices with their start and end apart: 8 -> 20, of which waited for: 6 -> 13; matrix products, arithmetic and copies ran while one was open for 8% -> 5% of each run, Pallas kernels for 2% -> 2%
where the time goes in v2:
time: 216 us; the launch traced here: 213 us
  waiting for transfers between devices  109 us (50%)
  starting transfers between devices  51 us (24%)
  Pallas kernels  27.7 us (13%)
  local copies, waits for them, and re-layouts  21.3 us (10%)
  other arithmetic  2.98 us (1%)
    all_to_all x1, waiting for transfers between devices, shards(): grads = lax.all_to_all(grads, 'section', 0, 0, tiled=True)  24.3 us
    all_to_all x1, waiting for transfers between devices, shards(): partial = lax.all_to_all(partial, 'section', 0, 0, tiled=True)  19.9 us
    all_to_all x1, waiting for transfers between devices, shards(): from_own = lax.all_to_all(sent, 'section', 0, 0, tiled=True)  15.4 us
    ppermute x3, waiting for transfers between devices, ring_gather(): rising = lax.ppermute(rising, 'dp', up)  14.2 us
    ppermute x4, waiting for transfers between devices, shards(): far = [lax.ppermute(piece, 'tensor', other_y) for piece in far]  12.6 us
    ppermute x3, starting transfers between devices, ring_gather(): falling = lax.ppermute(falling, 'dp', down)  11.3 us
    all_to_all x1, waiting for transfers between devices, shards(): back = lax.all_to_all(total, 'section', 0, 0, tiled=True)  11.1 us
    unnamed x30, local copies, waits for them, and re-layouts  9.8 us
  transfers between devices with their start and end apart: 20, of which 13 were waited for; matrix products, arithmetic and copies ran while one was open for 5% of the time, Pallas kernels for 2%

profile of v2, /device:TPU:8, one launch (start us, length us, event | category | flops | bytes accessed | tf_op | source)
XLA Modules:
  0.0 212.9 jit_solution(10084398629598611752)
XLA Ops:
  0.6 0.7 reshape.184
  2.0 0.2 select_reduce_fusion.8
  2.6 0.8 reshape.185.gain_ref
  3.4 0.9 reshape.186.bias_ref
  4.4 0.2 select_reduce_fusion.9
  4.6 1.9 copy-done
  6.5 3.9 %vision_norm.1 = bf16[8,64,1664]{2,1,0:T(8,128)(2,1)} custom-call(s32[4]{0:T(128)S(1)} %dynamic_slice.6.order_ref, s32[4]{0:T(128)S(1)} %get-tuple-element.19.live_ref, s32[4]{0:T(128)S(1)} %get-tuple-element.18.spot_ref, bf16[128,12800]{1,0:T(8,128)(2,1)S(1)} %copy-done, f32[1,12800]{1,0:T(1,128)S(1)} %reshape.185.gain_ref, f32[1,12800]{1,0:T(1,128)S(1)} %reshape.186.bias_ref), custom_call_target="tpu_custom_call" | custom-call | tf_op jit(solution)/shard_map/vision_norm/pallas_call | solution.py:238
  10.4 6.4 %all-to-all-start = ((bf16[8,64,1664]{2,1,0:T(8,128)(2,1)}), bf16[8,64,1664]{2,1,0:T(8,128)(2,1)}, u32[]{:S(2)}, u32[]{:S(2)}) async-start(bf16[8,64,1664]{2,1,0:T(8,128)(2,1)} %vision_norm.1), calls=%async_computation | async-start | bytes 3407872 | tf_op jit(solution)/shard_map/all_to_all | solution.py:256
  16.8 1.3 collective-permute-start.1
  18.1 4.0 %collective-permute-start.2 = (bf16[200,1024]{1,0:T(8,128)(2,1)S(1)}, bf16[200,1024]{1,0:T(8,128)(2,1)}, u32[]{:S(2)}, u32[]{:S(2)}) collective-permute-start(bf16[200,1024]{1,0:T(8,128)(2,1)S(1)} %copy-done.13), channel_id=1, source_target_pairs={{0,28},{4,0},{8,4},{12,8},{16,12},{20,16},{24,20},{28,24},{1,29},{... | collective-permute-start | bytes 1228808 | tf_op jit(solution)/shard_map/ppermute | solution.py:180
  22.1 15.4 %all-to-all-done.own_ref = bf16[8,64,1664]{2,1,0:T(8,128)(2,1)} async-done(((bf16[8,64,1664]{2,1,0:T(8,128)(2,1)}), bf16[8,64,1664]{2,1,0:T(8,128)(2,1)}, u32[]{:S(2)}, u32[]{:S(2)}) %all-to-all-start) | async-done | bytes 1703968 | tf_op jit(solution)/shard_map/all_to_all | solution.py:256
  37.5 1.9 collective-permute-start.3
  39.4 4.0 %collective-permute-start.4 = (bf16[200,1024]{1,0:T(8,128)(2,1)}, bf16[200,1024]{1,0:T(8,128)(2,1)}, u32[]{:S(2)}, u32[]{:S(2)}) collective-permute-start(bf16[200,1024]{1,0:T(8,128)(2,1)} %collective-permute-done.2), channel_id=1, source_target_pairs={{0,28},{4,0},{8,4},{12,8},{16,12},{20,16},{24,20},{28,24},{1,29},{... | collective-permute-start | bytes 1228808 | tf_op jit(solution)/shard_map/ppermute | solution.py:180
  43.5 0.4 broadcast_in_dim.123
  43.9 1.0 constant_dynamic-update-slice_fusion.8
  44.9 8.9 %collective-permute-done.3 = bf16[200,1024]{1,0:T(8,128)(2,1)} collective-permute-done((bf16[200,1024]{1,0:T(8,128)(2,1)}, bf16[200,1024]{1,0:T(8,128)(2,1)}, u32[]{:S(2)}, u32[]{:S(2)}) %collective-permute-start.3) | collective-permute-done | bytes 409632 | tf_op jit(solution)/shard_map/ppermute | solution.py:179
  53.8 3.2 %collective-permute-start.6 = (bf16[200,1024]{1,0:T(8,128)(2,1)}, bf16[200,1024]{1,0:T(8,128)(2,1)S(1)}, u32[]{:S(2)}, u32[]{:S(2)}) collective-permute-start(bf16[200,1024]{1,0:T(8,128)(2,1)} %collective-permute-done.4), channel_id=1, source_target_pairs={{0,28},{4,0},{8,4},{12,8},{16,12},{20,16},{24,20},{28,24},{1,29},{... | collective-permute-start | bytes 1228808 | tf_op jit(solution)/shard_map/ppermute | solution.py:180
  57.1 1.0 constant_dynamic-update-slice_fusion.7
  58.1 1.0 constant_dynamic-update-slice_fusion.6
  59.1 1.0 constant_dynamic-update-slice_fusion.5
  60.2 1.0 constant_dynamic-update-slice_fusion.4
  61.2 5.3 %collective-permute-done.5 = bf16[200,1024]{1,0:T(8,128)(2,1)S(1)} collective-permute-done((bf16[200,1024]{1,0:T(8,128)(2,1)}, bf16[200,1024]{1,0:T(8,128)(2,1)S(1)}, u32[]{:S(2)}, u32[]{:S(2)}) %collective-permute-start.5) | collective-permute-done | bytes 409632 | tf_op jit(solution)/shard_map/ppermute | solution.py:179
  66.7 3.3 %collective-permute-start.8 = (bf16[104,1024]{1,0:T(8,128)(2,1)S(1)}, bf16[104,1024]{1,0:T(8,128)(2,1)S(1)}, u32[]{:S(2)}, u32[]{:S(2)}) collective-permute-start(bf16[104,1024]{1,0:T(8,128)(2,1)S(1)} %slice.33), channel_id=1, source_target_pairs={{0,28},{4,0},{8,4},{12,8},{16,12},{20,16},{24,20},{28,24},{1,29},{... | collective-permute-start | bytes 638984 | tf_op jit(solution)/shard_map/ppermute | solution.py:188
  70.1 3.7 %collective-permute-done.7 = bf16[96,1024]{1,0:T(8,128)(2,1)S(1)} collective-permute-done((bf16[96,1024]{1,0:T(8,128)(2,1)S(1)}, bf16[96,1024]{1,0:T(8,128)(2,1)S(1)}, u32[]{:S(2)}, u32[]{:S(2)}) %collective-permute-start.7) | collective-permute-done | bytes 196640 | tf_op jit(solution)/shard_map/ppermute | solution.py:187
  73.8 6.0 %forward.1 = bf16[8,128,1024]{2,1,0:T(8,128)(2,1)S(1)} custom-call(s32[1]{0:T(128)} %bitcast.5.core_ref, bf16[8,64,1664]{2,1,0:T(8,128)(2,1)} %all-to-all-done.own_ref, bf16[8,64,1664]{2,1,0:T(8,128)(2,1)} %collective-permute-done.other_ref, bf16[1664,1024]{1,0:T(8,128)(2,1)S(1)} %constant_dynamic-update-slice_fusion.weight_ref), custom_call_target="tpu_custom_call" | custom-call | tf_op jit(solution)/shard_map/forward/pallas_call | solution.py:260
  79.9 1.3 copy-done.2
  81.2 5.8 %all-to-all-start.1 = ((bf16[8,128,1024]{2,1,0:T(8,128)(2,1)}), bf16[8,128,1024]{2,1,0:T(8,128)(2,1)}, u32[]{:S(2)}, u32[]{:S(2)}) async-start(bf16[8,128,1024]{2,1,0:T(8,128)(2,1)} %copy-done.2), calls=%async_computation.1 | async-start | bytes 4194304 | tf_op jit(solution)/shard_map/all_to_all | solution.py:283
  87.0 1.0 slice.25
  88.1 1.0 slice.26
  90.5 0.2 select_reduce_fusion.5
  90.7 0.2 select_reduce_fusion.4
  91.0 0.2 select_reduce_fusion.2.live_ref
  91.2 19.9 %all-to-all-done.1.parts_ref = bf16[8,128,1024]{2,1,0:T(8,128)(2,1)} async-done(((bf16[8,128,1024]{2,1,0:T(8,128)(2,1)}), bf16[8,128,1024]{2,1,0:T(8,128)(2,1)}, u32[]{:S(2)}, u32[]{:S(2)}) %all-to-all-start.1) | async-done | bytes 2097184 | tf_op jit(solution)/shard_map/all_to_all | solution.py:283
  111.1 0.9 copy-done.5
  112.1 0.9 copy-done.11
  113.0 2.3 %slots.1 = (bf16[128,1024]{1,0:T(8,128)(2,1)S(1)}, f32[128,1024]{1,0:T(8,128)S(1)}, f32[8,128]{1,0:T(8,128)S(1)}) custom-call(s32[8]{0:T(128)S(1)} %select_reduce_fusion.3.source_ref, s32[8]{0:T(128)S(1)} %select_reduce_fusion.2.live_ref, bf16[8,128,1024]{2,1,0:T(8,128)(2,1)} %all-to-all-done.1.parts_ref, bf16[128,1024]{1,0:T(8,128)(2,1)S(1)} %copy-done.11, ...), custom_call_target="tpu_custom_call" | custom-call | tf_op jit(solution)/shard_map/slots/pallas_call | solution.py:301
  115.4 1.2 collective-permute-done.9
  116.6 2.3 %collective-permute-start.10 = (f32[8,128]{1,0:T(8,128)S(1)}, f32[8,128]{1,0:T(8,128)S(1)}, u32[]{:S(2)}, u32[]{:S(2)}) collective-permute-start(f32[8,128]{1,0:T(8,128)S(1)} %add.195), channel_id=1, source_target_pairs={{0,2},{1,3},{2,0},{3,1},{4,6},{5,7},{6,4},{7,5},{8,10},{9,11},{10,... | collective-permute-start | bytes 12296 | tf_op jit(solution)/shard_map/ppermute | solution.py:314
  118.9 2.8 %collective-permute-done.10 = f32[8,128]{1,0:T(8,128)S(1)} collective-permute-done((f32[8,128]{1,0:T(8,128)S(1)}, f32[8,128]{1,0:T(8,128)S(1)}, u32[]{:S(2)}, u32[]{:S(2)}) %collective-permute-start.10) | collective-permute-done | bytes 4128 | tf_op jit(solution)/shard_map/ppermute | solution.py:314
  121.7 0.9 copy-done.6
  122.6 0.9 grads.1
  123.6 1.3 copy-done.3
  124.9 0.7 copy-done.7
  125.6 5.7 %all-to-all-start.2 = ((bf16[8,128,1024]{2,1,0:T(8,128)(2,1)}), bf16[8,128,1024]{2,1,0:T(8,128)(2,1)}, u32[]{:S(2)}, u32[]{:S(2)}) async-start(bf16[8,128,1024]{2,1,0:T(8,128)(2,1)} %copy-done.3), calls=%async_computation.2 | async-start | bytes 4194304 | tf_op jit(solution)/shard_map/all_to_all | solution.py:323
  131.6 0.2 select_reduce_fusion
  132.0 24.3 %all-to-all-done.2 = bf16[8,128,1024]{2,1,0:T(8,128)(2,1)} async-done(((bf16[8,128,1024]{2,1,0:T(8,128)(2,1)}), bf16[8,128,1024]{2,1,0:T(8,128)(2,1)}, u32[]{:S(2)}, u32[]{:S(2)}) %all-to-all-start.2) | async-done | bytes 2097184 | tf_op jit(solution)/shard_map/all_to_all | solution.py:323
  156.4 4.5 %give.1 = bf16[512,1664]{1,0:T(8,128)(2,1)S(1)} custom-call(s32[64]{0:T(128)S(1)} %add.202.pick_ref, bf16[64,16,1024]{2,1,0:T(8,128)(2,1)} %bitcast.9.grads_ref, bf16[1664,1024]{1,0:T(8,128)(2,1)S(1)} %constant_dynamic-update-slice_fusion.weight_ref), custom_call_target="tpu_custom_call" | custom-call | tf_op jit(solution)/shard_map/give/pallas_call | solution.py:343
  160.9 3.6 %collective-permute-done.11.got_ref = bf16[512,1664]{1,0:T(8,128)(2,1)S(1)} collective-permute-done((bf16[512,1664]{1,0:T(8,128)(2,1)S(1)}, bf16[512,1664]{1,0:T(8,128)(2,1)S(1)}, u32[]{:S(2)}, u32[]{:S(2)}) %collective-permute-start.11) | collective-permute-done | bytes 1703968 | tf_op jit(solution)/shard_map/ppermute | solution.py:358
  164.5 2.7 %far.1 = (bf16[64,1664]{1,0:T(8,128)(2,1)S(1)}, bf16[64,1664]{1,0:T(8,128)(2,1)S(1)}, bf16[64,1664]{1,0:T(8,128)(2,1)S(1)}, bf16[64,1664]{1,0:T(8,128)(2,1)S(1)}) custom-call(s32[64]{0:T(128)S(1)} %add.202.pick_ref, bf16[64,16,1024]{2,1,0:T(8,128)(2,1)} %bitcast.9.grads_ref, bf16[1664,1024]{1,0:T(8,128)(2,1)S(1)} %constant_dynamic-update-slice_fusion.weight_ref, ...), custom_call_target="tpu_custom_call" | custom-call | tf_op jit(solution)/shard_map/far/pallas_call | solution.py:360
  167.3 2.4 %collective-permute-start.12 = (bf16[64,1664]{1,0:T(8,128)(2,1)S(1)}, bf16[64,1664]{1,0:T(8,128)(2,1)S(1)}, u32[]{:S(2)}, u32[]{:S(2)}) collective-permute-start(bf16[64,1664]{1,0:T(8,128)(2,1)S(1)} %get-tuple-element.12), channel_id=1, source_target_pairs={{0,2},{1,3},{2,0},{3,1},{4,6},{5,7},{6,4},{7,5},{8,10},{9,11},{10,... | collective-permute-start | bytes 638984 | tf_op jit(solution)/shard_map/ppermute | solution.py:376
  169.6 1.2 collective-permute-start.13
  170.9 2.3 %collective-permute-start.14 = (bf16[64,1664]{1,0:T(8,128)(2,1)S(1)}, bf16[64,1664]{1,0:T(8,128)(2,1)S(1)}, u32[]{:S(2)}, u32[]{:S(2)}) collective-permute-start(bf16[64,1664]{1,0:T(8,128)(2,1)S(1)} %get-tuple-element.14), channel_id=1, source_target_pairs={{0,2},{1,3},{2,0},{3,1},{4,6},{5,7},{6,4},{7,5},{8,10},{9,11},{10,... | collective-permute-start | bytes 638984 | tf_op jit(solution)/shard_map/ppermute | solution.py:376
  173.2 1.2 collective-permute-start.15
  174.4 2.7 %near.1.near_ref = f32[256,1664]{1,0:T(8,128)S(1)} custom-call(s32[64]{0:T(128)S(1)} %add.202.pick_ref, bf16[64,16,1024]{2,1,0:T(8,128)(2,1)} %bitcast.9.grads_ref, bf16[1664,1024]{1,0:T(8,128)(2,1)S(1)} %constant_dynamic-update-slice_fusion.weight_ref, bf16[512,1664]{1,0:T(8,128)(2,1)S(1)} %collective-permute-done.11.got_ref), custom_call_target="tpu_custom_call" | custom-call | tf_op jit(solution)/shard_map/near/pallas_call | solution.py:377
  177.2 4.3 %collective-permute-done.13.refs_1_ = bf16[64,1664]{1,0:T(8,128)(2,1)S(1)} collective-permute-done((bf16[64,1664]{1,0:T(8,128)(2,1)S(1)}, bf16[64,1664]{1,0:T(8,128)(2,1)S(1)}, u32[]{:S(2)}, u32[]{:S(2)}) %collective-permute-start.13) | collective-permute-done | bytes 213024 | tf_op jit(solution)/shard_map/ppermute | solution.py:376
  181.5 4.6 %collective-permute-done.14.refs_2_ = bf16[64,1664]{1,0:T(8,128)(2,1)S(1)} collective-permute-done((bf16[64,1664]{1,0:T(8,128)(2,1)S(1)}, bf16[64,1664]{1,0:T(8,128)(2,1)S(1)}, u32[]{:S(2)}, u32[]{:S(2)}) %collective-permute-start.14) | collective-permute-done | bytes 213024 | tf_op jit(solution)/shard_map/ppermute | solution.py:376
  186.1 3.8 %collective-permute-done.15.refs_3_ = bf16[64,1664]{1,0:T(8,128)(2,1)S(1)} collective-permute-done((bf16[64,1664]{1,0:T(8,128)(2,1)S(1)}, bf16[64,1664]{1,0:T(8,128)(2,1)S(1)}, u32[]{:S(2)}, u32[]{:S(2)}) %collective-permute-start.15) | collective-permute-done | bytes 213024 | tf_op jit(solution)/shard_map/ppermute | solution.py:376
  189.8 0.2 total.1
  190.0 0.9 copy-done.4
  191.0 5.6 %all-to-all-start.3 = ((bf16[8,32,1664]{2,1,0:T(8,128)(2,1)}), bf16[8,32,1664]{2,1,0:T(8,128)(2,1)}, u32[]{:S(2)}, u32[]{:S(2)}) async-start(bf16[8,32,1664]{2,1,0:T(8,128)(2,1)} %copy-done.4), calls=%async_computation.3 | async-start | bytes 1703936 | tf_op jit(solution)/shard_map/all_to_all | solution.py:399
  196.6 0.9 normed.1
  197.5 11.1 %all-to-all-done.3.parts_ref = bf16[8,32,1664]{2,1,0:T(8,128)(2,1)} async-done(((bf16[8,32,1664]{2,1,0:T(8,128)(2,1)}), bf16[8,32,1664]{2,1,0:T(8,128)(2,1)}, u32[]{:S(2)}, u32[]{:S(2)}) %all-to-all-start.3) | async-done | bytes 852000 | tf_op jit(solution)/shard_map/all_to_all | solution.py:399
  208.5 0.8 copy-done.10
  209.3 3.5 %vision_back.1 = bf16[32,12800]{1,0:T(8,128)(2,1)} custom-call(s32[1]{0:T(128)} %bitcast.7.first_ref, bf16[8,32,1664]{2,1,0:T(8,128)(2,1)} %all-to-all-done.3.parts_ref, bf16[128,12800]{1,0:T(8,128)(2,1)S(1)} %copy-done.1, f32[1,12800]{1,0:T(1,128)S(1)} %copy-done.10), custom_call_target="tpu_custom_call" | custom-call | tf_op jit(solution)/shard_map/vision_back/pallas_call | solution.py:400
  (84 shorter events, 3.6 us)
Async XLA Ops:
  3.4 7.0 %copy-start.9 = (f32[1,12800]{1,0:T(1,128)}, f32[1,12800]{1,0:T(1,128)S(1)}, u32[]{:S(2)}) copy-start(f32[1,12800]{1,0:T(1,128)S(1)} %reshape.185.gain_ref) | copy-start | bytes 153604
  4.6 1.9 copy-start
  6.5 10.3 %copy-start.13 = (bf16[200,1024]{1,0:T(8,128)(2,1)S(1)}, bf16[200,1024]{1,0:T(8,128)(2,1)}, u32[]{:S(2)}) copy-start(bf16[200,1024]{1,0:T(8,128)(2,1)} %param.12) | copy-start | bytes 1228804
  10.4 27.1 %all-to-all-start = ((bf16[8,64,1664]{2,1,0:T(8,128)(2,1)}), bf16[8,64,1664]{2,1,0:T(8,128)(2,1)}, u32[]{:S(2)}, u32[]{:S(2)}) async-start(bf16[8,64,1664]{2,1,0:T(8,128)(2,1)} %vision_norm.1), calls=%async_computation | async-start | bytes 3407872 | tf_op jit(solution)/shard_map/all_to_all | solution.py:256
  16.8 20.8 %collective-permute-start.1 = (bf16[200,1024]{1,0:T(8,128)(2,1)S(1)}, bf16[200,1024]{1,0:T(8,128)(2,1)}, u32[]{:S(2)}, u32[]{:S(2)}) collective-permute-start(bf16[200,1024]{1,0:T(8,128)(2,1)S(1)} %copy-done.13), channel_id=1, source_target_pairs={{0,4},{4,8},{8,12},{12,16},{16,20},{20,24},{24,28},{28,0},{1,5},{5... | collective-permute-start | bytes 1228808 | tf_op jit(solution)/shard_map/ppermute | solution.py:179
  18.1 21.4 %collective-permute-start.2 = (bf16[200,1024]{1,0:T(8,128)(2,1)S(1)}, bf16[200,1024]{1,0:T(8,128)(2,1)}, u32[]{:S(2)}, u32[]{:S(2)}) collective-permute-start(bf16[200,1024]{1,0:T(8,128)(2,1)S(1)} %copy-done.13), channel_id=1, source_target_pairs={{0,28},{4,0},{8,4},{12,8},{16,12},{20,16},{24,20},{28,24},{1,29},{... | collective-permute-start | bytes 1228808 | tf_op jit(solution)/shard_map/ppermute | solution.py:180
  37.5 36.3 %collective-permute-start = (bf16[8,64,1664]{2,1,0:T(8,128)(2,1)}, bf16[8,64,1664]{2,1,0:T(8,128)(2,1)}, u32[]{:S(2)}, u32[]{:S(2)}) collective-permute-start(bf16[8,64,1664]{2,1,0:T(8,128)(2,1)} %all-to-all-done.own_ref), channel_id=1, source_target_pairs={{0,1},{1,0},{2,3},{3,2},{4,5},{5,4},{6,7},{7,6},{8,9},{9,8},{10,11... | collective-permute-start | bytes 5111816 | tf_op jit(solution)/shard_map/ppermute | solution.py:257
  37.5 16.3 %collective-permute-start.3 = (bf16[200,1024]{1,0:T(8,128)(2,1)}, bf16[200,1024]{1,0:T(8,128)(2,1)}, u32[]{:S(2)}, u32[]{:S(2)}) collective-permute-start(bf16[200,1024]{1,0:T(8,128)(2,1)} %collective-permute-done.1), channel_id=1, source_target_pairs={{0,4},{4,8},{8,12},{12,16},{16,20},{20,24},{24,28},{28,0},{1,5},{5... | collective-permute-start | bytes 1228808 | tf_op jit(solution)/shard_map/ppermute | solution.py:179
  39.4 14.4 %collective-permute-start.4 = (bf16[200,1024]{1,0:T(8,128)(2,1)}, bf16[200,1024]{1,0:T(8,128)(2,1)}, u32[]{:S(2)}, u32[]{:S(2)}) collective-permute-start(bf16[200,1024]{1,0:T(8,128)(2,1)} %collective-permute-done.2), channel_id=1, source_target_pairs={{0,28},{4,0},{8,4},{12,8},{16,12},{20,16},{24,20},{28,24},{1,29},{... | collective-permute-start | bytes 1228808 | tf_op jit(solution)/shard_map/ppermute | solution.py:180
  53.8 12.7 %collective-permute-start.5 = (bf16[200,1024]{1,0:T(8,128)(2,1)}, bf16[200,1024]{1,0:T(8,128)(2,1)S(1)}, u32[]{:S(2)}, u32[]{:S(2)}) collective-permute-start(bf16[200,1024]{1,0:T(8,128)(2,1)} %collective-permute-done.3), channel_id=1, source_target_pairs={{0,4},{4,8},{8,12},{12,16},{16,20},{20,24},{24,28},{28,0},{1,5},{5... | collective-permute-start | bytes 1228808 | tf_op jit(solution)/shard_map/ppermute | solution.py:179
  53.8 12.8 %collective-permute-start.6 = (bf16[200,1024]{1,0:T(8,128)(2,1)}, bf16[200,1024]{1,0:T(8,128)(2,1)S(1)}, u32[]{:S(2)}, u32[]{:S(2)}) collective-permute-start(bf16[200,1024]{1,0:T(8,128)(2,1)} %collective-permute-done.4), channel_id=1, source_target_pairs={{0,28},{4,0},{8,4},{12,8},{16,12},{20,16},{24,20},{28,24},{1,29},{... | collective-permute-start | bytes 1228808 | tf_op jit(solution)/shard_map/ppermute | solution.py:180
  66.6 7.2 %collective-permute-start.7 = (bf16[96,1024]{1,0:T(8,128)(2,1)S(1)}, bf16[96,1024]{1,0:T(8,128)(2,1)S(1)}, u32[]{:S(2)}, u32[]{:S(2)}) collective-permute-start(bf16[96,1024]{1,0:T(8,128)(2,1)S(1)} %slice.32), channel_id=1, source_target_pairs={{0,4},{4,8},{8,12},{12,16},{16,20},{20,24},{24,28},{28,0},{1,5},{5... | collective-permute-start | bytes 589832 | tf_op jit(solution)/shard_map/ppermute | solution.py:187
  66.7 7.1 %collective-permute-start.8 = (bf16[104,1024]{1,0:T(8,128)(2,1)S(1)}, bf16[104,1024]{1,0:T(8,128)(2,1)S(1)}, u32[]{:S(2)}, u32[]{:S(2)}) collective-permute-start(bf16[104,1024]{1,0:T(8,128)(2,1)S(1)} %slice.33), channel_id=1, source_target_pairs={{0,28},{4,0},{8,4},{12,8},{16,12},{20,16},{24,20},{28,24},{1,29},{... | collective-permute-start | bytes 638984 | tf_op jit(solution)/shard_map/ppermute | solution.py:188
  79.9 1.3 copy-start.2
  81.1 30.0 %copy-start.12 = (f32[1024]{0:T(1024)S(1)}, f32[1024]{0:T(1024)}, u32[]{:S(2)}) copy-start(f32[1024]{0:T(1024)} %param.14) | copy-start | bytes 12292
  81.2 30.0 %all-to-all-start.1 = ((bf16[8,128,1024]{2,1,0:T(8,128)(2,1)}), bf16[8,128,1024]{2,1,0:T(8,128)(2,1)}, u32[]{:S(2)}, u32[]{:S(2)}) async-start(bf16[8,128,1024]{2,1,0:T(8,128)(2,1)} %copy-done.2), calls=%async_computation.1 | async-start | bytes 4194304 | tf_op jit(solution)/shard_map/all_to_all | solution.py:283
  111.1 1.0 copy-start.5
  112.1 0.9 copy-start.11
  115.3 1.2 collective-permute-start.9
  116.6 5.1 %collective-permute-start.10 = (f32[8,128]{1,0:T(8,128)S(1)}, f32[8,128]{1,0:T(8,128)S(1)}, u32[]{:S(2)}, u32[]{:S(2)}) collective-permute-start(f32[8,128]{1,0:T(8,128)S(1)} %add.195), channel_id=1, source_target_pairs={{0,2},{1,3},{2,0},{3,1},{4,6},{5,7},{6,4},{7,5},{8,10},{9,11},{10,... | collective-permute-start | bytes 12296 | tf_op jit(solution)/shard_map/ppermute | solution.py:314
  121.7 1.0 copy-start.6
  122.6 8.7 %copy-start.14 = (s32[4]{0:T(128)S(1)}, s32[4]{0:T(128)}, u32[]{:S(2)}) copy-start(s32[4]{0:T(128)} %constant.140.clone) | copy-start | bytes 52
  123.6 1.3 copy-start.3
  124.9 0.7 copy-start.7
  125.6 30.8 %all-to-all-start.2 = ((bf16[8,128,1024]{2,1,0:T(8,128)(2,1)}), bf16[8,128,1024]{2,1,0:T(8,128)(2,1)}, u32[]{:S(2)}, u32[]{:S(2)}) async-start(bf16[8,128,1024]{2,1,0:T(8,128)(2,1)} %copy-done.3), calls=%async_computation.2 | async-start | bytes 4194304 | tf_op jit(solution)/shard_map/all_to_all | solution.py:323
  160.8 3.7 %collective-permute-start.11 = (bf16[512,1664]{1,0:T(8,128)(2,1)S(1)}, bf16[512,1664]{1,0:T(8,128)(2,1)S(1)}, u32[]{:S(2)}, u32[]{:S(2)}) collective-permute-start(bf16[512,1664]{1,0:T(8,128)(2,1)S(1)} %give.1), channel_id=1, source_target_pairs={{0,1},{1,0},{2,3},{3,2},{4,5},{5,4},{6,7},{7,6},{8,9},{9,8},{10,11... | collective-permute-start | bytes 5111816 | tf_op jit(solution)/shard_map/ppermute | solution.py:358
  167.3 9.9 %collective-permute-start.12 = (bf16[64,1664]{1,0:T(8,128)(2,1)S(1)}, bf16[64,1664]{1,0:T(8,128)(2,1)S(1)}, u32[]{:S(2)}, u32[]{:S(2)}) collective-permute-start(bf16[64,1664]{1,0:T(8,128)(2,1)S(1)} %get-tuple-element.12), channel_id=1, source_target_pairs={{0,2},{1,3},{2,0},{3,1},{4,6},{5,7},{6,4},{7,5},{8,10},{9,11},{10,... | collective-permute-start | bytes 638984 | tf_op jit(solution)/shard_map/ppermute | solution.py:376
  169.6 11.9 %collective-permute-start.13 = (bf16[64,1664]{1,0:T(8,128)(2,1)S(1)}, bf16[64,1664]{1,0:T(8,128)(2,1)S(1)}, u32[]{:S(2)}, u32[]{:S(2)}) collective-permute-start(bf16[64,1664]{1,0:T(8,128)(2,1)S(1)} %get-tuple-element.13), channel_id=1, source_target_pairs={{0,2},{1,3},{2,0},{3,1},{4,6},{5,7},{6,4},{7,5},{8,10},{9,11},{10,... | collective-permute-start | bytes 638984 | tf_op jit(solution)/shard_map/ppermute | solution.py:376
  170.9 15.2 %collective-permute-start.14 = (bf16[64,1664]{1,0:T(8,128)(2,1)S(1)}, bf16[64,1664]{1,0:T(8,128)(2,1)S(1)}, u32[]{:S(2)}, u32[]{:S(2)}) collective-permute-start(bf16[64,1664]{1,0:T(8,128)(2,1)S(1)} %get-tuple-element.14), channel_id=1, source_target_pairs={{0,2},{1,3},{2,0},{3,1},{4,6},{5,7},{6,4},{7,5},{8,10},{9,11},{10,... | collective-permute-start | bytes 638984 | tf_op jit(solution)/shard_map/ppermute | solution.py:376
  173.2 16.7 %collective-permute-start.15 = (bf16[64,1664]{1,0:T(8,128)(2,1)S(1)}, bf16[64,1664]{1,0:T(8,128)(2,1)S(1)}, u32[]{:S(2)}, u32[]{:S(2)}) collective-permute-start(bf16[64,1664]{1,0:T(8,128)(2,1)S(1)} %get-tuple-element.15), channel_id=1, source_target_pairs={{0,2},{1,3},{2,0},{3,1},{4,6},{5,7},{6,4},{7,5},{8,10},{9,11},{10,... | collective-permute-start | bytes 638984 | tf_op jit(solution)/shard_map/ppermute | solution.py:376
  177.2 19.4 %copy-start.8 = (bf16[128,1024]{1,0:T(8,128)(2,1)S(1)}, bf16[128,1024]{1,0:T(8,128)(2,1)}, u32[]{:S(2)}) copy-start(bf16[128,1024]{1,0:T(8,128)(2,1)} %copy-done.7) | copy-start | bytes 786436
  177.2 31.4 %copy-start.1 = (bf16[128,12800]{1,0:T(8,128)(2,1)S(1)}, bf16[128,12800]{1,0:T(8,128)(2,1)}, u32[]{:S(2)}) copy-start(bf16[128,12800]{1,0:T(8,128)(2,1)} %rows_ref.3) | copy-start | bytes 9830404
  190.0 0.9 copy-start.4
  191.0 17.6 %all-to-all-start.3 = ((bf16[8,32,1664]{2,1,0:T(8,128)(2,1)}), bf16[8,32,1664]{2,1,0:T(8,128)(2,1)}, u32[]{:S(2)}, u32[]{:S(2)}) async-start(bf16[8,32,1664]{2,1,0:T(8,128)(2,1)} %copy-done.4), calls=%async_computation.3 | async-start | bytes 1703936 | tf_op jit(solution)/shard_map/all_to_all | solution.py:399
  208.5 0.8 copy-start.10

commit v3 on v2

v3 whole, which is shorter than its diff:
```python
import functools

import jax
import jax.numpy as jnp
from jax import lax
from jax.experimental import pallas as pl
from jax.experimental.pallas import tpu as pltpu
from jax.sharding import Mesh
from jax.sharding import PartitionSpec as P

UNIT = 16
LANES = 128
VISION_EPS = 1e-05
EPSILON = 1e-06
HALF_ROOT = 0.7071067811865476
INV_ROOT_TWO_PI = 0.3989422804014327
BF = jnp.bfloat16
F32 = jnp.float32
VMEM = pl.BlockSpec(memory_space=pltpu.VMEM)
SMEM = pl.BlockSpec(memory_space=pltpu.SMEM)
ANY = pl.BlockSpec(memory_space=pl.ANY)
FREE = pl.CostEstimate(flops=0, transcendentals=0, bytes_accessed=0)
PARAMS = pltpu.CompilerParams(vmem_limit_bytes=40 * 2**20)
WIDE = pltpu.CompilerParams(vmem_limit_bytes=60 * 2**20)
NT = (((1,), (1,)), ((), ()))


def shape(dims, dtype):
    return jax.ShapeDtypeStruct(dims, dtype)


def norm_kernel(chunk, order_ref, live_ref, spot_ref, rows_ref, gain_ref, bias_ref, out_ref):
    step = pl.program_id(0)
    wide = rows_ref[...].astype(F32)
    centered = wide - jnp.mean(wide, axis=1, keepdims=True)
    inv = lax.rsqrt(jnp.mean(centered * centered, axis=1, keepdims=True) + VISION_EPS)
    gain, bias = gain_ref[...].reshape(1, -1), bias_ref[...].reshape(1, -1)
    normed = (centered * inv * gain + bias).astype(BF)
    parts, _, padded = out_ref.shape
    lane = lax.broadcasted_iota(jnp.int32, (UNIT, padded - chunk), 1)
    note = jnp.where(lane == 0, order_ref[step], jnp.where(lane == 1, live_ref[step], spot_ref[step]))
    note = note.astype(F32).astype(BF)
    for k in range(parts):
        out_ref[k] = jnp.concatenate([normed[:, k * chunk : (k + 1) * chunk], note], axis=1)


def forward_kernel(core_ref, own_ref, other_ref, weight_ref, out_ref, note_ref):
    step = pl.program_id(0)
    steps = pl.num_programs(0)

    def work(ref):
        sections, high, depth = ref.shape
        product = jnp.dot(
            ref[...].reshape(sections * high, depth), weight_ref[...], preferred_element_type=F32
        ).astype(BF)
        product = product.reshape(sections, high, product.shape[1])
        for j in range(high // UNIT):
            out_ref[j] = product[:, j * UNIT : (j + 1) * UNIT].reshape(sections * UNIT, -1)
            heads = [ref[s, j * UNIT : (j + 1) * UNIT, depth - LANES :][:1] for s in range(sections)]
            note_ref[j] = jnp.concatenate([head.astype(F32) for head in heads], axis=0)

    @pl.when(step < steps // 2)
    def _():
        work(own_ref)

    @pl.when(step >= steps // 2)
    def _():
        work(other_ref)


def prepare_kernel(text_ref, cot_ref, gain_ref, upstream_ref, stat_ref):
    upstream_ref[...] = cot_ref[...].astype(F32) * gain_ref[...]
    text = text_ref[...].astype(F32)
    square = jnp.sum(text * text, axis=1, keepdims=True)
    square = jnp.broadcast_to(square, (square.shape[0], LANES))
    stat_ref[...] = jnp.transpose(square)[: stat_ref.shape[0]]


def slots_kernel(place_ref, pick_ref, parts_ref, upstream_ref, text_stat_ref, feature_ref, slope_ref, stat_ref):
    del pick_ref
    lane = lax.broadcasted_iota(jnp.int32, (UNIT, LANES), 1)
    stats = []
    for s in range(feature_ref.shape[0] // UNIT):
        rows = slice(s * UNIT, (s + 1) * UNIT)
        projected = parts_ref[0, rows].astype(F32)
        for k in range(1, parts_ref.shape[0]):
            projected = projected + parts_ref[k, rows].astype(F32)
        gate = 0.5 * (1.0 + lax.erf(projected * HALF_ROOT))
        feature = (projected * gate).astype(BF)
        feature_ref[rows] = feature
        slope_ref[rows] = gate + projected * jnp.exp(-0.5 * projected * projected) * INV_ROOT_TWO_PI
        wide = feature.astype(F32)
        at = pl.ds(pl.multiple_of(place_ref[s] * UNIT, UNIT), UNIT)
        square = jnp.sum(wide * wide, axis=1, keepdims=True)
        cross = jnp.sum(upstream_ref[at] * wide, axis=1, keepdims=True)
        stats.append(jnp.where(lane == 0, square, cross))
    stat = jnp.transpose(jnp.concatenate(stats, axis=0))[: stat_ref.shape[0]]
    row = lax.broadcasted_iota(jnp.int32, stat.shape, 0)
    stat_ref[...] = jnp.where(row == 2, text_stat_ref[...], stat)


def row_scales(stat_refs, width):
    stat = sum(ref[...] for ref in stat_refs) / width
    pad = jnp.zeros((LANES - stat.shape[0], LANES), F32)
    return jnp.transpose(jnp.concatenate([stat, pad], axis=0))


def grad_kernel(
    width, place_ref, live_ref, feature_ref, slope_ref, upstream_ref, *refs
):
    stat_refs, grad_ref = refs[:-1], refs[-1]
    stat = row_scales(stat_refs, width)
    for s in range(feature_ref.shape[0] // UNIT):
        rows = slice(s * UNIT, (s + 1) * UNIT)
        inv, cross = lax.rsqrt(stat[rows, 0:1] + EPSILON), stat[rows, 1:2]
        wide = feature_ref[rows].astype(F32)
        at = pl.ds(pl.multiple_of(place_ref[s] * UNIT, UNIT), UNIT)
        hidden_grad = (inv * (upstream_ref[at] - wide * inv * inv * cross)).astype(BF)
        grad = (hidden_grad.astype(F32) * slope_ref[rows]).astype(BF)
        grad = jnp.where(live_ref[s] > 0, grad, jnp.zeros_like(grad))
        for k in range(grad_ref.shape[0]):
            grad_ref[k, rows] = grad


def normed_kernel(
    width, place_ref, live_ref, text_ref, feature_ref, gain_ref, *refs
):
    stat_refs, normed_ref = refs[:-1], refs[-1]
    stat = row_scales(stat_refs, width)
    inv = lax.rsqrt(stat[:, 2:3] + EPSILON)
    normed_ref[...] = (text_ref[...].astype(F32) * inv * gain_ref[...]).astype(BF)
    for s in range(feature_ref.shape[0] // UNIT):
        rows = slice(s * UNIT, (s + 1) * UNIT)
        at = pl.ds(pl.multiple_of(place_ref[s] * UNIT, UNIT), UNIT)

        @pl.when(live_ref[s] > 0)
        def _(rows=rows, at=at):
            inv = lax.rsqrt(stat[rows, 0:1] + EPSILON)
            normed_ref[at] = (feature_ref[rows].astype(F32) * inv * gain_ref[...]).astype(BF)


def give_kernel(first, pick_ref, grads_ref, weight_ref, out_ref):
    count = out_ref.shape[0] // UNIT
    grad = jnp.concatenate([grads_ref[pick_ref[first + m]] for m in range(count)], axis=0)
    out_ref[...] = lax.dot_general(grad, weight_ref[...], NT, preferred_element_type=F32).astype(BF)


def keep_kernel(first, pick_ref, grads_ref, weight_ref, low_ref, high_ref, out_ref):
    targets, share, _ = out_ref.shape
    count = targets * share // UNIT
    start = first + pl.program_id(0) * count
    grad = jnp.concatenate([grads_ref[pick_ref[start + m]] for m in range(count)], axis=0)
    total = lax.dot_general(grad, weight_ref[...], NT, preferred_element_type=F32)
    got = jnp.where(pl.program_id(0) == 0, low_ref[...], high_ref[...])
    total = (total + got.astype(F32)).astype(BF)
    for j in range(targets):
        out_ref[j] = total[j * share : (j + 1) * share]


def final_kernel(chunk, first_ref, parts_ref, rows_ref, gain_ref, out_ref):
    wide = rows_ref[...].astype(F32)
    centered = wide - jnp.mean(wide, axis=1, keepdims=True)
    inv = lax.rsqrt(jnp.mean(centered * centered, axis=1, keepdims=True) + VISION_EPS)
    hat = centered * inv
    grad = jnp.concatenate(
        [
            parts_ref[k][:, :chunk].astype(F32) + parts_ref[k + 1][:, :chunk].astype(F32)
            for k in range(0, parts_ref.shape[0], 2)
        ],
        axis=1,
    )
    weighted = grad * gain_ref[...].reshape(1, -1)
    weighted_mean = jnp.mean(weighted, axis=1, keepdims=True)
    cross = jnp.mean(weighted * hat, axis=1, keepdims=True)
    out_ref[...] = (inv * (weighted - weighted_mean - hat * cross)).astype(BF)


def ring_gather(block, rows, beside):
    groups = lax.axis_size("dp")
    me = lax.axis_index("dp")
    height = block.shape[0]
    up = [(i, (i + 1) % groups) for i in range(groups)]
    down = [(i, (i - 1) % groups) for i in range(groups)]
    out = jnp.zeros((rows, block.shape[1]), block.dtype)

    def put(out, piece, owner):
        return lax.dynamic_update_slice_in_dim(out, piece, owner % groups * height, 0)

    out = put(out, block, me)
    rising = falling = block
    for hop in range(1, (groups - 1) // 2 + 1):
        rising = lax.ppermute(rising, "dp", up)
        falling = lax.ppermute(falling, "dp", down)
        out, rising, falling = lax.optimization_barrier((out, rising, falling))
        if hop == 1:
            rising, falling, beside = lax.optimization_barrier((rising, falling, beside))
        out = put(out, rising, me - hop + groups)
        out = put(out, falling, me + hop)
    if groups % 2 == 0:
        out = put(out, lax.ppermute(rising, "dp", up), me + groups // 2)
    return out, rising, falling, beside


def fill_places(wanted, alive, places):
    taken = jnp.any((wanted[..., :, None] == places) & alive[..., :, None], axis=-2)
    free_rank = jnp.cumsum(~taken, axis=-1) - 1
    dead_rank = jnp.cumsum(~alive, axis=-1) - 1
    fits = (~taken)[..., None, :] & (free_rank[..., None, :] == dead_rank[..., :, None])
    filler = jnp.sum(jnp.where(fits, places, 0), axis=-1)
    return jnp.where(alive, wanted, filler).astype(jnp.int32)


def inverse(place, places):
    return jnp.sum(
        jnp.where(place[..., :, None] == places, places[:, None], 0), axis=-2
    ).astype(jnp.int32)


def shards(
    width, vision_rows, vision_gain, vision_bias, proj_weight, text_rows, text_gain, slot_of_row, out_cotangent
):
    sections = lax.axis_size("section")
    groups = lax.axis_size("dp")
    tensors = 2 * lax.axis_size("y_hi")
    rows, depth = vision_rows.shape
    slots, columns = text_rows.shape
    units = rows // UNIT
    chunk = depth // sections
    padded = -(-(chunk + 3) // LANES) * LANES
    section = lax.axis_index("section")
    core = lax.axis_index("core")
    tensor = lax.axis_index("y_hi") * 2 + core
    places = jnp.arange(units)
    swap_core = [(0, 1), (1, 0)]

    text_gain_row = text_gain.reshape(1, columns)

    unit_slot = slot_of_row.reshape(units, UNIT)[:, 0]
    alive = unit_slot >= 0
    safe = jnp.where(alive, unit_slot, 0)
    order = inverse(fill_places(safe // (slots * groups), alive, places), places)
    half = units // 2
    own = lax.dynamic_slice_in_dim(order, core * half, half)
    chosen = own[:, None] == places
    live = jnp.sum(jnp.where(chosen, alive, 0), axis=1).astype(jnp.int32)
    spot = jnp.sum(jnp.where(chosen, safe // UNIT % (slots // UNIT), 0), axis=1).astype(jnp.int32)
    sent = pl.pallas_call(
        functools.partial(norm_kernel, chunk),
        out_shape=pltpu.HBM((sections, half * UNIT, padded), BF),
        grid_spec=pltpu.PrefetchScalarGridSpec(
            num_scalar_prefetch=3,
            grid=(half,),
            in_specs=[
                pl.BlockSpec((UNIT, depth), lambda i, order, live, spot: (order[i], 0)),
                pl.BlockSpec((depth,), lambda i, order, live, spot: (0,)),
                pl.BlockSpec((depth,), lambda i, order, live, spot: (0,)),
            ],
            out_specs=pl.BlockSpec(
                (sections, UNIT, padded), lambda i, order, live, spot: (0, i, 0)
            ),
        ),
        compiler_params=WIDE,
        cost_estimate=FREE,
        name="vision_norm",
    )(own, live, spot, vision_rows, vision_gain, vision_bias)
    weight, rising, falling, sent = ring_gather(proj_weight, padded, sent)
    from_own = lax.all_to_all(sent, "section", 0, 0, tiled=True)
    from_own, *_ = lax.optimization_barrier((from_own, rising, falling))
    from_other = lax.ppermute(from_own, "core", swap_core)

    pair = 2 * UNIT
    spread = lambda i, core: ((i + core[0] * (half // 2)) % half, 0, 0)
    partial, table = pl.pallas_call(
        forward_kernel,
        out_shape=(
            pltpu.HBM((units, sections * UNIT, columns), BF),
            shape((units, sections, LANES), F32),
        ),
        grid_spec=pltpu.PrefetchScalarGridSpec(
            num_scalar_prefetch=1,
            grid=(half,),
            in_specs=[
                pl.BlockSpec(
                    (sections, pair, padded), lambda i, core: (0, jnp.minimum(i, half // 2 - 1), 0)
                ),
                pl.BlockSpec(
                    (sections, pair, padded), lambda i, core: (0, jnp.maximum(i - half // 2, 0), 0)
                ),
                pl.BlockSpec((padded, columns), lambda i, core: (0, 0)),
            ],
            out_specs=(
                pl.BlockSpec((2, sections * UNIT, columns), spread),
                pl.BlockSpec((2, sections, LANES), spread),
            ),
        ),
        compiler_params=PARAMS,
        cost_estimate=FREE,
        name="forward",
    )(core.reshape(1).astype(jnp.int32), from_own, from_other, weight)
    partial = lax.all_to_all(partial, "section", 0, 0, tiled=True)

    at = LANES - (padded - chunk)
    table = jnp.swapaxes(table[:, :, at : at + 3], 0, 1).astype(jnp.int32)
    here = lax.dynamic_slice_in_dim(table, section, 1, 1)[:, 0]
    has = here[:, 1] > 0
    spots = jnp.arange(sections)
    where = fill_places(here[:, 2], has, spots)
    has = has.astype(jnp.int32)
    place = inverse(table[:, :, 0], places)

    share = units // tensors
    runs = (jnp.arange(2)[::-1] ^ core)[:, None, None]
    runs = (2 * jnp.arange(2)[None, :, None] + runs) * share + jnp.arange(share)
    hit = runs[:, None, :, :, None] == places
    pick = jnp.sum(jnp.where(hit, place[None, :, None, None, :], 0), axis=4)
    pick = (pick * sections + spots[None, :, None, None]).reshape(-1).astype(jnp.int32)
    upstream, text_stat = pl.pallas_call(
        prepare_kernel,
        out_shape=(shape((slots, columns), F32), shape((8, LANES), F32)),
        in_specs=[VMEM] * 3,
        out_specs=(VMEM, VMEM),
        compiler_params=PARAMS,
        cost_estimate=FREE,
        name="prepare",
    )(text_rows, out_cotangent, text_gain_row)
    feature, slope, stat = pl.pallas_call(
        slots_kernel,
        out_shape=(
            shape((slots, columns), BF),
            shape((slots, columns), F32),
            shape((8, LANES), F32),
        ),
        in_specs=[SMEM, ANY, VMEM, VMEM, VMEM],
        out_specs=(VMEM, VMEM, VMEM),
        compiler_params=PARAMS,
        cost_estimate=FREE,
        name="slots",
    )(where, pick, partial, upstream, text_stat)
    stats = [stat] + [
        lax.ppermute(stat, ("y_hi", "core"), [(i, i ^ turn) for i in range(tensors)])
        for turn in range(1, tensors)
    ]
    grads = pl.pallas_call(
        functools.partial(grad_kernel, width),
        out_shape=pltpu.HBM((sections, slots, columns), BF),
        in_specs=[SMEM, SMEM] + [VMEM] * (3 + tensors),
        out_specs=VMEM,
        compiler_params=PARAMS,
        cost_estimate=FREE,
        name="grads",
    )(where, has, feature, slope, upstream, *stats)
    grads = lax.all_to_all(grads, "section", 0, 0, tiled=True)
    grads = grads.reshape(sections * sections, UNIT, columns)
    normed = pl.pallas_call(
        functools.partial(normed_kernel, width),
        out_shape=shape((slots, columns), BF),
        in_specs=[SMEM, SMEM] + [VMEM] * (3 + tensors),
        out_specs=VMEM,
        compiler_params=PARAMS,
        cost_estimate=FREE,
        name="normed",
    )(where, has, text_rows, feature, text_gain_row, *stats)

    targets = sections * 2
    runs_half = sections * units // 4
    full = [
        SMEM,
        pl.BlockSpec((sections * sections, UNIT, columns), lambda *i: (0, 0, 0)),
        pl.BlockSpec((padded, columns), lambda *i: (0, 0)),
    ]
    got = []
    for h in range(2):
        given = pl.pallas_call(
            functools.partial(give_kernel, h * runs_half),
            out_shape=shape((runs_half * UNIT, padded), BF),
            in_specs=[SMEM, VMEM, VMEM],
            out_specs=VMEM,
            compiler_params=PARAMS,
            cost_estimate=FREE,
            name=f"give{h}",
        )(pick, grads, weight)
        got.append(lax.ppermute(given, "core", swap_core))
    total = pl.pallas_call(
        functools.partial(keep_kernel, 2 * runs_half),
        out_shape=pltpu.HBM((targets, share * UNIT, padded), BF),
        grid=(2,),
        in_specs=full + [pl.BlockSpec((runs_half * UNIT, padded), lambda i: (0, 0))] * 2,
        out_specs=pl.BlockSpec((sections, share * UNIT, padded), lambda i: (i, 0, 0)),
        compiler_params=PARAMS,
        cost_estimate=FREE,
        name="keep",
    )(pick, grads, weight, *got)
    back = lax.all_to_all(total, ("section", "y_hi"), 0, 0, tiled=True)
    vision_grad = pl.pallas_call(
        functools.partial(final_kernel, chunk),
        out_shape=shape((share * UNIT, depth), BF),
        grid_spec=pltpu.PrefetchScalarGridSpec(
            num_scalar_prefetch=1,
            grid=(share,),
            in_specs=[
                pl.BlockSpec((targets, UNIT, padded), lambda i, first: (0, i, 0)),
                pl.BlockSpec((UNIT, depth), lambda i, first: (first[0] + i, 0)),
                pl.BlockSpec((depth,), lambda i, first: (0,)),
            ],
            out_specs=pl.BlockSpec((UNIT, depth), lambda i, first: (i, 0)),
        ),
        compiler_params=WIDE,
        cost_estimate=FREE,
        name="vision_back",
    )((tensor * share).reshape(1).astype(jnp.int32), back, vision_rows, vision_gain)
    return normed, vision_grad


def solution(mesh):
    mesh = Mesh(
        mesh.devices.reshape(mesh.shape["section"], mesh.shape["dp"], -1, 2),
        ("section", "dp", "y_hi", "core"),
    )
    tensor = ("y_hi", "core")
    in_specs = (
        P(("section", "dp"), None),
        P(),
        P(),
        P(("section", "dp"), tensor),
        P(("section", "dp"), tensor),
        P(tensor),
        P(("section", "dp")),
        P(("section", "dp"), tensor),
    )
    out_specs = (P(("section", "dp"), tensor), P(("section", "dp", *tensor), None))

    def program(*args):
        body = functools.partial(shards, args[4].shape[1])
        return jax.shard_map(
            body, mesh=mesh, in_specs=in_specs, out_specs=out_specs, check_vma=False
        )(*args)

    return program
```

time: 216 us -> 193 us (0.89)
  waiting for transfers between devices: 109 us -> 77.6 us
  blocking collectives: 0 us -> 31 us
  starting transfers between devices: 51 us -> 35.1 us
  local copies, waits for them, and re-layouts: 21.3 us -> 12.5 us
  Pallas kernels: 27.7 us -> 30.3 us
    all_to_all x0 -> x1, blocking collectives: none -> 31 us  [shards(): grads = lax.all_to_all(grads, 'section', 0, 0, tiled=True)]
    all_to_all x1, waiting for transfers between devices: 15.4 us -> 0.01 us  [shards(): from_own = lax.all_to_all(sent, 'section', 0, 0, tiled=True)]
    all_to_all x2 -> x1, waiting for transfers between devices: 35.4 us -> 24.5 us  [shards(): back = lax.all_to_all(total, ('section', 'y_hi'), 0, 0, tiled=True)]
    ppermute x10 -> x7, waiting for transfers between devices: 23.9 us -> 16.6 us  [the longest x1 9.62 us: ring_gather(): out = put(out, lax.ppermute(rising, 'dp', up), me + groups // 2)]
    ppermute x10 -> x7, starting transfers between devices: 13 us -> 5.8 us  [the longest x3 3.73 us: shards(): lax.ppermute(stat, ('y_hi', 'core'), [(i, i ^ turn) for i in range(tensor...]
    all_to_all x2 -> x1, starting transfers between devices: 11.3 us -> 5.33 us  [shards(): back = lax.all_to_all(total, ('section', 'y_hi'), 0, 0, tiled=True)]
    unnamed x30 -> x23, local copies, waits for them, and re-layouts: 9.8 us -> 4.25 us
    all_to_all x1, waiting for transfers between devices: 19.9 us -> 23.9 us  [shards(): partial = lax.all_to_all(partial, 'section', 0, 0, tiled=True)]
  transfers between devices with their start and end apart: 20 -> 16, of which waited for: 13 -> 10; matrix products, arithmetic and copies ran while one was open for 5% -> 6% of each run, Pallas kernels for 2% -> 4%
where the time goes in v3:
time: 193 us; the launch traced here: 190 us
  waiting for transfers between devices  77.6 us (40%)
  starting transfers between devices  35.1 us (18%)
  blocking collectives  31 us (16%)
  Pallas kernels  30.3 us (16%)
  local copies, waits for them, and re-layouts  12.5 us (6%)
  other arithmetic  3.02 us (2%)
    all_to_all x1, blocking collectives, shards(): grads = lax.all_to_all(grads, 'section', 0, 0, tiled=True)  31 us
    all_to_all x1, waiting for transfers between devices, shards(): back = lax.all_to_all(total, ('section', 'y_hi'), 0, 0, tiled=True)  24.5 us
    all_to_all x1, waiting for transfers between devices, shards(): partial = lax.all_to_all(partial, 'section', 0, 0, tiled=True)  23.9 us
    ppermute x3, waiting for transfers between devices, ring_gather(): rising = lax.ppermute(rising, 'dp', up)  12.7 us
    ppermute x1, waiting for transfers between devices, ring_gather(): out = put(out, lax.ppermute(rising, 'dp', up), me + groups // 2)  9.62 us
    ppermute x3, starting transfers between devices, ring_gather(): falling = lax.ppermute(falling, 'dp', down)  8.69 us
    pallas_call x1, Pallas kernels, shards(): pl.pallas_call(forward_kernel, out_shape=(pltpu.HBM((units, sections * UN...  7.17 us
    dynamic_update_slice x8, local copies, waits for them, and re-layouts, put(): lax.dynamic_update_slice_in_dim(out, piece, owner % groups * height, 0)  6.27 us
  transfers between devices with their start and end apart: 16, of which 10 were waited for; matrix products, arithmetic and copies ran while one was open for 6% of the time, Pallas kernels for 4%

profile of v3, /device:TPU:8, one launch (start us, length us, event | category | flops | bytes accessed | tf_op | source)
XLA Modules:
  0.0 190.5 jit_solution(3824206610653863377)
XLA Ops:
  0.6 2.0 %collective-permute-start = (bf16[200,1024]{1,0:T(8,128)(2,1)}, bf16[200,1024]{1,0:T(8,128)(2,1)}, u32[]{:S(2)}, u32[]{:S(2)}) collective-permute-start(bf16[200,1024]{1,0:T(8,128)(2,1)} %param.11), channel_id=1, source_target_pairs={{0,4},{4,8},{8,12},{12,16},{16,20},{20,24},{24,28},{28,0},{1,5},{5... | collective-permute-start | bytes 1228808 | tf_op jit(solution)/shard_map/ppermute | solution.py:192
  2.6 4.0 %collective-permute-start.1 = (bf16[200,1024]{1,0:T(8,128)(2,1)}, bf16[200,1024]{1,0:T(8,128)(2,1)}, u32[]{:S(2)}, u32[]{:S(2)}) collective-permute-start(bf16[200,1024]{1,0:T(8,128)(2,1)} %param.11), channel_id=1, source_target_pairs={{0,28},{4,0},{8,4},{12,8},{16,12},{20,16},{24,20},{28,24},{1,29},{... | collective-permute-start | bytes 1228808 | tf_op jit(solution)/shard_map/ppermute | solution.py:193
  6.7 0.7 reshape.199
  7.4 0.1 fusion.8
  7.5 0.1 reduce.1
  7.6 0.1 fusion.3
  7.9 0.2 add_reduce_fusion.2
  8.0 0.2 select_reduce_fusion.5
  8.3 0.2 slice_reduce_fusion
  8.7 0.7 select_reduce_fusion.6
  9.4 5.5 %vision_norm.1 = bf16[8,64,1664]{2,1,0:T(8,128)(2,1)} custom-call(s32[4]{0:T(128)} %copy-done.10, s32[4]{0:T(128)} %get-tuple-element.45.live_ref, s32[4]{0:T(128)} %get-tuple-element.44.spot_ref, bf16[128,12800]{1,0:T(8,128)(2,1)} %rows_ref.3, f32[12800]{0:T(1024)} %gain_ref.3, f32[12800]{0:T(1024)} %bias_ref.1), custom_call_target="tpu_custom_call" | custom-call | tf_op jit(solution)/shard_map/vision_norm/pallas_call | solution.py:247
  14.9 0.4 broadcast_in_dim.98
  15.4 1.0 collective-permute-done
  16.4 5.8 %all-to-all-start = ((bf16[8,64,1664]{2,1,0:T(8,128)(2,1)}), bf16[8,64,1664]{2,1,0:T(8,128)(2,1)}, u32[]{:S(2)}, u32[]{:S(2)}) async-start(bf16[8,64,1664]{2,1,0:T(8,128)(2,1)} %vision_norm.1), calls=%async_computation | async-start | bytes 3407872 | tf_op jit(solution)/shard_map/all_to_all | solution.py:267
  22.1 3.2 %collective-permute-start.3 = (bf16[200,1024]{1,0:T(8,128)(2,1)}, bf16[200,1024]{1,0:T(8,128)(2,1)}, u32[]{:S(2)}, u32[]{:S(2)}) collective-permute-start(bf16[200,1024]{1,0:T(8,128)(2,1)} %collective-permute-done.1), channel_id=1, source_target_pairs={{0,28},{4,0},{8,4},{12,8},{16,12},{20,16},{24,20},{28,24},{1,29},{... | collective-permute-start | bytes 1228808 | tf_op jit(solution)/shard_map/ppermute | solution.py:193
  25.3 1.0 constant_dynamic-update-slice_fusion.6
  26.4 1.0 constant_dynamic-update-slice_fusion.5
  27.4 6.3 %collective-permute-done.2 = bf16[200,1024]{1,0:T(8,128)(2,1)} collective-permute-done((bf16[200,1024]{1,0:T(8,128)(2,1)}, bf16[200,1024]{1,0:T(8,128)(2,1)}, u32[]{:S(2)}, u32[]{:S(2)}) %collective-permute-start.2) | collective-permute-done | bytes 409632 | tf_op jit(solution)/shard_map/ppermute | solution.py:192
  33.7 1.8 collective-permute-start.4
  35.6 1.4 collective-permute-start.5
  37.0 1.0 constant_dynamic-update-slice_fusion.4
  38.0 1.0 constant_dynamic-update-slice_fusion.3
  39.0 5.4 %collective-permute-done.4 = bf16[200,1024]{1,0:T(8,128)(2,1)} collective-permute-done((bf16[200,1024]{1,0:T(8,128)(2,1)}, bf16[200,1024]{1,0:T(8,128)(2,1)}, u32[]{:S(2)}, u32[]{:S(2)}) %collective-permute-start.4) | collective-permute-done | bytes 409632 | tf_op jit(solution)/shard_map/ppermute | solution.py:192
  44.5 0.1 rev.3
  44.6 0.9 copy-done.4
  45.6 0.9 copy-done.6
  46.5 0.2 prepare.1
  46.8 1.5 collective-permute-start.7
  48.4 1.0 constant_dynamic-update-slice_fusion.2
  49.4 1.0 constant_dynamic-update-slice_fusion.1
  50.5 9.6 %collective-permute-done.7 = bf16[200,1024]{1,0:T(8,128)(2,1)S(1)} collective-permute-done((bf16[200,1024]{1,0:T(8,128)(2,1)}, bf16[200,1024]{1,0:T(8,128)(2,1)S(1)}, u32[]{:S(2)}, u32[]{:S(2)}) %collective-permute-start.7) | collective-permute-done | bytes 409632 | tf_op jit(solution)/shard_map/ppermute | solution.py:200
  60.1 7.2 %forward.1 = (bf16[8,128,1024]{2,1,0:T(8,128)(2,1)}, f32[8,8,128]{2,1,0:T(8,128)S(1)}) custom-call(s32[1]{0:T(128)} %bitcast.core_ref, bf16[8,64,1664]{2,1,0:T(8,128)(2,1)} %all-to-all-done.own_ref, bf16[8,64,1664]{2,1,0:T(8,128)(2,1)} %collective-permute-done.6.other_ref, bf16[1664,1024]{1,0:T(8,128)(2,1)S(1)} %constant_dynamic-update-slice_fusion.weight_ref), custom_call_target="tpu_custom_call" | custom-call | tf_op jit(solution)/shard_map/forward/pallas_call | solution.py:273
  67.4 0.1 copy.27
  67.5 5.7 %all-to-all-start.1 = ((bf16[8,128,1024]{2,1,0:T(8,128)(2,1)}), bf16[8,128,1024]{2,1,0:T(8,128)(2,1)}, u32[]{:S(2)}, u32[]{:S(2)}) async-start(bf16[8,128,1024]{2,1,0:T(8,128)(2,1)} %get-tuple-element.36), calls=%async_computation.1 | async-start | bytes 4194304 | tf_op jit(solution)/shard_map/all_to_all | solution.py:300
  73.3 0.2 select_reduce_fusion
  73.5 0.1 copy.28
  73.6 0.1 add.203.pick_ref
  74.0 0.1 reduce.6
  74.1 0.1 fusion.5
  74.3 0.1 add_reduce_fusion.1
  74.4 0.1 add_reduce_fusion
  74.5 0.2 select_reduce_fusion.2
  74.7 23.9 %all-to-all-done.1.parts_ref = bf16[8,128,1024]{2,1,0:T(8,128)(2,1)} async-done(((bf16[8,128,1024]{2,1,0:T(8,128)(2,1)}), bf16[8,128,1024]{2,1,0:T(8,128)(2,1)}, u32[]{:S(2)}, u32[]{:S(2)}) %all-to-all-start.1) | async-done | bytes 2097184 | tf_op jit(solution)/shard_map/all_to_all | solution.py:300
  98.6 1.0 copy-done.1
  99.7 2.2 %slots.1 = (bf16[128,1024]{1,0:T(8,128)(2,1)S(1)}, f32[128,1024]{1,0:T(8,128)S(1)}, f32[8,128]{1,0:T(8,128)S(1)}) custom-call(s32[8]{0:T(128)S(1)} %fusion.7.place_ref, s32[64]{0:T(128)S(1)} %add.203.pick_ref, bf16[8,128,1024]{2,1,0:T(8,128)(2,1)} %all-to-all-done.1.parts_ref, f32[128,1024]{1,0:T(8,128)S(1)} %copy-done.1, ...), custom_call_target="tpu_custom_call" | custom-call | tf_op jit(solution)/shard_map/slots/pallas_call | solution.py:326
  101.9 1.6 collective-permute-start.10
  103.5 0.9 collective-permute-start.8
  104.4 1.2 collective-permute-start.9
  105.6 0.9 collective-permute-done.10.refs_3_
  106.5 3.0 %collective-permute-done.9.refs_2_ = f32[8,128]{1,0:T(8,128)S(1)} collective-permute-done((f32[8,128]{1,0:T(8,128)S(1)}, f32[8,128]{1,0:T(8,128)S(1)}, u32[]{:S(2)}, u32[]{:S(2)}) %collective-permute-start.9) | collective-permute-done | bytes 4128 | tf_op jit(solution)/shard_map/ppermute | solution.py:340
  109.5 2.3 %grads.1 = bf16[8,128,1024]{2,1,0:T(8,128)(2,1)} custom-call(s32[8]{0:T(128)S(1)} %fusion.7.place_ref, s32[8]{0:T(128)S(1)} %convert_element_type.60.live_ref, bf16[128,1024]{1,0:T(8,128)(2,1)S(1)} %get-tuple-element.39.feature_ref, f32[128,1024]{1,0:T(8,128)S(1)} %get-tuple-element.41.slope_ref, f32[128,1024]{1,0:T(8,128)S(1)} %copy-done.1, ...), custom_call_target="tpu_custom_call" | custom-call | tf_op jit(solution)/shard_map/grads/pallas_call | solution.py:343
  111.8 31.0 %all_to_all.20 = bf16[8,128,1024]{2,1,0:T(8,128)(2,1)S(1)} all-to-all(bf16[8,128,1024]{2,1,0:T(8,128)(2,1)} %grads.1), channel_id=1, replica_groups=mesh['section'=8,'dp'=8,'y_hi'=2,'core'=2] {'section'}, dimensions={0} | all-to-all | bytes 4194304 | tf_op jit(solution)/shard_map/all_to_all | solution.py:352
  142.8 1.7 give1.1
  144.5 1.7 give0.1
  146.2 0.1 collective-permute-start.12
  146.3 0.5 collective-permute-start.11
  146.8 1.9 collective-permute-done.12.high_ref
  148.7 1.2 collective-permute-done.11.low_ref
  149.9 3.8 %keep.1 = bf16[16,32,1664]{2,1,0:T(8,128)(2,1)} custom-call(s32[64]{0:T(128)S(1)} %add.203.pick_ref, bf16[64,16,1024]{2,1,0:T(8,128)(2,1)S(1)} %bitcast.20, bf16[1664,1024]{1,0:T(8,128)(2,1)S(1)} %constant_dynamic-update-slice_fusion.weight_ref, bf16[256,1664]{1,0:T(8,128)(2,1)S(1)} %collective-permute-done.11.low_ref, ...), custom_call_target="tpu_custom_call" | custom-call | tf_op jit(solution)/shard_map/keep/pallas_call | solution.py:383
  153.7 5.3 %all-to-all-start.3 = ((bf16[16,32,1664]{2,1,0:T(8,128)(2,1)}), bf16[16,32,1664]{2,1,0:T(8,128)(2,1)S(1)}, u32[]{:S(2)}, u32[]{:S(2)}) async-start(bf16[16,32,1664]{2,1,0:T(8,128)(2,1)} %keep.1), calls=%async_computation.3 | async-start | bytes 3407872 | tf_op jit(solution)/shard_map/all_to_all | solution.py:393
  159.1 1.9 %normed.1 = bf16[128,1024]{1,0:T(8,128)(2,1)} custom-call(s32[8]{0:T(128)S(1)} %fusion.7.place_ref, s32[8]{0:T(128)S(1)} %convert_element_type.60.live_ref, bf16[128,1024]{1,0:T(8,128)(2,1)S(1)} %copy-done.5, bf16[128,1024]{1,0:T(8,128)(2,1)S(1)} %copy-done.3, f32[1,1024]{1,0:T(1,128)S(1)} %bitcast.22, f32[8,128]{1,0:T(8,128)S(1)} %get-tuple-element.40.refs_0_, ...), custom_call_target="tpu_custom_call" | custom-call | tf_op jit(solution)/shard_map/normed/pallas_call | solution.py:354
  161.0 24.5 %all-to-all-done.3.parts_ref = bf16[16,32,1664]{2,1,0:T(8,128)(2,1)S(1)} async-done(((bf16[16,32,1664]{2,1,0:T(8,128)(2,1)}), bf16[16,32,1664]{2,1,0:T(8,128)(2,1)S(1)}, u32[]{:S(2)}, u32[]{:S(2)}) %all-to-all-start.3) | async-done | bytes 1703968 | tf_op jit(solution)/shard_map/all_to_all | solution.py:393
  185.5 1.2 copy-done.8
  186.7 3.8 %vision_back.1 = bf16[32,12800]{1,0:T(8,128)(2,1)} custom-call(s32[1]{0:T(128)} %bitcast.9.first_ref, bf16[16,32,1664]{2,1,0:T(8,128)(2,1)} %copy-done.8, bf16[128,12800]{1,0:T(8,128)(2,1)} %rows_ref.3, f32[12800]{0:T(1024)} %gain_ref.3), custom_call_target="tpu_custom_call" | custom-call | tf_op jit(solution)/shard_map/vision_back/pallas_call | solution.py:394
  (57 shorter events, 1.3 us)
Async XLA Ops:
  0.6 15.7 %collective-permute-start = (bf16[200,1024]{1,0:T(8,128)(2,1)}, bf16[200,1024]{1,0:T(8,128)(2,1)}, u32[]{:S(2)}, u32[]{:S(2)}) collective-permute-start(bf16[200,1024]{1,0:T(8,128)(2,1)} %param.11), channel_id=1, source_target_pairs={{0,4},{4,8},{8,12},{12,16},{16,20},{20,24},{24,28},{28,0},{1,5},{5... | collective-permute-start | bytes 1228808 | tf_op jit(solution)/shard_map/ppermute | solution.py:192
  2.6 13.7 %collective-permute-start.1 = (bf16[200,1024]{1,0:T(8,128)(2,1)}, bf16[200,1024]{1,0:T(8,128)(2,1)}, u32[]{:S(2)}, u32[]{:S(2)}) collective-permute-start(bf16[200,1024]{1,0:T(8,128)(2,1)} %param.11), channel_id=1, source_target_pairs={{0,28},{4,0},{8,4},{12,8},{16,12},{20,16},{24,20},{28,24},{1,29},{... | collective-permute-start | bytes 1228808 | tf_op jit(solution)/shard_map/ppermute | solution.py:193
  8.7 0.7 copy-start.10
  9.4 6.0 %copy-start.9 = (bf16[200,1024]{1,0:T(8,128)(2,1)S(1)}, bf16[200,1024]{1,0:T(8,128)(2,1)}, u32[]{:S(2)}) copy-start(bf16[200,1024]{1,0:T(8,128)(2,1)} %param.11) | copy-start | bytes 1228804
  15.4 29.2 %copy-start.7 = (f32[1024]{0:T(1024)S(1)}, f32[1024]{0:T(1024)}, u32[]{:S(2)}) copy-start(f32[1024]{0:T(1024)} %param.13) | copy-start | bytes 12292
  16.4 28.1 %all-to-all-start = ((bf16[8,64,1664]{2,1,0:T(8,128)(2,1)}), bf16[8,64,1664]{2,1,0:T(8,128)(2,1)}, u32[]{:S(2)}, u32[]{:S(2)}) async-start(bf16[8,64,1664]{2,1,0:T(8,128)(2,1)} %vision_norm.1), calls=%async_computation | async-start | bytes 3407872 | tf_op jit(solution)/shard_map/all_to_all | solution.py:267
  22.1 11.6 %collective-permute-start.2 = (bf16[200,1024]{1,0:T(8,128)(2,1)}, bf16[200,1024]{1,0:T(8,128)(2,1)}, u32[]{:S(2)}, u32[]{:S(2)}) collective-permute-start(bf16[200,1024]{1,0:T(8,128)(2,1)} %collective-permute-done), channel_id=1, source_target_pairs={{0,4},{4,8},{8,12},{12,16},{16,20},{20,24},{24,28},{28,0},{1,5},{5... | collective-permute-start | bytes 1228808 | tf_op jit(solution)/shard_map/ppermute | solution.py:192
  22.1 11.6 %collective-permute-start.3 = (bf16[200,1024]{1,0:T(8,128)(2,1)}, bf16[200,1024]{1,0:T(8,128)(2,1)}, u32[]{:S(2)}, u32[]{:S(2)}) collective-permute-start(bf16[200,1024]{1,0:T(8,128)(2,1)} %collective-permute-done.1), channel_id=1, source_target_pairs={{0,28},{4,0},{8,4},{12,8},{16,12},{20,16},{24,20},{28,24},{1,29},{... | collective-permute-start | bytes 1228808 | tf_op jit(solution)/shard_map/ppermute | solution.py:193
  33.7 10.7 %collective-permute-start.4 = (bf16[200,1024]{1,0:T(8,128)(2,1)}, bf16[200,1024]{1,0:T(8,128)(2,1)}, u32[]{:S(2)}, u32[]{:S(2)}) collective-permute-start(bf16[200,1024]{1,0:T(8,128)(2,1)} %collective-permute-done.2), channel_id=1, source_target_pairs={{0,4},{4,8},{8,12},{12,16},{16,20},{20,24},{24,28},{28,0},{1,5},{5... | collective-permute-start | bytes 1228808 | tf_op jit(solution)/shard_map/ppermute | solution.py:192
  35.6 8.9 %collective-permute-start.5 = (bf16[200,1024]{1,0:T(8,128)(2,1)}, bf16[200,1024]{1,0:T(8,128)(2,1)}, u32[]{:S(2)}, u32[]{:S(2)}) collective-permute-start(bf16[200,1024]{1,0:T(8,128)(2,1)} %collective-permute-done.3), channel_id=1, source_target_pairs={{0,28},{4,0},{8,4},{12,8},{16,12},{20,16},{24,20},{28,24},{1,29},{... | collective-permute-start | bytes 1228808 | tf_op jit(solution)/shard_map/ppermute | solution.py:193
  44.4 15.7 %collective-permute-start.6 = (bf16[8,64,1664]{2,1,0:T(8,128)(2,1)}, bf16[8,64,1664]{2,1,0:T(8,128)(2,1)}, u32[]{:S(2)}, u32[]{:S(2)}) collective-permute-start(bf16[8,64,1664]{2,1,0:T(8,128)(2,1)} %all-to-all-done.own_ref), channel_id=1, source_target_pairs={{0,1},{1,0},{2,3},{3,2},{4,5},{5,4},{6,7},{7,6},{8,9},{9,8},{10,11... | collective-permute-start | bytes 5111816 | tf_op jit(solution)/shard_map/ppermute | solution.py:269
  44.6 1.0 copy-start.4
  45.6 0.9 copy-start.6
  46.7 13.4 %copy-start = (f32[128,1024]{1,0:T(8,128)}, f32[128,1024]{1,0:T(8,128)S(1)}, u32[]{:S(2)}) copy-start(f32[128,1024]{1,0:T(8,128)S(1)} %get-tuple-element.37.upstream_ref) | copy-start | bytes 1572868
  46.8 13.2 %collective-permute-start.7 = (bf16[200,1024]{1,0:T(8,128)(2,1)}, bf16[200,1024]{1,0:T(8,128)(2,1)S(1)}, u32[]{:S(2)}, u32[]{:S(2)}) collective-permute-start(bf16[200,1024]{1,0:T(8,128)(2,1)} %collective-permute-done.4), channel_id=1, source_target_pairs={{0,4},{4,8},{8,12},{12,16},{16,20},{20,24},{24,28},{28,0},{1,5},{5... | collective-permute-start | bytes 1228808 | tf_op jit(solution)/shard_map/ppermute | solution.py:200
  67.5 31.1 %all-to-all-start.1 = ((bf16[8,128,1024]{2,1,0:T(8,128)(2,1)}), bf16[8,128,1024]{2,1,0:T(8,128)(2,1)}, u32[]{:S(2)}, u32[]{:S(2)}) async-start(bf16[8,128,1024]{2,1,0:T(8,128)(2,1)} %get-tuple-element.36), calls=%async_computation.1 | async-start | bytes 4194304 | tf_op jit(solution)/shard_map/all_to_all | solution.py:300
  98.6 1.0 copy-start.1
  101.9 40.9 %copy-start.2 = (bf16[128,1024]{1,0:T(8,128)(2,1)}, bf16[128,1024]{1,0:T(8,128)(2,1)S(1)}, u32[]{:S(2)}) copy-start(bf16[128,1024]{1,0:T(8,128)(2,1)S(1)} %get-tuple-element.39.feature_ref) | copy-start | bytes 786436
  101.9 4.6 %collective-permute-start.10 = (f32[8,128]{1,0:T(8,128)S(1)}, f32[8,128]{1,0:T(8,128)S(1)}, u32[]{:S(2)}, u32[]{:S(2)}) collective-permute-start(f32[8,128]{1,0:T(8,128)S(1)} %get-tuple-element.40.refs_0_), channel_id=1, source_target_pairs={{0,3},{1,2},{2,1},{3,0},{4,7},{5,6},{6,5},{7,4},{8,11},{9,10},{10,... | collective-permute-start | bytes 12296 | tf_op jit(solution)/shard_map/ppermute | solution.py:340
  103.5 3.0 %collective-permute-start.8 = (f32[8,128]{1,0:T(8,128)S(1)}, f32[8,128]{1,0:T(8,128)S(1)}, u32[]{:S(2)}, u32[]{:S(2)}) collective-permute-start(f32[8,128]{1,0:T(8,128)S(1)} %get-tuple-element.40.refs_0_), channel_id=1, source_target_pairs={{0,1},{1,0},{2,3},{3,2},{4,5},{5,4},{6,7},{7,6},{8,9},{9,8},{10,11... | collective-permute-start | bytes 12296 | tf_op jit(solution)/shard_map/ppermute | solution.py:340
  104.4 5.1 %collective-permute-start.9 = (f32[8,128]{1,0:T(8,128)S(1)}, f32[8,128]{1,0:T(8,128)S(1)}, u32[]{:S(2)}, u32[]{:S(2)}) collective-permute-start(f32[8,128]{1,0:T(8,128)S(1)} %get-tuple-element.40.refs_0_), channel_id=1, source_target_pairs={{0,2},{1,3},{2,0},{3,1},{4,6},{5,7},{6,4},{7,5},{8,10},{9,11},{10,... | collective-permute-start | bytes 12296 | tf_op jit(solution)/shard_map/ppermute | solution.py:340
  146.2 2.5 %collective-permute-start.12 = (bf16[256,1664]{1,0:T(8,128)(2,1)S(1)}, bf16[256,1664]{1,0:T(8,128)(2,1)S(1)}, u32[]{:S(2)}, u32[]{:S(2)}) collective-permute-start(bf16[256,1664]{1,0:T(8,128)(2,1)S(1)} %give1.1), channel_id=1, source_target_pairs={{0,1},{1,0},{2,3},{3,2},{4,5},{5,4},{6,7},{7,6},{8,9},{9,8},{10,11... | collective-permute-start | bytes 2555912 | tf_op jit(solution)/shard_map/ppermute | solution.py:382
  146.3 3.6 %collective-permute-start.11 = (bf16[256,1664]{1,0:T(8,128)(2,1)S(1)}, bf16[256,1664]{1,0:T(8,128)(2,1)S(1)}, u32[]{:S(2)}, u32[]{:S(2)}) collective-permute-start(bf16[256,1664]{1,0:T(8,128)(2,1)S(1)} %give0.1), channel_id=1, source_target_pairs={{0,1},{1,0},{2,3},{3,2},{4,5},{5,4},{6,7},{7,6},{8,9},{9,8},{10,11... | collective-permute-start | bytes 2555912 | tf_op jit(solution)/shard_map/ppermute | solution.py:382
  153.7 5.3 %copy-start.3 = (bf16[128,1024]{1,0:T(8,128)(2,1)S(1)}, bf16[128,1024]{1,0:T(8,128)(2,1)}, u32[]{:S(2)}) copy-start(bf16[128,1024]{1,0:T(8,128)(2,1)} %copy-done.2) | copy-start | bytes 786436
  153.7 5.3 %copy-start.5 = (bf16[128,1024]{1,0:T(8,128)(2,1)S(1)}, bf16[128,1024]{1,0:T(8,128)(2,1)}, u32[]{:S(2)}) copy-start(bf16[128,1024]{1,0:T(8,128)(2,1)} %text_ref.3) | copy-start | bytes 786436
  153.7 31.7 %all-to-all-start.3 = ((bf16[16,32,1664]{2,1,0:T(8,128)(2,1)}), bf16[16,32,1664]{2,1,0:T(8,128)(2,1)S(1)}, u32[]{:S(2)}, u32[]{:S(2)}) async-start(bf16[16,32,1664]{2,1,0:T(8,128)(2,1)} %keep.1), calls=%async_computation.3 | async-start | bytes 3407872 | tf_op jit(solution)/shard_map/all_to_all | solution.py:393
  185.5 1.2 copy-start.8

commit v4 on v3

--- a/solution.py
+++ b/solution.py
@@ -41,22 +41,27 @@
     note = jnp.where(lane == 0, order_ref[step], jnp.where(lane == 1, live_ref[step], spot_ref[step]))
     note = note.astype(F32).astype(BF)
     for k in range(parts):
-        out_ref[k] = jnp.concatenate([normed[:, k * chunk : (k + 1) * chunk], note], axis=1)
-
-
-def forward_kernel(core_ref, own_ref, other_ref, weight_ref, out_ref, note_ref):
+        at = (k % 2 * (parts // 2) + k // 2) * chunk
+        out_ref[k] = jnp.concatenate([normed[:, at : at + chunk], note], axis=1)
+
+
+def forward_kernel(core_ref, tile_ref, own_ref, other_ref, weight_ref, out_ref, window_ref, note_ref):
     step = pl.program_id(0)
     steps = pl.num_programs(0)
 
     def work(ref):
         sections, high, depth = ref.shape
+        at = pl.ds(pl.multiple_of(tile_ref[0] * LANES, LANES), window_ref.shape[2])
         product = jnp.dot(
             ref[...].reshape(sections * high, depth), weight_ref[...], preferred_element_type=F32
-        ).astype(BF)
+        )
         product = product.reshape(sections, high, product.shape[1])
         for j in range(high // UNIT):
-            out_ref[j] = product[:, j * UNIT : (j + 1) * UNIT].reshape(sections * UNIT, -1)
-            heads = [ref[s, j * UNIT : (j + 1) * UNIT, depth - LANES :][:1] for s in range(sections)]
+            rows = product[:, j * UNIT : (j + 1) * UNIT].reshape(sections * UNIT, -1)
+            out_ref[j] = rows
+            run = slice(j * UNIT, (j + 1) * UNIT)
+            window_ref[j] = ref[:, run, at].reshape(sections * UNIT, -1)
+            heads = [ref[s, run, depth - LANES :][:1] for s in range(sections)]
             note_ref[j] = jnp.concatenate([head.astype(F32) for head in heads], axis=0)
 
     @pl.when(step < steps // 2)
@@ -66,6 +71,12 @@
     @pl.when(step >= steps // 2)
     def _():
         work(other_ref)
+
+
+def tail_kernel(window_ref, weight_ref, main_ref, out_ref):
+    for target in range(out_ref.shape[0]):
+        product = jnp.dot(window_ref[target], weight_ref[...], preferred_element_type=F32)
+        out_ref[target] = (main_ref[target] + product).astype(BF)
 
 
 def prepare_kernel(text_ref, cot_ref, gain_ref, upstream_ref, stat_ref):
@@ -76,8 +87,10 @@
     stat_ref[...] = jnp.transpose(square)[: stat_ref.shape[0]]
 
 
-def slots_kernel(place_ref, pick_ref, parts_ref, upstream_ref, text_stat_ref, feature_ref, slope_ref, stat_ref):
-    del pick_ref
+def slots_kernel(
+    place_ref, pick_ref, hat_ref, parts_ref, upstream_ref, text_stat_ref, feature_ref, slope_ref, stat_ref
+):
+    del pick_ref, hat_ref
     lane = lax.broadcasted_iota(jnp.int32, (UNIT, LANES), 1)
     stats = []
     for s in range(feature_ref.shape[0] // UNIT):
@@ -118,8 +131,7 @@
         hidden_grad = (inv * (upstream_ref[at] - wide * inv * inv * cross)).astype(BF)
         grad = (hidden_grad.astype(F32) * slope_ref[rows]).astype(BF)
         grad = jnp.where(live_ref[s] > 0, grad, jnp.zeros_like(grad))
-        for k in range(grad_ref.shape[0]):
-            grad_ref[k, rows] = grad
+        grad_ref[s] = grad
 
 
 def normed_kernel(
@@ -139,40 +151,53 @@
             normed_ref[at] = (feature_ref[rows].astype(F32) * inv * gain_ref[...]).astype(BF)
 
 
-def give_kernel(first, pick_ref, grads_ref, weight_ref, out_ref):
-    count = out_ref.shape[0] // UNIT
-    grad = jnp.concatenate([grads_ref[pick_ref[first + m]] for m in range(count)], axis=0)
-    out_ref[...] = lax.dot_general(grad, weight_ref[...], NT, preferred_element_type=F32).astype(BF)
-
-
-def keep_kernel(first, pick_ref, grads_ref, weight_ref, low_ref, high_ref, out_ref):
+def arrange_kernel(pick_ref, *refs):
+    blocks, out_ref = refs[:-1], refs[-1]
+    for b, ref in enumerate(blocks):
+        for s in range(ref.shape[0]):
+            out_ref[pick_ref[b * ref.shape[0] + s]] = ref[s]
+
+
+def back_kernel(grads_ref, weight_ref, out_ref):
+    grad = grads_ref[...].reshape(out_ref.shape[0], -1)
+    product = lax.dot_general(grad, weight_ref[...], NT, preferred_element_type=F32)
+    out_ref[...] = product.astype(out_ref.dtype)
+
+
+def join_kernel(own_ref, low_ref, high_ref, out_ref):
+    got = jnp.where(pl.program_id(0) == 0, low_ref[...], high_ref[...])
+    total = (own_ref[...] + got.astype(F32)).astype(BF)
     targets, share, _ = out_ref.shape
-    count = targets * share // UNIT
-    start = first + pl.program_id(0) * count
-    grad = jnp.concatenate([grads_ref[pick_ref[start + m]] for m in range(count)], axis=0)
-    total = lax.dot_general(grad, weight_ref[...], NT, preferred_element_type=F32)
-    got = jnp.where(pl.program_id(0) == 0, low_ref[...], high_ref[...])
-    total = (total + got.astype(F32)).astype(BF)
     for j in range(targets):
         out_ref[j] = total[j * share : (j + 1) * share]
 
 
-def final_kernel(chunk, first_ref, parts_ref, rows_ref, gain_ref, out_ref):
+def hat_kernel(first_ref, table_ref, rows_ref, hat_ref, inv_ref):
+    del table_ref
     wide = rows_ref[...].astype(F32)
     centered = wide - jnp.mean(wide, axis=1, keepdims=True)
     inv = lax.rsqrt(jnp.mean(centered * centered, axis=1, keepdims=True) + VISION_EPS)
-    hat = centered * inv
+    hat_ref[...] = centered * inv
+    inv_ref[...] = jnp.broadcast_to(inv, inv_ref.shape)
+
+
+def final_kernel(chunk, order, parts_ref, hat_ref, inv_ref, gain_ref, out_ref):
     grad = jnp.concatenate(
         [
-            parts_ref[k][:, :chunk].astype(F32) + parts_ref[k + 1][:, :chunk].astype(F32)
-            for k in range(0, parts_ref.shape[0], 2)
+            parts_ref[a][:, :chunk].astype(F32) + parts_ref[b][:, :chunk].astype(F32)
+            for a, b in order
         ],
         axis=1,
     )
+    hat, inv = hat_ref[...], inv_ref[:, 0:1]
     weighted = grad * gain_ref[...].reshape(1, -1)
     weighted_mean = jnp.mean(weighted, axis=1, keepdims=True)
     cross = jnp.mean(weighted * hat, axis=1, keepdims=True)
     out_ref[...] = (inv * (weighted - weighted_mean - hat * cross)).astype(BF)
+
+
+def after_kernel(array_ref, before_ref, out_ref):
+    del array_ref, before_ref, out_ref
 
 
 def ring_gather(block, rows, beside):
@@ -187,18 +212,19 @@
         return lax.dynamic_update_slice_in_dim(out, piece, owner % groups * height, 0)
 
     out = put(out, block, me)
-    rising = falling = block
+    rising = falling = rising_once = block
     for hop in range(1, (groups - 1) // 2 + 1):
         rising = lax.ppermute(rising, "dp", up)
         falling = lax.ppermute(falling, "dp", down)
         out, rising, falling = lax.optimization_barrier((out, rising, falling))
         if hop == 1:
             rising, falling, beside = lax.optimization_barrier((rising, falling, beside))
+            rising_once = rising
         out = put(out, rising, me - hop + groups)
         out = put(out, falling, me + hop)
-    if groups % 2 == 0:
-        out = put(out, lax.ppermute(rising, "dp", up), me + groups // 2)
-    return out, rising, falling, beside
+    last = lax.ppermute(rising, "dp", up)
+    owner = (me + groups // 2) % groups
+    return out, last, owner * height, rising, falling, rising_once, beside
 
 
 def fill_places(wanted, alive, places):
@@ -219,7 +245,9 @@
 def shards(
     width, vision_rows, vision_gain, vision_bias, proj_weight, text_rows, text_gain, slot_of_row, out_cotangent
 ):
-    sections = lax.axis_size("section")
+    along = lax.axis_size("x")
+    sections = 2 * along
+    along_first = ("x", "y_lo")
     groups = lax.axis_size("dp")
     tensors = 2 * lax.axis_size("y_hi")
     rows, depth = vision_rows.shape
@@ -227,7 +255,8 @@
     units = rows // UNIT
     chunk = depth // sections
     padded = -(-(chunk + 3) // LANES) * LANES
-    section = lax.axis_index("section")
+    y_lo = lax.axis_index("y_lo")
+    section = lax.axis_index("x") * 2 + y_lo
     core = lax.axis_index("core")
     tensor = lax.axis_index("y_hi") * 2 + core
     places = jnp.arange(units)
@@ -238,7 +267,9 @@
     unit_slot = slot_of_row.reshape(units, UNIT)[:, 0]
     alive = unit_slot >= 0
     safe = jnp.where(alive, unit_slot, 0)
-    order = inverse(fill_places(safe // (slots * groups), alive, places), places)
+    target = safe // (slots * groups)
+    target = target % along * 2 + target // along
+    order = inverse(fill_places(target, alive, places), places)
     half = units // 2
     own = lax.dynamic_slice_in_dim(order, core * half, half)
     chosen = own[:, None] == places
@@ -263,41 +294,65 @@
         cost_estimate=FREE,
         name="vision_norm",
     )(own, live, spot, vision_rows, vision_gain, vision_bias)
-    weight, rising, falling, sent = ring_gather(proj_weight, padded, sent)
-    from_own = lax.all_to_all(sent, "section", 0, 0, tiled=True)
+    early_weight, last, last_row, rising, falling, rising_once, sent = ring_gather(proj_weight, padded, sent)
+    sent = pl.pallas_call(
+        after_kernel,
+        out_shape=pltpu.HBM(sent.shape, sent.dtype),
+        in_specs=[ANY, ANY],
+        out_specs=ANY,
+        input_output_aliases={0: 0},
+        cost_estimate=FREE,
+        name="after",
+    )(sent, rising_once)
+    from_own = lax.all_to_all(sent, along_first, 0, 0, tiled=True)
     from_own, *_ = lax.optimization_barrier((from_own, rising, falling))
     from_other = lax.ppermute(from_own, "core", swap_core)
 
     pair = 2 * UNIT
-    spread = lambda i, core: ((i + core[0] * (half // 2)) % half, 0, 0)
-    partial, table = pl.pallas_call(
+    spread = lambda i, *_: ((i + _[0][0] * (half // 2)) % half, 0, 0)
+    sides = [
+        pl.BlockSpec((sections, pair, padded), lambda i, *_: (0, jnp.minimum(i, half // 2 - 1), 0)),
+        pl.BlockSpec((sections, pair, padded), lambda i, *_: (0, jnp.maximum(i - half // 2, 0), 0)),
+    ]
+    core_index = core.reshape(1).astype(jnp.int32)
+    height = last.shape[0]
+    window = -(-(height + LANES - 8) // LANES) * LANES
+    tile = jnp.minimum(last_row // LANES, (padded - window) // LANES).astype(jnp.int32)
+    main, x_window, table = pl.pallas_call(
         forward_kernel,
         out_shape=(
-            pltpu.HBM((units, sections * UNIT, columns), BF),
+            shape((units, sections * UNIT, columns), F32),
+            shape((units, sections * UNIT, window), BF),
             shape((units, sections, LANES), F32),
         ),
         grid_spec=pltpu.PrefetchScalarGridSpec(
-            num_scalar_prefetch=1,
+            num_scalar_prefetch=2,
             grid=(half,),
-            in_specs=[
-                pl.BlockSpec(
-                    (sections, pair, padded), lambda i, core: (0, jnp.minimum(i, half // 2 - 1), 0)
-                ),
-                pl.BlockSpec(
-                    (sections, pair, padded), lambda i, core: (0, jnp.maximum(i - half // 2, 0), 0)
-                ),
-                pl.BlockSpec((padded, columns), lambda i, core: (0, 0)),
-            ],
+            in_specs=sides + [pl.BlockSpec((padded, columns), lambda i, *_: (0, 0))],
             out_specs=(
                 pl.BlockSpec((2, sections * UNIT, columns), spread),
+                pl.BlockSpec((2, sections * UNIT, window), spread),
                 pl.BlockSpec((2, sections, LANES), spread),
             ),
         ),
         compiler_params=PARAMS,
         cost_estimate=FREE,
         name="forward",
-    )(core.reshape(1).astype(jnp.int32), from_own, from_other, weight)
-    partial = lax.all_to_all(partial, "section", 0, 0, tiled=True)
+    )(core_index, tile.reshape(1), from_own, from_other, early_weight)
+    last_window = lax.dynamic_update_slice_in_dim(
+        jnp.zeros((window, columns), BF), last, last_row - tile * LANES, 0
+    )
+    partial = pl.pallas_call(
+        tail_kernel,
+        out_shape=pltpu.HBM((units, sections * UNIT, columns), BF),
+        in_specs=[VMEM, VMEM, VMEM],
+        out_specs=VMEM,
+        compiler_params=PARAMS,
+        cost_estimate=FREE,
+        name="tail",
+    )(x_window, last_window, main)
+    partial = lax.all_to_all(partial, along_first, 0, 0, tiled=True)
+    weight = lax.dynamic_update_slice_in_dim(early_weight, last, last_row, 0)
 
     at = LANES - (padded - chunk)
     table = jnp.swapaxes(table[:, :, at : at + 3], 0, 1).astype(jnp.int32)
@@ -306,14 +361,33 @@
     spots = jnp.arange(sections)
     where = fill_places(here[:, 2], has, spots)
     has = has.astype(jnp.int32)
-    place = inverse(table[:, :, 0], places)
 
     share = units // tensors
-    runs = (jnp.arange(2)[::-1] ^ core)[:, None, None]
-    runs = (2 * jnp.arange(2)[None, :, None] + runs) * share + jnp.arange(share)
-    hit = runs[:, None, :, :, None] == places
-    pick = jnp.sum(jnp.where(hit, place[None, :, None, None, :], 0), axis=4)
-    pick = (pick * sections + spots[None, :, None, None]).reshape(-1).astype(jnp.int32)
+    back = jnp.array([0, 0, 1, 1, -1, -1, 2, 2])
+    from_section = (section // 2 - back) % along * 2 + (y_lo ^ jnp.array([0, 1] * 4))
+    run = jnp.sum(
+        jnp.where(from_section[:, None, None] == spots, table[None, :, :, 0], 0), axis=2
+    )
+    side = run // share
+    pick = (side % 2 == core) * along + spots // 2
+    pick = ((pick * 2 + side // 2) * 2 + spots % 2) * share + run % share
+    pick = pick.reshape(-1).astype(jnp.int32)
+    hat, hat_inv = pl.pallas_call(
+        hat_kernel,
+        out_shape=(shape((share * UNIT, depth), F32), shape((share * UNIT, LANES), F32)),
+        grid_spec=pltpu.PrefetchScalarGridSpec(
+            num_scalar_prefetch=1,
+            grid=(share,),
+            in_specs=[ANY, pl.BlockSpec((UNIT, depth), lambda i, first: (first[0] + i, 0))],
+            out_specs=(
+                pl.BlockSpec((UNIT, depth), lambda i, first: (i, 0)),
+                pl.BlockSpec((UNIT, LANES), lambda i, first: (i, 0)),
+            ),
+        ),
+        compiler_params=WIDE,
+        cost_estimate=FREE,
+        name="vision_hat",
+    )((tensor * share).reshape(1).astype(jnp.int32), table, vision_rows)
     upstream, text_stat = pl.pallas_call(
         prepare_kernel,
         out_shape=(shape((slots, columns), F32), shape((8, LANES), F32)),
@@ -330,27 +404,45 @@
             shape((slots, columns), F32),
             shape((8, LANES), F32),
         ),
-        in_specs=[SMEM, ANY, VMEM, VMEM, VMEM],
+        in_specs=[SMEM, ANY, ANY, VMEM, VMEM, VMEM],
         out_specs=(VMEM, VMEM, VMEM),
         compiler_params=PARAMS,
         cost_estimate=FREE,
         name="slots",
-    )(where, pick, partial, upstream, text_stat)
+    )(where, pick, hat, partial, upstream, text_stat)
     stats = [stat] + [
         lax.ppermute(stat, ("y_hi", "core"), [(i, i ^ turn) for i in range(tensors)])
         for turn in range(1, tensors)
     ]
     grads = pl.pallas_call(
         functools.partial(grad_kernel, width),
-        out_shape=pltpu.HBM((sections, slots, columns), BF),
+        out_shape=shape((sections, UNIT, columns), BF),
         in_specs=[SMEM, SMEM] + [VMEM] * (3 + tensors),
         out_specs=VMEM,
         compiler_params=PARAMS,
         cost_estimate=FREE,
         name="grads",
     )(where, has, feature, slope, upstream, *stats)
-    grads = lax.all_to_all(grads, "section", 0, 0, tiled=True)
-    grads = grads.reshape(sections * sections, UNIT, columns)
+    def turn(block, dx, dy=0):
+        moves = [
+            (i, (i // along ^ dy) * along + (i + dx) % along) for i in range(sections)
+        ]
+        return lax.ppermute(block, ("y_lo", "x"), moves)
+
+    across = turn(grads, 0, 1)
+    left, right = lax.optimization_barrier((turn(grads, 1), turn(grads, -1)))
+    left_across, right_across = turn(across, 1), turn(across, -1)
+    opposite, opposite_across = turn(left, 1), turn(right_across, -1)
+    blocks = [grads, across, left, left_across, right, right_across, opposite, opposite_across]
+    grads = pl.pallas_call(
+        arrange_kernel,
+        out_shape=shape((sections * sections, UNIT, columns), BF),
+        in_specs=[SMEM] + [VMEM] * sections,
+        out_specs=VMEM,
+        compiler_params=PARAMS,
+        cost_estimate=FREE,
+        name="arrange",
+    )(pick, *blocks)
     normed = pl.pallas_call(
         functools.partial(normed_kernel, width),
         out_shape=shape((slots, columns), BF),
@@ -361,73 +453,78 @@
         name="normed",
     )(where, has, text_rows, feature, text_gain_row, *stats)
 
-    targets = sections * 2
-    runs_half = sections * units // 4
-    full = [
-        SMEM,
-        pl.BlockSpec((sections * sections, UNIT, columns), lambda *i: (0, 0, 0)),
-        pl.BlockSpec((padded, columns), lambda *i: (0, 0)),
-    ]
-    got = []
-    for h in range(2):
-        given = pl.pallas_call(
-            functools.partial(give_kernel, h * runs_half),
-            out_shape=shape((runs_half * UNIT, padded), BF),
-            in_specs=[SMEM, VMEM, VMEM],
-            out_specs=VMEM,
+    peers = sections * 2
+    quarter = sections * units // 4
+
+    def product(first, count, dtype, name):
+        return pl.pallas_call(
+            back_kernel,
+            out_shape=shape((count * quarter * UNIT, padded), dtype),
+            grid=(count,),
+            in_specs=[
+                pl.BlockSpec((quarter, UNIT, columns), lambda i: (first + i, 0, 0)),
+                pl.BlockSpec((padded, columns), lambda i: (0, 0)),
+            ],
+            out_specs=pl.BlockSpec((quarter * UNIT, padded), lambda i: (i, 0)),
             compiler_params=PARAMS,
             cost_estimate=FREE,
-            name=f"give{h}",
-        )(pick, grads, weight)
-        got.append(lax.ppermute(given, "core", swap_core))
+            name=name,
+        )(grads, weight)
+
+    got = [
+        lax.ppermute(product(h, 1, BF, f"give{h}"), "core", swap_core) for h in range(2)
+    ]
     total = pl.pallas_call(
-        functools.partial(keep_kernel, 2 * runs_half),
-        out_shape=pltpu.HBM((targets, share * UNIT, padded), BF),
+        join_kernel,
+        out_shape=pltpu.HBM((peers, share * UNIT, padded), BF),
         grid=(2,),
-        in_specs=full + [pl.BlockSpec((runs_half * UNIT, padded), lambda i: (0, 0))] * 2,
+        in_specs=[pl.BlockSpec((quarter * UNIT, padded), lambda i: (i, 0))]
+        + [pl.BlockSpec((quarter * UNIT, padded), lambda i: (0, 0))] * 2,
         out_specs=pl.BlockSpec((sections, share * UNIT, padded), lambda i: (i, 0, 0)),
         compiler_params=PARAMS,
         cost_estimate=FREE,
-        name="keep",
-    )(pick, grads, weight, *got)
-    back = lax.all_to_all(total, ("section", "y_hi"), 0, 0, tiled=True)
+        name="join",
+    )(product(2, 2, F32, "keep"), *got)
+    back = lax.all_to_all(total, ("x", "y_hi", "y_lo"), 0, 0, tiled=True)
+    order = []
+    for y_lo in range(2):
+        for x in range(along):
+            order.append([(x * 2 + y_hi) * 2 + y_lo for y_hi in range(2)])
     vision_grad = pl.pallas_call(
-        functools.partial(final_kernel, chunk),
+        functools.partial(final_kernel, chunk, order),
         out_shape=shape((share * UNIT, depth), BF),
-        grid_spec=pltpu.PrefetchScalarGridSpec(
-            num_scalar_prefetch=1,
-            grid=(share,),
-            in_specs=[
-                pl.BlockSpec((targets, UNIT, padded), lambda i, first: (0, i, 0)),
-                pl.BlockSpec((UNIT, depth), lambda i, first: (first[0] + i, 0)),
-                pl.BlockSpec((depth,), lambda i, first: (0,)),
-            ],
-            out_specs=pl.BlockSpec((UNIT, depth), lambda i, first: (i, 0)),
-        ),
-        compiler_params=WIDE,
+        grid=(share,),
+        in_specs=[
+            pl.BlockSpec((peers, UNIT, padded), lambda i: (0, i, 0)),
+            pl.BlockSpec((UNIT, depth), lambda i: (i, 0)),
+            pl.BlockSpec((UNIT, LANES), lambda i: (i, 0)),
+            pl.BlockSpec((depth,), lambda i: (0,)),
+        ],
+        out_specs=pl.BlockSpec((UNIT, depth), lambda i: (i, 0)),
+        compiler_params=PARAMS,
         cost_estimate=FREE,
         name="vision_back",
-    )((tensor * share).reshape(1).astype(jnp.int32), back, vision_rows, vision_gain)
+    )(back, hat, hat_inv, vision_gain)
     return normed, vision_grad
 
 
 def solution(mesh):
     mesh = Mesh(
-        mesh.devices.reshape(mesh.shape["section"], mesh.shape["dp"], -1, 2),
-        ("section", "dp", "y_hi", "core"),
+        mesh.devices.reshape(2, mesh.shape["section"] // 2, mesh.shape["dp"], -1, 2),
+        ("y_lo", "x", "dp", "y_hi", "core"),
     )
-    tensor = ("y_hi", "core")
+    rows, tensor = ("y_lo", "x", "dp"), ("y_hi", "core")
     in_specs = (
-        P(("section", "dp"), None),
+        P(rows, None),
         P(),
         P(),
-        P(("section", "dp"), tensor),
-        P(("section", "dp"), tensor),
+        P(rows, tensor),
+        P(rows, tensor),
         P(tensor),
-        P(("section", "dp")),
-        P(("section", "dp"), tensor),
+        P(rows),
+        P(rows, tensor),
     )
-    out_specs = (P(("section", "dp"), tensor), P(("section", "dp", *tensor), None))
+    out_specs = (P(rows, tensor), P((*rows, *tensor), None))
 
     def program(*args):
         body = functools.partial(shards, args[4].shape[1])

time: 193 us -> 178 us (0.922)
  blocking collectives: 31 us -> 0 us
  starting transfers between devices: 35.1 us -> 48.9 us
  local copies, waits for them, and re-layouts: 12.5 us -> 15.2 us
    all_to_all x1 -> x0, blocking collectives: 31 us -> none  [shards(): grads = lax.all_to_all(grads, 'section', 0, 0, tiled=True)]
    ppermute x3 -> x10, starting transfers between devices: 2.07 us -> 13.9 us  [the longest x7 11.3 us: turn(): return lax.ppermute(block, ('y_lo', 'x'), moves)]
    ppermute x3 -> x10, waiting for transfers between devices: 12.7 us -> 15.8 us  [the longest x7 12 us: turn(): return lax.ppermute(block, ('y_lo', 'x'), moves)]
    all_to_all x3, waiting for transfers between devices: 48.4 us -> 45.7 us  [the longest x1 25 us: shards(): partial = lax.all_to_all(partial, along_first, 0, 0, tiled=True)]
    unnamed x23 -> x31, local copies, waits for them, and re-layouts: 4.25 us -> 6.78 us
    pallas_call x6 -> x11, Pallas kernels: 20.5 us -> 21 us  [the longest x1 6.03 us: shards(): pl.pallas_call(forward_kernel, out_shape=(shape((units, sections * UNIT,...]
    dynamic_update_slice x8 -> x7, local copies, waits for them, and re-layouts: 6.27 us -> 6.23 us  [put(): lax.dynamic_update_slice_in_dim(out, piece, owner % groups * height, 0)]
  transfers between devices with their start and end apart: 16 -> 23, of which waited for: 10 -> 15; matrix products, arithmetic and copies ran while one was open for 6% -> 7% of each run, Pallas kernels for 4% -> 11%
where the time goes in v4:
time: 178 us; the launch traced here: 177 us
  waiting for transfers between devices  77.3 us (43%)
  starting transfers between devices  48.9 us (27%)
  Pallas kernels  31 us (17%)
  local copies, waits for them, and re-layouts  15.2 us (9%)
  other arithmetic  3.57 us (2%)
    all_to_all x1, waiting for transfers between devices, shards(): partial = lax.all_to_all(partial, along_first, 0, 0, tiled=True)  25 us
    all_to_all x1, waiting for transfers between devices, shards(): back = lax.all_to_all(total, ('x', 'y_hi', 'y_lo'), 0, 0, tiled=True)  20.6 us
    ppermute x7, waiting for transfers between devices, turn(): return lax.ppermute(block, ('y_lo', 'x'), moves)  12 us
    ppermute x3, waiting for transfers between devices, ring_gather(): rising = lax.ppermute(rising, 'dp', up)  11.9 us
    ppermute x7, starting transfers between devices, turn(): return lax.ppermute(block, ('y_lo', 'x'), moves)  11.3 us
    ppermute x3, starting transfers between devices, ring_gather(): falling = lax.ppermute(falling, 'dp', down)  8.7 us
    unnamed x31, local copies, waits for them, and re-layouts  6.78 us
    all_to_all x1, starting transfers between devices, shards(): partial = lax.all_to_all(partial, along_first, 0, 0, tiled=True)  6.62 us
  transfers between devices with their start and end apart: 23, of which 15 were waited for; matrix products, arithmetic and copies ran while one was open for 7% of the time, Pallas kernels for 11%

profile of v4, /device:TPU:8, one launch (start us, length us, event | category | flops | bytes accessed | tf_op | source)
XLA Modules:
  0.0 177.0 jit_solution(1959363570054961133)
XLA Ops:
  0.6 2.0 %collective-permute-start = (bf16[200,1024]{1,0:T(8,128)(2,1)}, bf16[200,1024]{1,0:T(8,128)(2,1)}, u32[]{:S(2)}, u32[]{:S(2)}) collective-permute-start(bf16[200,1024]{1,0:T(8,128)(2,1)} %param.13), channel_id=1, source_target_pairs={{0,4},{4,8},{8,12},{12,16},{16,20},{20,24},{24,28},{28,0},{1,5},{5... | collective-permute-start | bytes 1228808 | tf_op jit(solution)/shard_map/ppermute | solution.py:217
  2.6 4.0 %collective-permute-start.1 = (bf16[200,1024]{1,0:T(8,128)(2,1)}, bf16[200,1024]{1,0:T(8,128)(2,1)}, u32[]{:S(2)}, u32[]{:S(2)}) collective-permute-start(bf16[200,1024]{1,0:T(8,128)(2,1)} %param.13), channel_id=1, source_target_pairs={{0,28},{4,0},{8,4},{12,8},{16,12},{20,16},{24,20},{28,24},{1,29},{... | collective-permute-start | bytes 1228808 | tf_op jit(solution)/shard_map/ppermute | solution.py:218
  6.7 0.7 reshape.191
  8.6 0.7 and_select_fusion.7
  9.3 0.8 select_reduce_fusion.5
  10.1 5.6 %vision_norm.1.array_ref = bf16[8,64,1664]{2,1,0:T(8,128)(2,1)} custom-call(s32[4]{0:T(128)} %copy-done.14, s32[4]{0:T(128)} %get-tuple-element.53.live_ref, s32[4]{0:T(128)} %get-tuple-element.52.spot_ref, bf16[128,12800]{1,0:T(8,128)(2,1)} %rows_ref.3, f32[12800]{0:T(1024)} %gain_ref.3, f32[12800]{0:T(1024)} %bias_ref.1), custom_call_target="tpu_custom_call" | custom-call | tf_op jit(solution)/shard_map/vision_norm/pallas_call | solution.py:278
  15.7 0.4 broadcast_in_dim.86
  16.4 5.9 %all-to-all-start = ((bf16[8,64,1664]{2,1,0:T(8,128)(2,1)}), bf16[8,64,1664]{2,1,0:T(8,128)(2,1)}, u32[]{:S(2)}, u32[]{:S(2)}) async-start(bf16[8,64,1664]{2,1,0:T(8,128)(2,1)} %after.1), calls=%async_computation | async-start | bytes 3407872 | tf_op jit(solution)/shard_map/all_to_all | solution.py:307
  22.2 3.2 %collective-permute-start.3 = (bf16[200,1024]{1,0:T(8,128)(2,1)}, bf16[200,1024]{1,0:T(8,128)(2,1)}, u32[]{:S(2)}, u32[]{:S(2)}) collective-permute-start(bf16[200,1024]{1,0:T(8,128)(2,1)} %collective-permute-done.1), channel_id=1, source_target_pairs={{0,28},{4,0},{8,4},{12,8},{16,12},{20,16},{24,20},{28,24},{1,29},{... | collective-permute-start | bytes 1228808 | tf_op jit(solution)/shard_map/ppermute | solution.py:218
  25.5 1.0 constant_dynamic-update-slice_fusion.7
  26.5 1.0 constant_dynamic-update-slice_fusion.6
  27.6 6.3 %collective-permute-done.2 = bf16[200,1024]{1,0:T(8,128)(2,1)} collective-permute-done((bf16[200,1024]{1,0:T(8,128)(2,1)}, bf16[200,1024]{1,0:T(8,128)(2,1)}, u32[]{:S(2)}, u32[]{:S(2)}) %collective-permute-start.2) | collective-permute-done | bytes 409632 | tf_op jit(solution)/shard_map/ppermute | solution.py:217
  33.9 1.8 %collective-permute-start.4 = (bf16[200,1024]{1,0:T(8,128)(2,1)}, bf16[200,1024]{1,0:T(8,128)(2,1)}, u32[]{:S(2)}, u32[]{:S(2)}) collective-permute-start(bf16[200,1024]{1,0:T(8,128)(2,1)} %collective-permute-done.2), channel_id=1, source_target_pairs={{0,4},{4,8},{8,12},{12,16},{16,20},{20,24},{24,28},{28,0},{1,5},{5... | collective-permute-start | bytes 1228808 | tf_op jit(solution)/shard_map/ppermute | solution.py:217
  35.7 1.4 collective-permute-start.5
  37.1 1.0 constant_dynamic-update-slice_fusion.5
  38.2 1.0 constant_dynamic-update-slice_fusion.4
  39.2 5.4 %collective-permute-done.4 = bf16[200,1024]{1,0:T(8,128)(2,1)} collective-permute-done((bf16[200,1024]{1,0:T(8,128)(2,1)}, bf16[200,1024]{1,0:T(8,128)(2,1)}, u32[]{:S(2)}, u32[]{:S(2)}) %collective-permute-start.4) | collective-permute-done | bytes 409632 | tf_op jit(solution)/shard_map/ppermute | solution.py:217
  44.9 0.9 copy-done.4
  45.8 0.9 copy-done.8
  47.0 2.0 %collective-permute-start.7 = (bf16[200,1024]{1,0:T(8,128)(2,1)}, bf16[200,1024]{1,0:T(8,128)(2,1)S(1)}, u32[]{:S(2)}, u32[]{:S(2)}) collective-permute-start(bf16[200,1024]{1,0:T(8,128)(2,1)} %collective-permute-done.4), channel_id=1, source_target_pairs={{0,4},{4,8},{8,12},{12,16},{16,20},{20,24},{24,28},{28,0},{1,5},{5... | collective-permute-start | bytes 1228808 | tf_op jit(solution)/shard_map/ppermute | solution.py:225
  49.1 1.0 constant_dynamic-update-slice_fusion.3
  50.1 1.0 constant_dynamic-update-slice_fusion.2.weight_ref
  51.2 6.0 %forward.1 = (f32[8,128,1024]{2,1,0:T(8,128)S(1)}, bf16[8,128,384]{2,1,0:T(8,128)(2,1)S(1)}, f32[8,8,128]{2,1,0:T(8,128)S(1)}) custom-call(s32[1]{0:T(128)} %bitcast.core_ref, s32[1]{0:T(128)} %bitcast.1.tile_ref, bf16[8,64,1664]{2,1,0:T(8,128)(2,1)} %all-to-all-done.own_ref, bf16[8,64,1664]{2,1,0:T(8,128)(2,1)} %collective-permute-done.6.other_ref, ...), custom_call_target="tpu_custom_call" | custom-call | tf_op jit(solution)/shard_map/forward/pallas_call | solution.py:321
  57.2 3.0 %collective-permute-done.7 = bf16[200,1024]{1,0:T(8,128)(2,1)S(1)} collective-permute-done((bf16[200,1024]{1,0:T(8,128)(2,1)}, bf16[200,1024]{1,0:T(8,128)(2,1)S(1)}, u32[]{:S(2)}, u32[]{:S(2)}) %collective-permute-start.7) | collective-permute-done | bytes 409632 | tf_op jit(solution)/shard_map/ppermute | solution.py:225
  60.4 2.6 %tail.1 = bf16[8,128,1024]{2,1,0:T(8,128)(2,1)} custom-call(bf16[8,128,384]{2,1,0:T(8,128)(2,1)S(1)} %get-tuple-element.42.window_ref, bf16[384,1024]{1,0:T(8,128)(2,1)S(1)} %get-tuple-element.61.weight_ref, f32[8,128,1024]{2,1,0:T(8,128)S(1)} %get-tuple-element.43.main_ref), custom_call_target="tpu_custom_call" | custom-call | tf_op jit(solution)/shard_map/tail/pallas_call | solution.py:345
  63.0 6.6 %all-to-all-start.1 = ((bf16[8,128,1024]{2,1,0:T(8,128)(2,1)}), bf16[8,128,1024]{2,1,0:T(8,128)(2,1)}, u32[]{:S(2)}, u32[]{:S(2)}) async-start(bf16[8,128,1024]{2,1,0:T(8,128)(2,1)} %tail.1), calls=%async_computation.1 | async-start | bytes 4194304 | tf_op jit(solution)/shard_map/all_to_all | solution.py:354
  69.7 0.2 slice_reduce_fusion
  70.0 0.4 copy-done.13
  70.3 2.8 %vision_hat.1 = (f32[32,12800]{1,0:T(8,128)}, f32[32,128]{1,0:T(8,128)}) custom-call(s32[1]{0:T(128)} %bitcast.8.first_ref, s32[8,8,3]{2,1,0:T(8,128)} %copy-done.13, bf16[128,12800]{1,0:T(8,128)(2,1)} %rows_ref.3), custom_call_target="tpu_custom_call" | custom-call | tf_op jit(solution)/shard_map/vision_hat/pallas_call | solution.py:375
  73.2 0.2 select_reduce_fusion
  74.2 0.2 select_reduce_fusion.1
  74.5 25.0 %all-to-all-done.1.parts_ref = bf16[8,128,1024]{2,1,0:T(8,128)(2,1)} async-done(((bf16[8,128,1024]{2,1,0:T(8,128)(2,1)}), bf16[8,128,1024]{2,1,0:T(8,128)(2,1)}, u32[]{:S(2)}, u32[]{:S(2)}) %all-to-all-start.1) | async-done | bytes 2097184 | tf_op jit(solution)/shard_map/all_to_all | solution.py:354
  99.5 1.4 copy-done
  100.9 1.0 copy-done.3
  102.0 2.2 %slots.1 = (bf16[128,1024]{1,0:T(8,128)(2,1)S(1)}, f32[128,1024]{1,0:T(8,128)S(1)}, f32[8,128]{1,0:T(8,128)S(1)}) custom-call(s32[8]{0:T(128)S(1)} %fusion.18.place_ref, s32[64]{0:T(128)S(1)} %fusion.12.pick_ref, f32[32,12800]{1,0:T(8,128)S(1)} %copy-done, bf16[8,128,1024]{2,1,0:T(8,128)(2,1)} %all-to-all-done.1.parts_ref, f32[128,1024]{1,0:T(8,128)S(1)} %copy-done.3, ...), custom_call_target="tpu_custom_call" | custom-call | tf_op jit(solution)/shard_map/slots/pallas_call | solution.py:400
  104.2 0.9 collective-permute-start.10
  105.1 1.6 collective-permute-start.8
  106.7 1.2 collective-permute-start.9
  107.9 0.9 collective-permute-done.10.refs_3_
  108.8 3.0 %collective-permute-done.9.refs_2_ = f32[8,128]{1,0:T(8,128)S(1)} collective-permute-done((f32[8,128]{1,0:T(8,128)S(1)}, f32[8,128]{1,0:T(8,128)S(1)}, u32[]{:S(2)}, u32[]{:S(2)}) %collective-permute-start.9) | collective-permute-done | bytes 4128 | tf_op jit(solution)/shard_map/ppermute | solution.py:414
  111.8 0.9 grads.1.refs_0_
  112.7 2.5 %collective-permute-start.11 = (bf16[8,16,1024]{2,1,0:T(8,128)(2,1)S(1)}, bf16[8,16,1024]{2,1,0:T(8,128)(2,1)S(1)}, u32[]{:S(2)}, u32[]{:S(2)}) collective-permute-start(bf16[8,16,1024]{2,1,0:T(8,128)(2,1)S(1)} %grads.1.refs_0_), channel_id=1, source_target_pairs={{0,128},{32,160},{64,192},{96,224},{128,0},{160,32},{192,64},{224,... | collective-permute-start | bytes 786440 | tf_op jit(solution)/shard_map/ppermute | solution.py:430
  115.2 3.2 %collective-permute-start.13 = (bf16[8,16,1024]{2,1,0:T(8,128)(2,1)S(1)}, bf16[8,16,1024]{2,1,0:T(8,128)(2,1)S(1)}, u32[]{:S(2)}, u32[]{:S(2)}) collective-permute-start(bf16[8,16,1024]{2,1,0:T(8,128)(2,1)S(1)} %grads.1.refs_0_), channel_id=1, source_target_pairs={{0,96},{32,0},{64,32},{96,64},{128,224},{160,128},{192,160},{224,1... | collective-permute-start | bytes 786440 | tf_op jit(solution)/shard_map/ppermute | solution.py:430
  118.4 2.1 %collective-permute-done.11.refs_1_ = bf16[8,16,1024]{2,1,0:T(8,128)(2,1)S(1)} collective-permute-done((bf16[8,16,1024]{2,1,0:T(8,128)(2,1)S(1)}, bf16[8,16,1024]{2,1,0:T(8,128)(2,1)S(1)}, u32[]{:S(2)}, u32[]{:S(2)}) %collective-permute-start.11) | collective-permute-done | bytes 262176 | tf_op jit(solution)/shard_map/ppermute | solution.py:430
  120.5 2.7 %collective-permute-done.12.refs_2_ = bf16[8,16,1024]{2,1,0:T(8,128)(2,1)S(1)} collective-permute-done((bf16[8,16,1024]{2,1,0:T(8,128)(2,1)S(1)}, bf16[8,16,1024]{2,1,0:T(8,128)(2,1)S(1)}, u32[]{:S(2)}, u32[]{:S(2)}) %collective-permute-start.12) | collective-permute-done | bytes 262176 | tf_op jit(solution)/shard_map/ppermute | solution.py:430
  123.2 2.0 %collective-permute-done.13.refs_4_ = bf16[8,16,1024]{2,1,0:T(8,128)(2,1)S(1)} collective-permute-done((bf16[8,16,1024]{2,1,0:T(8,128)(2,1)S(1)}, bf16[8,16,1024]{2,1,0:T(8,128)(2,1)S(1)}, u32[]{:S(2)}, u32[]{:S(2)}) %collective-permute-start.13) | collective-permute-done | bytes 262176 | tf_op jit(solution)/shard_map/ppermute | solution.py:430
  125.2 1.9 %collective-permute-start.14 = (bf16[8,16,1024]{2,1,0:T(8,128)(2,1)S(1)}, bf16[8,16,1024]{2,1,0:T(8,128)(2,1)S(1)}, u32[]{:S(2)}, u32[]{:S(2)}) collective-permute-start(bf16[8,16,1024]{2,1,0:T(8,128)(2,1)S(1)} %collective-permute-done.11.refs_1_), channel_id=1, source_target_pairs={{0,32},{32,64},{64,96},{96,0},{128,160},{160,192},{192,224},{224,1... | collective-permute-start | bytes 786440 | tf_op jit(solution)/shard_map/ppermute | solution.py:430
  127.1 1.0 collective-permute-done.15.refs_5_
  128.1 3.7 %collective-permute-start.17 = (bf16[8,16,1024]{2,1,0:T(8,128)(2,1)S(1)}, bf16[8,16,1024]{2,1,0:T(8,128)(2,1)S(1)}, u32[]{:S(2)}, u32[]{:S(2)}) collective-permute-start(bf16[8,16,1024]{2,1,0:T(8,128)(2,1)S(1)} %collective-permute-done.15.refs_5_), channel_id=1, source_target_pairs={{0,96},{32,0},{64,32},{96,64},{128,224},{160,128},{192,160},{224,1... | collective-permute-start | bytes 786440 | tf_op jit(solution)/shard_map/ppermute | solution.py:430
  131.8 1.5 collective-permute-done.16.refs_6_
  133.2 2.8 %collective-permute-done.14.refs_3_ = bf16[8,16,1024]{2,1,0:T(8,128)(2,1)S(1)} collective-permute-done((bf16[8,16,1024]{2,1,0:T(8,128)(2,1)S(1)}, bf16[8,16,1024]{2,1,0:T(8,128)(2,1)S(1)}, u32[]{:S(2)}, u32[]{:S(2)}) %collective-permute-start.14) | collective-permute-done | bytes 262176 | tf_op jit(solution)/shard_map/ppermute | solution.py:430
  136.0 0.7 arrange.1.grads_ref
  136.7 1.1 give1.1
  137.9 1.1 give0.1
  139.2 0.5 collective-permute-start.18
  139.7 2.3 %keep.1.own_ref = f32[512,1664]{1,0:T(8,128)S(1)} custom-call(bf16[64,16,1024]{2,1,0:T(8,128)(2,1)S(1)} %arrange.1.grads_ref, bf16[1664,1024]{1,0:T(8,128)(2,1)S(1)} %get-tuple-element.60.weight_ref), custom_call_target="tpu_custom_call" | custom-call | tf_op jit(solution)/shard_map/keep/pallas_call | solution.py:460
  142.0 0.8 collective-permute-done.18.low_ref
  142.7 1.4 join.1
  144.2 6.2 %all-to-all-start.2 = ((bf16[16,32,1664]{2,1,0:T(8,128)(2,1)}), bf16[16,32,1664]{2,1,0:T(8,128)(2,1)S(1)}, u32[]{:S(2)}, u32[]{:S(2)}) async-start(bf16[16,32,1664]{2,1,0:T(8,128)(2,1)} %join.1), calls=%async_computation.2 | async-start | bytes 3407872 | tf_op jit(solution)/shard_map/all_to_all | solution.py:488
  150.4 0.9 copy-done.5
  151.3 0.9 copy-done.7
  152.3 2.1 %normed.1 = bf16[128,1024]{1,0:T(8,128)(2,1)} custom-call(s32[8]{0:T(128)S(1)} %fusion.18.place_ref, s32[8]{0:T(128)S(1)} %convert_element_type.60.live_ref, bf16[128,1024]{1,0:T(8,128)(2,1)S(1)} %copy-done.5, bf16[128,1024]{1,0:T(8,128)(2,1)S(1)} %copy-done.7, f32[1,1024]{1,0:T(1,128)S(1)} %bitcast.17, f32[8,128]{1,0:T(8,128)S(1)} %get-tuple-element.47.refs_0_, ...), custom_call_target="tpu_custom_call" | custom-call | tf_op jit(solution)/shard_map/normed/pallas_call | solution.py:446
  154.3 20.6 %all-to-all-done.2.parts_ref = bf16[16,32,1664]{2,1,0:T(8,128)(2,1)S(1)} async-done(((bf16[16,32,1664]{2,1,0:T(8,128)(2,1)}), bf16[16,32,1664]{2,1,0:T(8,128)(2,1)S(1)}, u32[]{:S(2)}, u32[]{:S(2)}) %all-to-all-start.2) | async-done | bytes 1703968 | tf_op jit(solution)/shard_map/all_to_all | solution.py:488
  175.0 2.0 %vision_back.1 = bf16[32,12800]{1,0:T(8,128)(2,1)} custom-call(bf16[16,32,1664]{2,1,0:T(8,128)(2,1)S(1)} %all-to-all-done.2.parts_ref, f32[32,12800]{1,0:T(8,128)S(1)} %copy-done.1, f32[32,128]{1,0:T(8,128)S(1)} %copy-done.10, f32[12800]{0:T(1024)S(1)} %copy-done.9), custom_call_target="tpu_custom_call" | custom-call | tf_op jit(solution)/shard_map/vision_back/pallas_call | solution.py:493
  (83 shorter events, 3.2 us)
Async XLA Ops:
  0.6 15.7 %collective-permute-start = (bf16[200,1024]{1,0:T(8,128)(2,1)}, bf16[200,1024]{1,0:T(8,128)(2,1)}, u32[]{:S(2)}, u32[]{:S(2)}) collective-permute-start(bf16[200,1024]{1,0:T(8,128)(2,1)} %param.13), channel_id=1, source_target_pairs={{0,4},{4,8},{8,12},{12,16},{16,20},{20,24},{24,28},{28,0},{1,5},{5... | collective-permute-start | bytes 1228808 | tf_op jit(solution)/shard_map/ppermute | solution.py:217
  2.6 13.7 %collective-permute-start.1 = (bf16[200,1024]{1,0:T(8,128)(2,1)}, bf16[200,1024]{1,0:T(8,128)(2,1)}, u32[]{:S(2)}, u32[]{:S(2)}) collective-permute-start(bf16[200,1024]{1,0:T(8,128)(2,1)} %param.13), channel_id=1, source_target_pairs={{0,28},{4,0},{8,4},{12,8},{16,12},{20,16},{24,20},{28,24},{1,29},{... | collective-permute-start | bytes 1228808 | tf_op jit(solution)/shard_map/ppermute | solution.py:218
  8.6 1.5 copy-start.14
  10.1 6.0 %copy-start.12 = (bf16[200,1024]{1,0:T(8,128)(2,1)S(1)}, bf16[200,1024]{1,0:T(8,128)(2,1)}, u32[]{:S(2)}) copy-start(bf16[200,1024]{1,0:T(8,128)(2,1)} %param.13) | copy-start | bytes 1228804
  16.4 28.5 %copy-start.11 = (f32[1024]{0:T(1024)S(1)}, f32[1024]{0:T(1024)}, u32[]{:S(2)}) copy-start(f32[1024]{0:T(1024)} %param.15) | copy-start | bytes 12292
  16.4 28.3 %all-to-all-start = ((bf16[8,64,1664]{2,1,0:T(8,128)(2,1)}), bf16[8,64,1664]{2,1,0:T(8,128)(2,1)}, u32[]{:S(2)}, u32[]{:S(2)}) async-start(bf16[8,64,1664]{2,1,0:T(8,128)(2,1)} %after.1), calls=%async_computation | async-start | bytes 3407872 | tf_op jit(solution)/shard_map/all_to_all | solution.py:307
  22.2 11.6 %collective-permute-start.2 = (bf16[200,1024]{1,0:T(8,128)(2,1)}, bf16[200,1024]{1,0:T(8,128)(2,1)}, u32[]{:S(2)}, u32[]{:S(2)}) collective-permute-start(bf16[200,1024]{1,0:T(8,128)(2,1)} %collective-permute-done.before_ref), channel_id=1, source_target_pairs={{0,4},{4,8},{8,12},{12,16},{16,20},{20,24},{24,28},{28,0},{1,5},{5... | collective-permute-start | bytes 1228808 | tf_op jit(solution)/shard_map/ppermute | solution.py:217
  22.2 11.6 %collective-permute-start.3 = (bf16[200,1024]{1,0:T(8,128)(2,1)}, bf16[200,1024]{1,0:T(8,128)(2,1)}, u32[]{:S(2)}, u32[]{:S(2)}) collective-permute-start(bf16[200,1024]{1,0:T(8,128)(2,1)} %collective-permute-done.1), channel_id=1, source_target_pairs={{0,28},{4,0},{8,4},{12,8},{16,12},{20,16},{24,20},{28,24},{1,29},{... | collective-permute-start | bytes 1228808 | tf_op jit(solution)/shard_map/ppermute | solution.py:218
  33.9 10.7 %collective-permute-start.4 = (bf16[200,1024]{1,0:T(8,128)(2,1)}, bf16[200,1024]{1,0:T(8,128)(2,1)}, u32[]{:S(2)}, u32[]{:S(2)}) collective-permute-start(bf16[200,1024]{1,0:T(8,128)(2,1)} %collective-permute-done.2), channel_id=1, source_target_pairs={{0,4},{4,8},{8,12},{12,16},{16,20},{20,24},{24,28},{28,0},{1,5},{5... | collective-permute-start | bytes 1228808 | tf_op jit(solution)/shard_map/ppermute | solution.py:217
  35.7 8.9 %collective-permute-start.5 = (bf16[200,1024]{1,0:T(8,128)(2,1)}, bf16[200,1024]{1,0:T(8,128)(2,1)}, u32[]{:S(2)}, u32[]{:S(2)}) collective-permute-start(bf16[200,1024]{1,0:T(8,128)(2,1)} %collective-permute-done.3), channel_id=1, source_target_pairs={{0,28},{4,0},{8,4},{12,8},{16,12},{20,16},{24,20},{28,24},{1,29},{... | collective-permute-start | bytes 1228808 | tf_op jit(solution)/shard_map/ppermute | solution.py:218
  44.6 6.5 %collective-permute-start.6 = (bf16[8,64,1664]{2,1,0:T(8,128)(2,1)}, bf16[8,64,1664]{2,1,0:T(8,128)(2,1)}, u32[]{:S(2)}, u32[]{:S(2)}) collective-permute-start(bf16[8,64,1664]{2,1,0:T(8,128)(2,1)} %all-to-all-done.own_ref), channel_id=1, source_target_pairs={{0,1},{1,0},{2,3},{3,2},{4,5},{5,4},{6,7},{7,6},{8,9},{9,8},{10,11... | collective-permute-start | bytes 5111816 | tf_op jit(solution)/shard_map/ppermute | solution.py:309
  44.9 1.0 copy-start.4
  45.8 0.9 copy-start.8
  47.0 4.2 %copy-start.2 = (f32[128,1024]{1,0:T(8,128)}, f32[128,1024]{1,0:T(8,128)S(1)}, u32[]{:S(2)}) copy-start(f32[128,1024]{1,0:T(8,128)S(1)} %get-tuple-element.44.upstream_ref) | copy-start | bytes 1572868
  47.0 13.3 %collective-permute-start.7 = (bf16[200,1024]{1,0:T(8,128)(2,1)}, bf16[200,1024]{1,0:T(8,128)(2,1)S(1)}, u32[]{:S(2)}, u32[]{:S(2)}) collective-permute-start(bf16[200,1024]{1,0:T(8,128)(2,1)} %collective-permute-done.4), channel_id=1, source_target_pairs={{0,4},{4,8},{8,12},{12,16},{16,20},{20,24},{24,28},{28,0},{1,5},{5... | collective-permute-start | bytes 1228808 | tf_op jit(solution)/shard_map/ppermute | solution.py:225
  63.0 36.5 %all-to-all-start.1 = ((bf16[8,128,1024]{2,1,0:T(8,128)(2,1)}), bf16[8,128,1024]{2,1,0:T(8,128)(2,1)}, u32[]{:S(2)}, u32[]{:S(2)}) async-start(bf16[8,128,1024]{2,1,0:T(8,128)(2,1)} %tail.1), calls=%async_computation.1 | async-start | bytes 4194304 | tf_op jit(solution)/shard_map/all_to_all | solution.py:354
  69.7 0.6 copy-start.13
  99.5 1.4 copy-start
  100.9 1.0 copy-start.3
  104.2 33.7 %copy-start.6 = (bf16[128,1024]{1,0:T(8,128)(2,1)}, bf16[128,1024]{1,0:T(8,128)(2,1)S(1)}, u32[]{:S(2)}) copy-start(bf16[128,1024]{1,0:T(8,128)(2,1)S(1)} %get-tuple-element.46.feature_ref) | copy-start | bytes 786436
  104.2 4.6 %collective-permute-start.10 = (f32[8,128]{1,0:T(8,128)S(1)}, f32[8,128]{1,0:T(8,128)S(1)}, u32[]{:S(2)}, u32[]{:S(2)}) collective-permute-start(f32[8,128]{1,0:T(8,128)S(1)} %get-tuple-element.47.refs_0_), channel_id=1, source_target_pairs={{0,3},{1,2},{2,1},{3,0},{4,7},{5,6},{6,5},{7,4},{8,11},{9,10},{10,... | collective-permute-start | bytes 12296 | tf_op jit(solution)/shard_map/ppermute | solution.py:414
  105.1 3.8 %collective-permute-start.8 = (f32[8,128]{1,0:T(8,128)S(1)}, f32[8,128]{1,0:T(8,128)S(1)}, u32[]{:S(2)}, u32[]{:S(2)}) collective-permute-start(f32[8,128]{1,0:T(8,128)S(1)} %get-tuple-element.47.refs_0_), channel_id=1, source_target_pairs={{0,1},{1,0},{2,3},{3,2},{4,5},{5,4},{6,7},{7,6},{8,9},{9,8},{10,11... | collective-permute-start | bytes 12296 | tf_op jit(solution)/shard_map/ppermute | solution.py:414
  106.7 5.1 %collective-permute-start.9 = (f32[8,128]{1,0:T(8,128)S(1)}, f32[8,128]{1,0:T(8,128)S(1)}, u32[]{:S(2)}, u32[]{:S(2)}) collective-permute-start(f32[8,128]{1,0:T(8,128)S(1)} %get-tuple-element.47.refs_0_), channel_id=1, source_target_pairs={{0,2},{1,3},{2,0},{3,1},{4,6},{5,7},{6,4},{7,5},{8,10},{9,11},{10,... | collective-permute-start | bytes 12296 | tf_op jit(solution)/shard_map/ppermute | solution.py:414
  112.7 7.8 %collective-permute-start.11 = (bf16[8,16,1024]{2,1,0:T(8,128)(2,1)S(1)}, bf16[8,16,1024]{2,1,0:T(8,128)(2,1)S(1)}, u32[]{:S(2)}, u32[]{:S(2)}) collective-permute-start(bf16[8,16,1024]{2,1,0:T(8,128)(2,1)S(1)} %grads.1.refs_0_), channel_id=1, source_target_pairs={{0,128},{32,160},{64,192},{96,224},{128,0},{160,32},{192,64},{224,... | collective-permute-start | bytes 786440 | tf_op jit(solution)/shard_map/ppermute | solution.py:430
  115.2 8.0 %collective-permute-start.12 = (bf16[8,16,1024]{2,1,0:T(8,128)(2,1)S(1)}, bf16[8,16,1024]{2,1,0:T(8,128)(2,1)S(1)}, u32[]{:S(2)}, u32[]{:S(2)}) collective-permute-start(bf16[8,16,1024]{2,1,0:T(8,128)(2,1)S(1)} %grads.1.refs_0_), channel_id=1, source_target_pairs={{0,32},{32,64},{64,96},{96,0},{128,160},{160,192},{192,224},{224,1... | collective-permute-start | bytes 786440 | tf_op jit(solution)/shard_map/ppermute | solution.py:430
  115.2 10.0 %collective-permute-start.13 = (bf16[8,16,1024]{2,1,0:T(8,128)(2,1)S(1)}, bf16[8,16,1024]{2,1,0:T(8,128)(2,1)S(1)}, u32[]{:S(2)}, u32[]{:S(2)}) collective-permute-start(bf16[8,16,1024]{2,1,0:T(8,128)(2,1)S(1)} %grads.1.refs_0_), channel_id=1, source_target_pairs={{0,96},{32,0},{64,32},{96,64},{128,224},{160,128},{192,160},{224,1... | collective-permute-start | bytes 786440 | tf_op jit(solution)/shard_map/ppermute | solution.py:430
  120.5 7.6 %collective-permute-start.15 = (bf16[8,16,1024]{2,1,0:T(8,128)(2,1)S(1)}, bf16[8,16,1024]{2,1,0:T(8,128)(2,1)S(1)}, u32[]{:S(2)}, u32[]{:S(2)}) collective-permute-start(bf16[8,16,1024]{2,1,0:T(8,128)(2,1)S(1)} %collective-permute-done.11.refs_1_), channel_id=1, source_target_pairs={{0,96},{32,0},{64,32},{96,64},{128,224},{160,128},{192,160},{224,1... | collective-permute-start | bytes 786440 | tf_op jit(solution)/shard_map/ppermute | solution.py:430
  125.2 8.0 %collective-permute-start.16 = (bf16[8,16,1024]{2,1,0:T(8,128)(2,1)S(1)}, bf16[8,16,1024]{2,1,0:T(8,128)(2,1)S(1)}, u32[]{:S(2)}, u32[]{:S(2)}) collective-permute-start(bf16[8,16,1024]{2,1,0:T(8,128)(2,1)S(1)} %collective-permute-done.12.refs_2_), channel_id=1, source_target_pairs={{0,32},{32,64},{64,96},{96,0},{128,160},{160,192},{192,224},{224,1... | collective-permute-start | bytes 786440 | tf_op jit(solution)/shard_map/ppermute | solution.py:430
  125.2 10.8 %collective-permute-start.14 = (bf16[8,16,1024]{2,1,0:T(8,128)(2,1)S(1)}, bf16[8,16,1024]{2,1,0:T(8,128)(2,1)S(1)}, u32[]{:S(2)}, u32[]{:S(2)}) collective-permute-start(bf16[8,16,1024]{2,1,0:T(8,128)(2,1)S(1)} %collective-permute-done.11.refs_1_), channel_id=1, source_target_pairs={{0,32},{32,64},{64,96},{96,0},{128,160},{160,192},{192,224},{224,1... | collective-permute-start | bytes 786440 | tf_op jit(solution)/shard_map/ppermute | solution.py:430
  128.1 8.0 %collective-permute-start.17 = (bf16[8,16,1024]{2,1,0:T(8,128)(2,1)S(1)}, bf16[8,16,1024]{2,1,0:T(8,128)(2,1)S(1)}, u32[]{:S(2)}, u32[]{:S(2)}) collective-permute-start(bf16[8,16,1024]{2,1,0:T(8,128)(2,1)S(1)} %collective-permute-done.15.refs_5_), channel_id=1, source_target_pairs={{0,96},{32,0},{64,32},{96,64},{128,224},{160,128},{192,160},{224,1... | collective-permute-start | bytes 786440 | tf_op jit(solution)/shard_map/ppermute | solution.py:430
  139.1 2.9 %collective-permute-start.19 = (bf16[256,1664]{1,0:T(8,128)(2,1)S(1)}, bf16[256,1664]{1,0:T(8,128)(2,1)S(1)}, u32[]{:S(2)}, u32[]{:S(2)}) collective-permute-start(bf16[256,1664]{1,0:T(8,128)(2,1)S(1)} %give1.1), channel_id=1, source_target_pairs={{0,1},{1,0},{2,3},{3,2},{4,5},{5,4},{6,7},{7,6},{8,9},{9,8},{10,11... | collective-permute-start | bytes 2555912 | tf_op jit(solution)/shard_map/ppermute | solution.py:475
  139.2 3.6 %collective-permute-start.18 = (bf16[256,1664]{1,0:T(8,128)(2,1)S(1)}, bf16[256,1664]{1,0:T(8,128)(2,1)S(1)}, u32[]{:S(2)}, u32[]{:S(2)}) collective-permute-start(bf16[256,1664]{1,0:T(8,128)(2,1)S(1)} %give0.1), channel_id=1, source_target_pairs={{0,1},{1,0},{2,3},{3,2},{4,5},{5,4},{6,7},{7,6},{8,9},{9,8},{10,11... | collective-permute-start | bytes 2555912 | tf_op jit(solution)/shard_map/ppermute | solution.py:475
  144.2 30.8 %copy-start.1 = (f32[32,12800]{1,0:T(8,128)S(1)}, f32[32,12800]{1,0:T(8,128)}, u32[]{:S(2)}) copy-start(f32[32,12800]{1,0:T(8,128)} %get-tuple-element.41.hat_ref) | copy-start | bytes 4915204
  144.2 30.8 %copy-start.9 = (f32[12800]{0:T(1024)S(1)}, f32[12800]{0:T(1024)}, u32[]{:S(2)}) copy-start(f32[12800]{0:T(1024)} %gain_ref.3) | copy-start | bytes 153604
  144.2 30.8 %copy-start.10 = (f32[32,128]{1,0:T(8,128)S(1)}, f32[32,128]{1,0:T(8,128)}, u32[]{:S(2)}) copy-start(f32[32,128]{1,0:T(8,128)} %get-tuple-element.51.inv_ref) | copy-start | bytes 49156
  144.2 30.8 %all-to-all-start.2 = ((bf16[16,32,1664]{2,1,0:T(8,128)(2,1)}), bf16[16,32,1664]{2,1,0:T(8,128)(2,1)S(1)}, u32[]{:S(2)}, u32[]{:S(2)}) async-start(bf16[16,32,1664]{2,1,0:T(8,128)(2,1)} %join.1), calls=%async_computation.2 | async-start | bytes 3407872 | tf_op jit(solution)/shard_map/all_to_all | solution.py:488
  150.4 0.9 copy-start.5
  151.3 0.9 copy-start.7

commit v5 on v4

--- a/solution.py
+++ b/solution.py
@@ -29,57 +29,93 @@
     return jax.ShapeDtypeStruct(dims, dtype)
 
 
-def norm_kernel(chunk, order_ref, live_ref, spot_ref, rows_ref, gain_ref, bias_ref, out_ref):
-    step = pl.program_id(0)
-    wide = rows_ref[...].astype(F32)
-    centered = wide - jnp.mean(wide, axis=1, keepdims=True)
-    inv = lax.rsqrt(jnp.mean(centered * centered, axis=1, keepdims=True) + VISION_EPS)
+def run_order(slot_ref, units, section_slots, along):
+    slots = [slot_ref[u * UNIT] for u in range(units)]
+    alive = [slot >= 0 for slot in slots]
+    target = [jnp.maximum(slot, 0) // section_slots for slot in slots]
+    target = [t % along * 2 + t // along for t in target]
+    place = [jnp.where(a, t, -1) for a, t in zip(alive, target)]
+    taken = []
+    for spot in range(units):
+        hits = [jnp.where(p == spot, 1, 0) for p in place]
+        taken.append(functools.reduce(lambda a, b: a + b, hits))
+    dead_rank = jnp.int32(0)
+    for u in range(units):
+        free_rank = jnp.int32(0)
+        filler = jnp.int32(0)
+        for spot in range(units):
+            free = 1 - taken[spot]
+            filler = jnp.where((free > 0) & (free_rank == dead_rank), spot, filler)
+            free_rank = free_rank + free
+        place[u] = jnp.where(alive[u], place[u], filler)
+        dead_rank = dead_rank + jnp.where(alive[u], 0, 1)
+    return slots, alive, place
+
+
+def norm_kernel(
+    chunk, own_slots, section_slots, along, slot_ref, core_ref, rows_ref, gain_ref, bias_ref, out_ref, held, sems
+):
+    parts, high, padded = out_ref.shape
+    half = high // UNIT
+    units = 2 * half
+    slots, alive, place = run_order(slot_ref, units, section_slots, along)
+    notes = []
+    for i in range(half):
+        run, slot, live = jnp.int32(0), jnp.int32(0), jnp.int32(0)
+        for u in range(units):
+            here = place[u] == core_ref[0] * half + i
+            run = jnp.where(here, u, run)
+            slot = jnp.where(here, slots[u], slot)
+            live = jnp.where(here & alive[u], 1, live)
+        spot = jnp.where(live > 0, slot // UNIT % (own_slots // UNIT), 0)
+        notes.append((run, live, spot))
+    copies = []
+    for i, (run, _, _) in enumerate(notes):
+        rows = pl.ds(pl.multiple_of(run * UNIT, UNIT), UNIT)
+        copies.append(pltpu.make_async_copy(rows_ref.at[rows], held.at[i], sems.at[i]))
+        copies[i].start()
     gain, bias = gain_ref[...].reshape(1, -1), bias_ref[...].reshape(1, -1)
-    normed = (centered * inv * gain + bias).astype(BF)
-    parts, _, padded = out_ref.shape
     lane = lax.broadcasted_iota(jnp.int32, (UNIT, padded - chunk), 1)
-    note = jnp.where(lane == 0, order_ref[step], jnp.where(lane == 1, live_ref[step], spot_ref[step]))
-    note = note.astype(F32).astype(BF)
-    for k in range(parts):
-        at = (k % 2 * (parts // 2) + k // 2) * chunk
-        out_ref[k] = jnp.concatenate([normed[:, at : at + chunk], note], axis=1)
-
-
-def forward_kernel(core_ref, tile_ref, own_ref, other_ref, weight_ref, out_ref, window_ref, note_ref):
-    step = pl.program_id(0)
-    steps = pl.num_programs(0)
-
-    def work(ref):
-        sections, high, depth = ref.shape
-        at = pl.ds(pl.multiple_of(tile_ref[0] * LANES, LANES), window_ref.shape[2])
-        product = jnp.dot(
-            ref[...].reshape(sections * high, depth), weight_ref[...], preferred_element_type=F32
-        )
-        product = product.reshape(sections, high, product.shape[1])
-        for j in range(high // UNIT):
-            rows = product[:, j * UNIT : (j + 1) * UNIT].reshape(sections * UNIT, -1)
-            out_ref[j] = rows
-            run = slice(j * UNIT, (j + 1) * UNIT)
-            window_ref[j] = ref[:, run, at].reshape(sections * UNIT, -1)
-            heads = [ref[s, run, depth - LANES :][:1] for s in range(sections)]
-            note_ref[j] = jnp.concatenate([head.astype(F32) for head in heads], axis=0)
-
-    @pl.when(step < steps // 2)
-    def _():
-        work(own_ref)
-
-    @pl.when(step >= steps // 2)
-    def _():
-        work(other_ref)
-
-
-def tail_kernel(window_ref, weight_ref, main_ref, out_ref):
-    for target in range(out_ref.shape[0]):
-        product = jnp.dot(window_ref[target], weight_ref[...], preferred_element_type=F32)
-        out_ref[target] = (main_ref[target] + product).astype(BF)
-
-
-def prepare_kernel(text_ref, cot_ref, gain_ref, upstream_ref, stat_ref):
+    for i, (run, live, spot) in enumerate(notes):
+        copies[i].wait()
+        wide = held[i].astype(F32)
+        centered = wide - jnp.mean(wide, axis=1, keepdims=True)
+        inv = lax.rsqrt(jnp.mean(centered * centered, axis=1, keepdims=True) + VISION_EPS)
+        normed = (centered * inv * gain + bias).astype(BF)
+        note = jnp.where(lane == 0, run, jnp.where(lane == 1, live, spot)).astype(F32).astype(BF)
+        for k in range(parts):
+            at = (k % 2 * (parts // 2) + k // 2) * chunk
+            out_ref[k, i * UNIT : (i + 1) * UNIT] = jnp.concatenate(
+                [normed[:, at : at + chunk], note], axis=1
+            )
+
+
+def forward_kernel(tile_ref, rows_ref, weight_ref, out_ref, window_ref, note_ref):
+    sections, high, depth = rows_ref.shape
+    at = pl.ds(pl.multiple_of(tile_ref[0] * LANES, LANES), window_ref.shape[2])
+    product = jnp.dot(
+        rows_ref[...].reshape(sections * high, depth), weight_ref[...], preferred_element_type=F32
+    )
+    product = product.reshape(sections, high, product.shape[1])
+    for j in range(high // UNIT):
+        run = slice(j * UNIT, (j + 1) * UNIT)
+        out_ref[j] = product[:, run].reshape(sections * UNIT, -1)
+        window_ref[j] = rows_ref[:, run, at].reshape(sections * UNIT, -1)
+        heads = [rows_ref[s, run, depth - LANES :][:1] for s in range(sections)]
+        note_ref[j] = jnp.concatenate([head.astype(F32) for head in heads], axis=0)
+
+
+def tail_kernel(core_ref, own_window_ref, other_window_ref, weight_ref, own_ref, other_ref, out_ref):
+    half = own_ref.shape[0]
+    halves = ((core_ref[0], own_window_ref, own_ref), (1 - core_ref[0], other_window_ref, other_ref))
+    for side, window_ref, main_ref in halves:
+        for j in range(half):
+            product = jnp.dot(window_ref[j], weight_ref[...], preferred_element_type=F32)
+            out_ref[side * half + j] = (main_ref[j] + product).astype(BF)
+
+
+def prepare_kernel(before_ref, text_ref, cot_ref, gain_ref, upstream_ref, stat_ref):
+    del before_ref
     upstream_ref[...] = cot_ref[...].astype(F32) * gain_ref[...]
     text = text_ref[...].astype(F32)
     square = jnp.sum(text * text, axis=1, keepdims=True)
@@ -196,10 +232,6 @@
     out_ref[...] = (inv * (weighted - weighted_mean - hat * cross)).astype(BF)
 
 
-def after_kernel(array_ref, before_ref, out_ref):
-    del array_ref, before_ref, out_ref
-
-
 def ring_gather(block, rows, beside):
     groups = lax.axis_size("dp")
     me = lax.axis_index("dp")
@@ -212,19 +244,18 @@
         return lax.dynamic_update_slice_in_dim(out, piece, owner % groups * height, 0)
 
     out = put(out, block, me)
-    rising = falling = rising_once = block
+    rising = falling = block
     for hop in range(1, (groups - 1) // 2 + 1):
         rising = lax.ppermute(rising, "dp", up)
         falling = lax.ppermute(falling, "dp", down)
         out, rising, falling = lax.optimization_barrier((out, rising, falling))
         if hop == 1:
             rising, falling, beside = lax.optimization_barrier((rising, falling, beside))
-            rising_once = rising
         out = put(out, rising, me - hop + groups)
         out = put(out, falling, me + hop)
     last = lax.ppermute(rising, "dp", up)
     owner = (me + groups // 2) % groups
-    return out, last, owner * height, rising, falling, rising_once, beside
+    return out, last, owner * height, rising, falling, beside
 
 
 def fill_places(wanted, alive, places):
@@ -264,97 +295,77 @@
 
     text_gain_row = text_gain.reshape(1, columns)
 
-    unit_slot = slot_of_row.reshape(units, UNIT)[:, 0]
-    alive = unit_slot >= 0
-    safe = jnp.where(alive, unit_slot, 0)
-    target = safe // (slots * groups)
-    target = target % along * 2 + target // along
-    order = inverse(fill_places(target, alive, places), places)
     half = units // 2
-    own = lax.dynamic_slice_in_dim(order, core * half, half)
-    chosen = own[:, None] == places
-    live = jnp.sum(jnp.where(chosen, alive, 0), axis=1).astype(jnp.int32)
-    spot = jnp.sum(jnp.where(chosen, safe // UNIT % (slots // UNIT), 0), axis=1).astype(jnp.int32)
+    core_index = core.reshape(1).astype(jnp.int32)
     sent = pl.pallas_call(
-        functools.partial(norm_kernel, chunk),
+        functools.partial(norm_kernel, chunk, slots, slots * groups, along),
         out_shape=pltpu.HBM((sections, half * UNIT, padded), BF),
-        grid_spec=pltpu.PrefetchScalarGridSpec(
-            num_scalar_prefetch=3,
-            grid=(half,),
-            in_specs=[
-                pl.BlockSpec((UNIT, depth), lambda i, order, live, spot: (order[i], 0)),
-                pl.BlockSpec((depth,), lambda i, order, live, spot: (0,)),
-                pl.BlockSpec((depth,), lambda i, order, live, spot: (0,)),
-            ],
-            out_specs=pl.BlockSpec(
-                (sections, UNIT, padded), lambda i, order, live, spot: (0, i, 0)
-            ),
-        ),
+        in_specs=[SMEM, SMEM, ANY, VMEM, VMEM],
+        out_specs=VMEM,
+        scratch_shapes=[pltpu.VMEM((half, UNIT, depth), BF), pltpu.SemaphoreType.DMA((half,))],
         compiler_params=WIDE,
         cost_estimate=FREE,
         name="vision_norm",
-    )(own, live, spot, vision_rows, vision_gain, vision_bias)
-    early_weight, last, last_row, rising, falling, rising_once, sent = ring_gather(proj_weight, padded, sent)
-    sent = pl.pallas_call(
-        after_kernel,
-        out_shape=pltpu.HBM(sent.shape, sent.dtype),
-        in_specs=[ANY, ANY],
-        out_specs=ANY,
-        input_output_aliases={0: 0},
-        cost_estimate=FREE,
-        name="after",
-    )(sent, rising_once)
+    )(slot_of_row, core_index, vision_rows, vision_gain, vision_bias)
+    early_weight, last, last_row, rising, falling, sent = ring_gather(proj_weight, padded, sent)
     from_own = lax.all_to_all(sent, along_first, 0, 0, tiled=True)
     from_own, *_ = lax.optimization_barrier((from_own, rising, falling))
     from_other = lax.ppermute(from_own, "core", swap_core)
 
     pair = 2 * UNIT
-    spread = lambda i, *_: ((i + _[0][0] * (half // 2)) % half, 0, 0)
-    sides = [
-        pl.BlockSpec((sections, pair, padded), lambda i, *_: (0, jnp.minimum(i, half // 2 - 1), 0)),
-        pl.BlockSpec((sections, pair, padded), lambda i, *_: (0, jnp.maximum(i - half // 2, 0), 0)),
-    ]
-    core_index = core.reshape(1).astype(jnp.int32)
     height = last.shape[0]
     window = -(-(height + LANES - 8) // LANES) * LANES
     tile = jnp.minimum(last_row // LANES, (padded - window) // LANES).astype(jnp.int32)
-    main, x_window, table = pl.pallas_call(
-        forward_kernel,
-        out_shape=(
-            shape((units, sections * UNIT, columns), F32),
-            shape((units, sections * UNIT, window), BF),
-            shape((units, sections, LANES), F32),
-        ),
-        grid_spec=pltpu.PrefetchScalarGridSpec(
-            num_scalar_prefetch=2,
-            grid=(half,),
-            in_specs=sides + [pl.BlockSpec((padded, columns), lambda i, *_: (0, 0))],
-            out_specs=(
-                pl.BlockSpec((2, sections * UNIT, columns), spread),
-                pl.BlockSpec((2, sections * UNIT, window), spread),
-                pl.BlockSpec((2, sections, LANES), spread),
+
+    def forward(rows, name):
+        return pl.pallas_call(
+            forward_kernel,
+            out_shape=(
+                shape((half, sections * UNIT, columns), F32),
+                shape((half, sections * UNIT, window), BF),
+                shape((half, sections, LANES), F32),
             ),
-        ),
-        compiler_params=PARAMS,
-        cost_estimate=FREE,
-        name="forward",
-    )(core_index, tile.reshape(1), from_own, from_other, early_weight)
+            grid_spec=pltpu.PrefetchScalarGridSpec(
+                num_scalar_prefetch=1,
+                grid=(half // 2,),
+                in_specs=[
+                    pl.BlockSpec((sections, pair, padded), lambda i, tile: (0, i, 0)),
+                    pl.BlockSpec((padded, columns), lambda i, tile: (0, 0)),
+                ],
+                out_specs=(
+                    pl.BlockSpec((2, sections * UNIT, columns), lambda i, tile: (i, 0, 0)),
+                    pl.BlockSpec((2, sections * UNIT, window), lambda i, tile: (i, 0, 0)),
+                    pl.BlockSpec((2, sections, LANES), lambda i, tile: (i, 0, 0)),
+                ),
+            ),
+            compiler_params=PARAMS,
+            cost_estimate=FREE,
+            name=name,
+        )(tile.reshape(1), rows, early_weight)
+
+    own_main, own_window, own_notes = forward(from_own, "forward_own")
+    other_main, other_window, other_notes = forward(from_other, "forward_other")
     last_window = lax.dynamic_update_slice_in_dim(
         jnp.zeros((window, columns), BF), last, last_row - tile * LANES, 0
     )
     partial = pl.pallas_call(
         tail_kernel,
         out_shape=pltpu.HBM((units, sections * UNIT, columns), BF),
-        in_specs=[VMEM, VMEM, VMEM],
+        in_specs=[SMEM] + [VMEM] * 5,
         out_specs=VMEM,
         compiler_params=PARAMS,
         cost_estimate=FREE,
         name="tail",
-    )(x_window, last_window, main)
+    )(core_index, own_window, other_window, last_window, own_main, other_main)
     partial = lax.all_to_all(partial, along_first, 0, 0, tiled=True)
     weight = lax.dynamic_update_slice_in_dim(early_weight, last, last_row, 0)
 
     at = LANES - (padded - chunk)
+    table = jnp.where(
+        core == 0,
+        jnp.concatenate([own_notes, other_notes]),
+        jnp.concatenate([other_notes, own_notes]),
+    )
     table = jnp.swapaxes(table[:, :, at : at + 3], 0, 1).astype(jnp.int32)
     here = lax.dynamic_slice_in_dim(table, section, 1, 1)[:, 0]
     has = here[:, 1] > 0
@@ -391,12 +402,12 @@
     upstream, text_stat = pl.pallas_call(
         prepare_kernel,
         out_shape=(shape((slots, columns), F32), shape((8, LANES), F32)),
-        in_specs=[VMEM] * 3,
+        in_specs=[ANY] + [VMEM] * 3,
         out_specs=(VMEM, VMEM),
         compiler_params=PARAMS,
         cost_estimate=FREE,
         name="prepare",
-    )(text_rows, out_cotangent, text_gain_row)
+    )(hat_inv, text_rows, out_cotangent, text_gain_row)
     feature, slope, stat = pl.pallas_call(
         slots_kernel,
         out_shape=(
@@ -409,7 +420,7 @@
         compiler_params=PARAMS,
         cost_estimate=FREE,
         name="slots",
-    )(where, pick, hat, partial, upstream, text_stat)
+    )(where, pick, hat_inv, partial, upstream, text_stat)
     stats = [stat] + [
         lax.ppermute(stat, ("y_hi", "core"), [(i, i ^ turn) for i in range(tensors)])
         for turn in range(1, tensors)

time: 178 us -> 176 us (0.989)
  other arithmetic: 3.57 us -> 1.1 us
    all_to_all x1, waiting for transfers between devices: 25 us -> 20.9 us  [shards(): partial = lax.all_to_all(partial, along_first, 0, 0, tiled=True)]
    ppermute x3, waiting for transfers between devices: 11.9 us -> 15.3 us  [ring_gather(): rising = lax.ppermute(rising, 'dp', up)]
    unnamed x31 -> x36, local copies, waits for them, and re-layouts: 6.78 us -> 8.54 us
  transfers between devices with their start and end apart: 23 -> 23, of which waited for: 15 -> 15; matrix products, arithmetic and copies ran while one was open for 7% -> 5% of each run, Pallas kernels for 11% -> 11%
where the time goes in v5:
time: 176 us; the launch traced here: 175 us
  waiting for transfers between devices  76.2 us (43%)
  starting transfers between devices  48.4 us (28%)
  Pallas kernels  31.8 us (18%)
  local copies, waits for them, and re-layouts  16.7 us (9%)
    all_to_all x1, waiting for transfers between devices, shards(): partial = lax.all_to_all(partial, along_first, 0, 0, tiled=True)  20.9 us
    all_to_all x1, waiting for transfers between devices, shards(): back = lax.all_to_all(total, ('x', 'y_hi', 'y_lo'), 0, 0, tiled=True)  20.6 us
    ppermute x3, waiting for transfers between devices, ring_gather(): rising = lax.ppermute(rising, 'dp', up)  15.3 us
    ppermute x7, waiting for transfers between devices, turn(): return lax.ppermute(block, ('y_lo', 'x'), moves)  12 us
    ppermute x7, starting transfers between devices, turn(): return lax.ppermute(block, ('y_lo', 'x'), moves)  11.3 us
    ppermute x3, starting transfers between devices, ring_gather(): falling = lax.ppermute(falling, 'dp', down)  8.68 us
    unnamed x36, local copies, waits for them, and re-layouts  8.54 us
    pallas_call x2, Pallas kernels, forward(): pl.pallas_call(forward_kernel, out_shape=(shape((half, sections * UNIT, c...  6.85 us
  transfers between devices with their start and end apart: 23, of which 15 were waited for; matrix products, arithmetic and copies ran while one was open for 5% of the time, Pallas kernels for 11%

profile of v5, /device:TPU:8, one launch (start us, length us, event | category | flops | bytes accessed | tf_op | source)
XLA Modules:
  0.0 175.2 jit_solution(4514113429125633208)
XLA Ops:
  0.6 2.0 %collective-permute-start = (bf16[200,1024]{1,0:T(8,128)(2,1)}, bf16[200,1024]{1,0:T(8,128)(2,1)}, u32[]{:S(2)}, u32[]{:S(2)}) collective-permute-start(bf16[200,1024]{1,0:T(8,128)(2,1)} %param.13), channel_id=1, source_target_pairs={{0,4},{4,8},{8,12},{12,16},{16,20},{20,24},{24,28},{28,0},{1,5},{5... | collective-permute-start | bytes 1228808 | tf_op jit(solution)/shard_map/ppermute | solution.py:249
  2.6 4.0 %collective-permute-start.1 = (bf16[200,1024]{1,0:T(8,128)(2,1)}, bf16[200,1024]{1,0:T(8,128)(2,1)}, u32[]{:S(2)}, u32[]{:S(2)}) collective-permute-start(bf16[200,1024]{1,0:T(8,128)(2,1)} %param.13), channel_id=1, source_target_pairs={{0,28},{4,0},{8,4},{12,8},{16,12},{20,16},{24,20},{28,24},{1,29},{... | collective-permute-start | bytes 1228808 | tf_op jit(solution)/shard_map/ppermute | solution.py:250
  6.7 5.6 %vision_norm.1 = bf16[8,64,1664]{2,1,0:T(8,128)(2,1)} custom-call(s32[128]{0:T(128)} %slot_ref.1, s32[1]{0:T(128)} %bitcast.1.core_ref, bf16[128,12800]{1,0:T(8,128)(2,1)} %rows_ref.3, f32[12800]{0:T(1024)} %gain_ref.3, f32[12800]{0:T(1024)} %bias_ref.1), custom_call_target="tpu_custom_call" | custom-call | tf_op jit(solution)/shard_map/vision_norm/pallas_call | solution.py:300
  12.3 0.4 broadcast_in_dim.45
  12.8 3.6 %collective-permute-done = bf16[200,1024]{1,0:T(8,128)(2,1)} collective-permute-done((bf16[200,1024]{1,0:T(8,128)(2,1)}, bf16[200,1024]{1,0:T(8,128)(2,1)}, u32[]{:S(2)}, u32[]{:S(2)}) %collective-permute-start) | collective-permute-done | bytes 409632 | tf_op jit(solution)/shard_map/ppermute | solution.py:249
  16.3 5.8 %all-to-all-start = ((bf16[8,64,1664]{2,1,0:T(8,128)(2,1)}), bf16[8,64,1664]{2,1,0:T(8,128)(2,1)}, u32[]{:S(2)}, u32[]{:S(2)}) async-start(bf16[8,64,1664]{2,1,0:T(8,128)(2,1)} %vision_norm.1), calls=%async_computation | async-start | bytes 3407872 | tf_op jit(solution)/shard_map/all_to_all | solution.py:311
  22.1 3.2 %collective-permute-start.3 = (bf16[200,1024]{1,0:T(8,128)(2,1)}, bf16[200,1024]{1,0:T(8,128)(2,1)}, u32[]{:S(2)}, u32[]{:S(2)}) collective-permute-start(bf16[200,1024]{1,0:T(8,128)(2,1)} %collective-permute-done.1), channel_id=1, source_target_pairs={{0,28},{4,0},{8,4},{12,8},{16,12},{20,16},{24,20},{28,24},{1,29},{... | collective-permute-start | bytes 1228808 | tf_op jit(solution)/shard_map/ppermute | solution.py:250
  25.3 1.0 constant_dynamic-update-slice_fusion.7
  26.4 1.0 constant_dynamic-update-slice_fusion.6
  27.4 6.3 %collective-permute-done.2 = bf16[200,1024]{1,0:T(8,128)(2,1)} collective-permute-done((bf16[200,1024]{1,0:T(8,128)(2,1)}, bf16[200,1024]{1,0:T(8,128)(2,1)}, u32[]{:S(2)}, u32[]{:S(2)}) %collective-permute-start.2) | collective-permute-done | bytes 409632 | tf_op jit(solution)/shard_map/ppermute | solution.py:249
  33.7 1.8 %collective-permute-start.4 = (bf16[200,1024]{1,0:T(8,128)(2,1)}, bf16[200,1024]{1,0:T(8,128)(2,1)}, u32[]{:S(2)}, u32[]{:S(2)}) collective-permute-start(bf16[200,1024]{1,0:T(8,128)(2,1)} %collective-permute-done.2), channel_id=1, source_target_pairs={{0,4},{4,8},{8,12},{12,16},{16,20},{20,24},{24,28},{28,0},{1,5},{5... | collective-permute-start | bytes 1228808 | tf_op jit(solution)/shard_map/ppermute | solution.py:249
  35.5 1.4 collective-permute-start.5
  37.0 1.0 constant_dynamic-update-slice_fusion.5
  38.0 1.0 constant_dynamic-update-slice_fusion.4
  39.0 5.4 %collective-permute-done.4 = bf16[200,1024]{1,0:T(8,128)(2,1)} collective-permute-done((bf16[200,1024]{1,0:T(8,128)(2,1)}, bf16[200,1024]{1,0:T(8,128)(2,1)}, u32[]{:S(2)}, u32[]{:S(2)}) %collective-permute-start.4) | collective-permute-done | bytes 409632 | tf_op jit(solution)/shard_map/ppermute | solution.py:249
  44.8 1.5 collective-permute-start.7
  46.3 1.0 constant_dynamic-update-slice_fusion.3
  47.4 1.0 constant_dynamic-update-slice_fusion.2.weight_ref
  48.4 3.4 %forward_own.1 = (f32[4,128,1024]{2,1,0:T(8,128)S(1)}, bf16[4,128,384]{2,1,0:T(8,128)(2,1)S(1)}, f32[4,8,128]{2,1,0:T(8,128)S(1)}) custom-call(s32[1]{0:T(128)} %bitcast.tile_ref, bf16[8,64,1664]{2,1,0:T(8,128)(2,1)} %all-to-all-done.rows_ref, bf16[1664,1024]{1,0:T(8,128)(2,1)S(1)} %constant_dynamic-update-slice_fusion.2.weight_ref), custom_call_target="tpu_custom_call" | custom-call | tf_op jit(solution)/shard_map/forward_own/pallas_call | solution.py:321
  51.9 3.4 %forward_other.1 = (f32[4,128,1024]{2,1,0:T(8,128)S(1)}, bf16[4,128,384]{2,1,0:T(8,128)(2,1)S(1)}, f32[4,8,128]{2,1,0:T(8,128)S(1)}) custom-call(s32[1]{0:T(128)} %bitcast.tile_ref, bf16[8,64,1664]{2,1,0:T(8,128)(2,1)} %collective-permute-done.6.rows_ref, bf16[1664,1024]{1,0:T(8,128)(2,1)S(1)} %constant_dynamic-update-slice_fusion.2.weight_ref), custom_call_target="tpu_custom_call" | custom-call | tf_op jit(solution)/shard_map/forward_other/pallas_call | solution.py:321
  55.3 2.8 %collective-permute-done.7 = bf16[200,1024]{1,0:T(8,128)(2,1)S(1)} collective-permute-done((bf16[200,1024]{1,0:T(8,128)(2,1)}, bf16[200,1024]{1,0:T(8,128)(2,1)S(1)}, u32[]{:S(2)}, u32[]{:S(2)}) %collective-permute-start.7) | collective-permute-done | bytes 409632 | tf_op jit(solution)/shard_map/ppermute | solution.py:256
  58.2 2.6 %tail.1 = bf16[8,128,1024]{2,1,0:T(8,128)(2,1)} custom-call(s32[1]{0:T(128)} %bitcast.1.core_ref, bf16[4,128,384]{2,1,0:T(8,128)(2,1)S(1)} %get-tuple-element.46.own_window_ref, bf16[4,128,384]{2,1,0:T(8,128)(2,1)S(1)} %get-tuple-element.47.other_window_ref, bf16[384,1024]{1,0:T(8,128)(2,1)S(1)} %get-tuple-element.59.weight_ref, ...), custom_call_target="tpu_custom_call" | custom-call | tf_op jit(solution)/shard_map/tail/pallas_call | solution.py:351
  60.8 6.8 %all-to-all-start.1 = ((bf16[8,128,1024]{2,1,0:T(8,128)(2,1)}), bf16[8,128,1024]{2,1,0:T(8,128)(2,1)}, u32[]{:S(2)}, u32[]{:S(2)}) async-start(bf16[8,128,1024]{2,1,0:T(8,128)(2,1)} %tail.1), calls=%async_computation.1 | async-start | bytes 4194304 | tf_op jit(solution)/shard_map/all_to_all | solution.py:360
  67.9 0.4 copy-done.15
  68.3 2.8 %vision_hat.1 = (f32[32,12800]{1,0:T(8,128)}, f32[32,128]{1,0:T(8,128)}) custom-call(s32[1]{0:T(128)} %bitcast.9.first_ref, s32[8,8,3]{2,1,0:T(8,128)} %bitcast.25, bf16[128,12800]{1,0:T(8,128)(2,1)} %rows_ref.3), custom_call_target="tpu_custom_call" | custom-call | tf_op jit(solution)/shard_map/vision_hat/pallas_call | solution.py:386
  71.4 0.8 constant_dynamic-slice_fusion
  72.7 0.9 copy-done.4
  73.7 0.9 copy-done.8
  74.6 0.7 copy-done.10
  75.5 0.8 copy-done
  76.5 20.9 %all-to-all-done.1.parts_ref = bf16[8,128,1024]{2,1,0:T(8,128)(2,1)} async-done(((bf16[8,128,1024]{2,1,0:T(8,128)(2,1)}), bf16[8,128,1024]{2,1,0:T(8,128)(2,1)}, u32[]{:S(2)}, u32[]{:S(2)}) %all-to-all-start.1) | async-done | bytes 2097184 | tf_op jit(solution)/shard_map/all_to_all | solution.py:360
  97.4 1.0 copy-done.1
  98.5 0.7 copy-done.11
  99.2 2.2 %slots.1 = (bf16[128,1024]{1,0:T(8,128)(2,1)S(1)}, f32[128,1024]{1,0:T(8,128)S(1)}, f32[8,128]{1,0:T(8,128)S(1)}) custom-call(s32[8]{0:T(128)S(1)} %fusion.9.place_ref, s32[64]{0:T(128)S(1)} %fusion.4.pick_ref, f32[32,128]{1,0:T(8,128)S(1)} %copy-done.11, bf16[8,128,1024]{2,1,0:T(8,128)(2,1)} %all-to-all-done.1.parts_ref, f32[128,1024]{1,0:T(8,128)S(1)} %copy-done.1, ...), custom_call_target="tpu_custom_call" | custom-call | tf_op jit(solution)/shard_map/slots/pallas_call | solution.py:411
  101.4 0.9 collective-permute-start.10
  102.3 1.6 collective-permute-start.8
  103.9 1.2 collective-permute-start.9
  105.1 0.9 collective-permute-done.10.refs_3_
  106.0 3.0 %collective-permute-done.9.refs_2_ = f32[8,128]{1,0:T(8,128)S(1)} collective-permute-done((f32[8,128]{1,0:T(8,128)S(1)}, f32[8,128]{1,0:T(8,128)S(1)}, u32[]{:S(2)}, u32[]{:S(2)}) %collective-permute-start.9) | collective-permute-done | bytes 4128 | tf_op jit(solution)/shard_map/ppermute | solution.py:425
  109.0 1.0 copy-done.2
  110.1 0.9 grads.1.refs_0_
  110.9 2.5 %collective-permute-start.11 = (bf16[8,16,1024]{2,1,0:T(8,128)(2,1)S(1)}, bf16[8,16,1024]{2,1,0:T(8,128)(2,1)S(1)}, u32[]{:S(2)}, u32[]{:S(2)}) collective-permute-start(bf16[8,16,1024]{2,1,0:T(8,128)(2,1)S(1)} %grads.1.refs_0_), channel_id=1, source_target_pairs={{0,128},{32,160},{64,192},{96,224},{128,0},{160,32},{192,64},{224,... | collective-permute-start | bytes 786440 | tf_op jit(solution)/shard_map/ppermute | solution.py:441
  113.4 3.2 %collective-permute-start.13 = (bf16[8,16,1024]{2,1,0:T(8,128)(2,1)S(1)}, bf16[8,16,1024]{2,1,0:T(8,128)(2,1)S(1)}, u32[]{:S(2)}, u32[]{:S(2)}) collective-permute-start(bf16[8,16,1024]{2,1,0:T(8,128)(2,1)S(1)} %grads.1.refs_0_), channel_id=1, source_target_pairs={{0,96},{32,0},{64,32},{96,64},{128,224},{160,128},{192,160},{224,1... | collective-permute-start | bytes 786440 | tf_op jit(solution)/shard_map/ppermute | solution.py:441
  116.7 2.1 %collective-permute-done.11.refs_1_ = bf16[8,16,1024]{2,1,0:T(8,128)(2,1)S(1)} collective-permute-done((bf16[8,16,1024]{2,1,0:T(8,128)(2,1)S(1)}, bf16[8,16,1024]{2,1,0:T(8,128)(2,1)S(1)}, u32[]{:S(2)}, u32[]{:S(2)}) %collective-permute-start.11) | collective-permute-done | bytes 262176 | tf_op jit(solution)/shard_map/ppermute | solution.py:441
  118.8 2.7 %collective-permute-done.12.refs_2_ = bf16[8,16,1024]{2,1,0:T(8,128)(2,1)S(1)} collective-permute-done((bf16[8,16,1024]{2,1,0:T(8,128)(2,1)S(1)}, bf16[8,16,1024]{2,1,0:T(8,128)(2,1)S(1)}, u32[]{:S(2)}, u32[]{:S(2)}) %collective-permute-start.12) | collective-permute-done | bytes 262176 | tf_op jit(solution)/shard_map/ppermute | solution.py:441
  121.4 2.0 %collective-permute-done.13.refs_4_ = bf16[8,16,1024]{2,1,0:T(8,128)(2,1)S(1)} collective-permute-done((bf16[8,16,1024]{2,1,0:T(8,128)(2,1)S(1)}, bf16[8,16,1024]{2,1,0:T(8,128)(2,1)S(1)}, u32[]{:S(2)}, u32[]{:S(2)}) %collective-permute-start.13) | collective-permute-done | bytes 262176 | tf_op jit(solution)/shard_map/ppermute | solution.py:441
  123.4 1.9 %collective-permute-start.14 = (bf16[8,16,1024]{2,1,0:T(8,128)(2,1)S(1)}, bf16[8,16,1024]{2,1,0:T(8,128)(2,1)S(1)}, u32[]{:S(2)}, u32[]{:S(2)}) collective-permute-start(bf16[8,16,1024]{2,1,0:T(8,128)(2,1)S(1)} %collective-permute-done.11.refs_1_), channel_id=1, source_target_pairs={{0,32},{32,64},{64,96},{96,0},{128,160},{160,192},{192,224},{224,1... | collective-permute-start | bytes 786440 | tf_op jit(solution)/shard_map/ppermute | solution.py:441
  125.3 1.0 collective-permute-done.15.refs_5_
  126.3 3.7 %collective-permute-start.17 = (bf16[8,16,1024]{2,1,0:T(8,128)(2,1)S(1)}, bf16[8,16,1024]{2,1,0:T(8,128)(2,1)S(1)}, u32[]{:S(2)}, u32[]{:S(2)}) collective-permute-start(bf16[8,16,1024]{2,1,0:T(8,128)(2,1)S(1)} %collective-permute-done.15.refs_5_), channel_id=1, source_target_pairs={{0,96},{32,0},{64,32},{96,64},{128,224},{160,128},{192,160},{224,1... | collective-permute-start | bytes 786440 | tf_op jit(solution)/shard_map/ppermute | solution.py:441
  130.0 1.5 collective-permute-done.16.refs_6_
  131.5 2.8 %collective-permute-done.14.refs_3_ = bf16[8,16,1024]{2,1,0:T(8,128)(2,1)S(1)} collective-permute-done((bf16[8,16,1024]{2,1,0:T(8,128)(2,1)S(1)}, bf16[8,16,1024]{2,1,0:T(8,128)(2,1)S(1)}, u32[]{:S(2)}, u32[]{:S(2)}) %collective-permute-start.14) | collective-permute-done | bytes 262176 | tf_op jit(solution)/shard_map/ppermute | solution.py:441
  134.3 0.7 arrange.1.grads_ref
  135.0 1.1 give1.1
  136.2 1.1 give0.1
  137.4 0.5 collective-permute-start.18
  137.9 2.3 %keep.1.own_ref = f32[512,1664]{1,0:T(8,128)S(1)} custom-call(bf16[64,16,1024]{2,1,0:T(8,128)(2,1)S(1)} %arrange.1.grads_ref, bf16[1664,1024]{1,0:T(8,128)(2,1)S(1)} %get-tuple-element.58.weight_ref), custom_call_target="tpu_custom_call" | custom-call | tf_op jit(solution)/shard_map/keep/pallas_call | solution.py:471
  140.2 0.8 collective-permute-done.18.low_ref
  141.0 1.4 join.1
  142.4 6.2 %all-to-all-start.2 = ((bf16[16,32,1664]{2,1,0:T(8,128)(2,1)}), bf16[16,32,1664]{2,1,0:T(8,128)(2,1)S(1)}, u32[]{:S(2)}, u32[]{:S(2)}) async-start(bf16[16,32,1664]{2,1,0:T(8,128)(2,1)} %join.1), calls=%async_computation.2 | async-start | bytes 3407872 | tf_op jit(solution)/shard_map/all_to_all | solution.py:499
  148.6 0.9 copy-done.5
  149.5 0.9 copy-done.7
  150.5 2.1 %normed.1 = bf16[128,1024]{1,0:T(8,128)(2,1)} custom-call(s32[8]{0:T(128)S(1)} %fusion.9.place_ref, s32[8]{0:T(128)S(1)} %get-tuple-element.60.live_ref, bf16[128,1024]{1,0:T(8,128)(2,1)S(1)} %copy-done.5, bf16[128,1024]{1,0:T(8,128)(2,1)S(1)} %copy-done.7, f32[1,1024]{1,0:T(1,128)S(1)} %bitcast.23, f32[8,128]{1,0:T(8,128)S(1)} %get-tuple-element.53.refs_0_, ...), custom_call_target="tpu_custom_call" | custom-call | tf_op jit(solution)/shard_map/normed/pallas_call | solution.py:457
  152.5 20.6 %all-to-all-done.2.parts_ref = bf16[16,32,1664]{2,1,0:T(8,128)(2,1)S(1)} async-done(((bf16[16,32,1664]{2,1,0:T(8,128)(2,1)}), bf16[16,32,1664]{2,1,0:T(8,128)(2,1)S(1)}, u32[]{:S(2)}, u32[]{:S(2)}) %all-to-all-start.2) | async-done | bytes 1703968 | tf_op jit(solution)/shard_map/all_to_all | solution.py:499
  173.2 2.0 %vision_back.1 = bf16[32,12800]{1,0:T(8,128)(2,1)} custom-call(bf16[16,32,1664]{2,1,0:T(8,128)(2,1)S(1)} %all-to-all-done.2.parts_ref, f32[32,12800]{1,0:T(8,128)S(1)} %copy-done.3, f32[32,128]{1,0:T(8,128)S(1)} %copy-done.12, f32[12800]{0:T(1024)S(1)} %copy-done.9), custom_call_target="tpu_custom_call" | custom-call | tf_op jit(solution)/shard_map/vision_back/pallas_call | solution.py:504
  (68 shorter events, 2.2 us)
Async XLA Ops:
  0.6 15.7 %collective-permute-start = (bf16[200,1024]{1,0:T(8,128)(2,1)}, bf16[200,1024]{1,0:T(8,128)(2,1)}, u32[]{:S(2)}, u32[]{:S(2)}) collective-permute-start(bf16[200,1024]{1,0:T(8,128)(2,1)} %param.13), channel_id=1, source_target_pairs={{0,4},{4,8},{8,12},{12,16},{16,20},{20,24},{24,28},{28,0},{1,5},{5... | collective-permute-start | bytes 1228808 | tf_op jit(solution)/shard_map/ppermute | solution.py:249
  2.6 13.7 %collective-permute-start.1 = (bf16[200,1024]{1,0:T(8,128)(2,1)}, bf16[200,1024]{1,0:T(8,128)(2,1)}, u32[]{:S(2)}, u32[]{:S(2)}) collective-permute-start(bf16[200,1024]{1,0:T(8,128)(2,1)} %param.13), channel_id=1, source_target_pairs={{0,28},{4,0},{8,4},{12,8},{16,12},{20,16},{24,20},{28,24},{1,29},{... | collective-permute-start | bytes 1228808 | tf_op jit(solution)/shard_map/ppermute | solution.py:250
  6.7 6.1 %copy-start.14 = (bf16[200,1024]{1,0:T(8,128)(2,1)S(1)}, bf16[200,1024]{1,0:T(8,128)(2,1)}, u32[]{:S(2)}) copy-start(bf16[200,1024]{1,0:T(8,128)(2,1)} %param.13) | copy-start | bytes 1228804
  12.8 32.0 %copy-start.16 = (s32[8]{0:T(128)S(1)}, s32[8]{0:T(128)}, u32[]{:S(2)}) copy-start(s32[8]{0:T(128)} %constant.190.clone) | copy-start | bytes 100
  12.8 31.9 %copy-start.17 = (s32[8]{0:T(128)S(1)}, s32[8]{0:T(128)}, u32[]{:S(2)}) copy-start(s32[8]{0:T(128)} %constant.192) | copy-start | bytes 100
  16.3 28.1 %all-to-all-start = ((bf16[8,64,1664]{2,1,0:T(8,128)(2,1)}), bf16[8,64,1664]{2,1,0:T(8,128)(2,1)}, u32[]{:S(2)}, u32[]{:S(2)}) async-start(bf16[8,64,1664]{2,1,0:T(8,128)(2,1)} %vision_norm.1), calls=%async_computation | async-start | bytes 3407872 | tf_op jit(solution)/shard_map/all_to_all | solution.py:311
  22.1 11.6 %collective-permute-start.2 = (bf16[200,1024]{1,0:T(8,128)(2,1)}, bf16[200,1024]{1,0:T(8,128)(2,1)}, u32[]{:S(2)}, u32[]{:S(2)}) collective-permute-start(bf16[200,1024]{1,0:T(8,128)(2,1)} %collective-permute-done), channel_id=1, source_target_pairs={{0,4},{4,8},{8,12},{12,16},{16,20},{20,24},{24,28},{28,0},{1,5},{5... | collective-permute-start | bytes 1228808 | tf_op jit(solution)/shard_map/ppermute | solution.py:249
  22.1 11.6 %collective-permute-start.3 = (bf16[200,1024]{1,0:T(8,128)(2,1)}, bf16[200,1024]{1,0:T(8,128)(2,1)}, u32[]{:S(2)}, u32[]{:S(2)}) collective-permute-start(bf16[200,1024]{1,0:T(8,128)(2,1)} %collective-permute-done.1), channel_id=1, source_target_pairs={{0,28},{4,0},{8,4},{12,8},{16,12},{20,16},{24,20},{28,24},{1,29},{... | collective-permute-start | bytes 1228808 | tf_op jit(solution)/shard_map/ppermute | solution.py:250
  33.7 10.7 %collective-permute-start.4 = (bf16[200,1024]{1,0:T(8,128)(2,1)}, bf16[200,1024]{1,0:T(8,128)(2,1)}, u32[]{:S(2)}, u32[]{:S(2)}) collective-permute-start(bf16[200,1024]{1,0:T(8,128)(2,1)} %collective-permute-done.2), channel_id=1, source_target_pairs={{0,4},{4,8},{8,12},{12,16},{16,20},{20,24},{24,28},{28,0},{1,5},{5... | collective-permute-start | bytes 1228808 | tf_op jit(solution)/shard_map/ppermute | solution.py:249
  35.5 8.9 %collective-permute-start.5 = (bf16[200,1024]{1,0:T(8,128)(2,1)}, bf16[200,1024]{1,0:T(8,128)(2,1)}, u32[]{:S(2)}, u32[]{:S(2)}) collective-permute-start(bf16[200,1024]{1,0:T(8,128)(2,1)} %collective-permute-done.3), channel_id=1, source_target_pairs={{0,28},{4,0},{8,4},{12,8},{16,12},{20,16},{24,20},{28,24},{1,29},{... | collective-permute-start | bytes 1228808 | tf_op jit(solution)/shard_map/ppermute | solution.py:250
  44.4 7.4 %collective-permute-start.6 = (bf16[8,64,1664]{2,1,0:T(8,128)(2,1)}, bf16[8,64,1664]{2,1,0:T(8,128)(2,1)}, u32[]{:S(2)}, u32[]{:S(2)}) collective-permute-start(bf16[8,64,1664]{2,1,0:T(8,128)(2,1)} %all-to-all-done.rows_ref), channel_id=1, source_target_pairs={{0,1},{1,0},{2,3},{3,2},{4,5},{5,4},{6,7},{7,6},{8,9},{9,8},{10,11... | collective-permute-start | bytes 5111816 | tf_op jit(solution)/shard_map/ppermute | solution.py:313
  44.8 13.3 %collective-permute-start.7 = (bf16[200,1024]{1,0:T(8,128)(2,1)}, bf16[200,1024]{1,0:T(8,128)(2,1)S(1)}, u32[]{:S(2)}, u32[]{:S(2)}) collective-permute-start(bf16[200,1024]{1,0:T(8,128)(2,1)} %collective-permute-done.4), channel_id=1, source_target_pairs={{0,4},{4,8},{8,12},{12,16},{16,20},{20,24},{24,28},{28,0},{1,5},{5... | collective-permute-start | bytes 1228808 | tf_op jit(solution)/shard_map/ppermute | solution.py:256
  60.8 11.9 %copy-start.13 = (f32[1024]{0:T(1024)S(1)}, f32[1024]{0:T(1024)}, u32[]{:S(2)}) copy-start(f32[1024]{0:T(1024)} %param.15) | copy-start | bytes 12292
  60.8 36.6 %all-to-all-start.1 = ((bf16[8,128,1024]{2,1,0:T(8,128)(2,1)}), bf16[8,128,1024]{2,1,0:T(8,128)(2,1)}, u32[]{:S(2)}, u32[]{:S(2)}) async-start(bf16[8,128,1024]{2,1,0:T(8,128)(2,1)} %tail.1), calls=%async_computation.1 | async-start | bytes 4194304 | tf_op jit(solution)/shard_map/all_to_all | solution.py:360
  67.7 0.6 copy-start.15
  72.7 1.0 copy-start.4
  73.7 0.9 copy-start.8
  74.6 0.7 copy-start.10
  75.5 0.8 copy-start
  97.4 1.0 copy-start.1
  98.5 0.7 copy-start.11
  101.4 34.7 %copy-start.6 = (bf16[128,1024]{1,0:T(8,128)(2,1)}, bf16[128,1024]{1,0:T(8,128)(2,1)S(1)}, u32[]{:S(2)}) copy-start(bf16[128,1024]{1,0:T(8,128)(2,1)S(1)} %get-tuple-element.52.feature_ref) | copy-start | bytes 786436
  101.4 4.6 %collective-permute-start.10 = (f32[8,128]{1,0:T(8,128)S(1)}, f32[8,128]{1,0:T(8,128)S(1)}, u32[]{:S(2)}, u32[]{:S(2)}) collective-permute-start(f32[8,128]{1,0:T(8,128)S(1)} %get-tuple-element.53.refs_0_), channel_id=1, source_target_pairs={{0,3},{1,2},{2,1},{3,0},{4,7},{5,6},{6,5},{7,4},{8,11},{9,10},{10,... | collective-permute-start | bytes 12296 | tf_op jit(solution)/shard_map/ppermute | solution.py:425
  102.3 3.8 %collective-permute-start.8 = (f32[8,128]{1,0:T(8,128)S(1)}, f32[8,128]{1,0:T(8,128)S(1)}, u32[]{:S(2)}, u32[]{:S(2)}) collective-permute-start(f32[8,128]{1,0:T(8,128)S(1)} %get-tuple-element.53.refs_0_), channel_id=1, source_target_pairs={{0,1},{1,0},{2,3},{3,2},{4,5},{5,4},{6,7},{7,6},{8,9},{9,8},{10,11... | collective-permute-start | bytes 12296 | tf_op jit(solution)/shard_map/ppermute | solution.py:425
  103.9 5.1 %collective-permute-start.9 = (f32[8,128]{1,0:T(8,128)S(1)}, f32[8,128]{1,0:T(8,128)S(1)}, u32[]{:S(2)}, u32[]{:S(2)}) collective-permute-start(f32[8,128]{1,0:T(8,128)S(1)} %get-tuple-element.53.refs_0_), channel_id=1, source_target_pairs={{0,2},{1,3},{2,0},{3,1},{4,6},{5,7},{6,4},{7,5},{8,10},{9,11},{10,... | collective-permute-start | bytes 12296 | tf_op jit(solution)/shard_map/ppermute | solution.py:425
  109.0 1.0 copy-start.2
  110.9 7.8 %collective-permute-start.11 = (bf16[8,16,1024]{2,1,0:T(8,128)(2,1)S(1)}, bf16[8,16,1024]{2,1,0:T(8,128)(2,1)S(1)}, u32[]{:S(2)}, u32[]{:S(2)}) collective-permute-start(bf16[8,16,1024]{2,1,0:T(8,128)(2,1)S(1)} %grads.1.refs_0_), channel_id=1, source_target_pairs={{0,128},{32,160},{64,192},{96,224},{128,0},{160,32},{192,64},{224,... | collective-permute-start | bytes 786440 | tf_op jit(solution)/shard_map/ppermute | solution.py:441
  113.4 8.0 %collective-permute-start.12 = (bf16[8,16,1024]{2,1,0:T(8,128)(2,1)S(1)}, bf16[8,16,1024]{2,1,0:T(8,128)(2,1)S(1)}, u32[]{:S(2)}, u32[]{:S(2)}) collective-permute-start(bf16[8,16,1024]{2,1,0:T(8,128)(2,1)S(1)} %grads.1.refs_0_), channel_id=1, source_target_pairs={{0,32},{32,64},{64,96},{96,0},{128,160},{160,192},{192,224},{224,1... | collective-permute-start | bytes 786440 | tf_op jit(solution)/shard_map/ppermute | solution.py:441
  113.4 10.0 %collective-permute-start.13 = (bf16[8,16,1024]{2,1,0:T(8,128)(2,1)S(1)}, bf16[8,16,1024]{2,1,0:T(8,128)(2,1)S(1)}, u32[]{:S(2)}, u32[]{:S(2)}) collective-permute-start(bf16[8,16,1024]{2,1,0:T(8,128)(2,1)S(1)} %grads.1.refs_0_), channel_id=1, source_target_pairs={{0,96},{32,0},{64,32},{96,64},{128,224},{160,128},{192,160},{224,1... | collective-permute-start | bytes 786440 | tf_op jit(solution)/shard_map/ppermute | solution.py:441
  118.8 7.6 %collective-permute-start.15 = (bf16[8,16,1024]{2,1,0:T(8,128)(2,1)S(1)}, bf16[8,16,1024]{2,1,0:T(8,128)(2,1)S(1)}, u32[]{:S(2)}, u32[]{:S(2)}) collective-permute-start(bf16[8,16,1024]{2,1,0:T(8,128)(2,1)S(1)} %collective-permute-done.11.refs_1_), channel_id=1, source_target_pairs={{0,96},{32,0},{64,32},{96,64},{128,224},{160,128},{192,160},{224,1... | collective-permute-start | bytes 786440 | tf_op jit(solution)/shard_map/ppermute | solution.py:441
  123.4 8.0 %collective-permute-start.16 = (bf16[8,16,1024]{2,1,0:T(8,128)(2,1)S(1)}, bf16[8,16,1024]{2,1,0:T(8,128)(2,1)S(1)}, u32[]{:S(2)}, u32[]{:S(2)}) collective-permute-start(bf16[8,16,1024]{2,1,0:T(8,128)(2,1)S(1)} %collective-permute-done.12.refs_2_), channel_id=1, source_target_pairs={{0,32},{32,64},{64,96},{96,0},{128,160},{160,192},{192,224},{224,1... | collective-permute-start | bytes 786440 | tf_op jit(solution)/shard_map/ppermute | solution.py:441
  123.4 10.8 %collective-permute-start.14 = (bf16[8,16,1024]{2,1,0:T(8,128)(2,1)S(1)}, bf16[8,16,1024]{2,1,0:T(8,128)(2,1)S(1)}, u32[]{:S(2)}, u32[]{:S(2)}) collective-permute-start(bf16[8,16,1024]{2,1,0:T(8,128)(2,1)S(1)} %collective-permute-done.11.refs_1_), channel_id=1, source_target_pairs={{0,32},{32,64},{64,96},{96,0},{128,160},{160,192},{192,224},{224,1... | collective-permute-start | bytes 786440 | tf_op jit(solution)/shard_map/ppermute | solution.py:441
  126.3 8.0 %collective-permute-start.17 = (bf16[8,16,1024]{2,1,0:T(8,128)(2,1)S(1)}, bf16[8,16,1024]{2,1,0:T(8,128)(2,1)S(1)}, u32[]{:S(2)}, u32[]{:S(2)}) collective-permute-start(bf16[8,16,1024]{2,1,0:T(8,128)(2,1)S(1)} %collective-permute-done.15.refs_5_), channel_id=1, source_target_pairs={{0,96},{32,0},{64,32},{96,64},{128,224},{160,128},{192,160},{224,1... | collective-permute-start | bytes 786440 | tf_op jit(solution)/shard_map/ppermute | solution.py:441
  137.3 2.9 %collective-permute-start.19 = (bf16[256,1664]{1,0:T(8,128)(2,1)S(1)}, bf16[256,1664]{1,0:T(8,128)(2,1)S(1)}, u32[]{:S(2)}, u32[]{:S(2)}) collective-permute-start(bf16[256,1664]{1,0:T(8,128)(2,1)S(1)} %give1.1), channel_id=1, source_target_pairs={{0,1},{1,0},{2,3},{3,2},{4,5},{5,4},{6,7},{7,6},{8,9},{9,8},{10,11... | collective-permute-start | bytes 2555912 | tf_op jit(solution)/shard_map/ppermute | solution.py:486
  137.4 3.6 %collective-permute-start.18 = (bf16[256,1664]{1,0:T(8,128)(2,1)S(1)}, bf16[256,1664]{1,0:T(8,128)(2,1)S(1)}, u32[]{:S(2)}, u32[]{:S(2)}) collective-permute-start(bf16[256,1664]{1,0:T(8,128)(2,1)S(1)} %give0.1), channel_id=1, source_target_pairs={{0,1},{1,0},{2,3},{3,2},{4,5},{5,4},{6,7},{7,6},{8,9},{9,8},{10,11... | collective-permute-start | bytes 2555912 | tf_op jit(solution)/shard_map/ppermute | solution.py:486
  142.4 30.8 %copy-start.3 = (f32[32,12800]{1,0:T(8,128)S(1)}, f32[32,12800]{1,0:T(8,128)}, u32[]{:S(2)}) copy-start(f32[32,12800]{1,0:T(8,128)} %get-tuple-element.57.hat_ref) | copy-start | bytes 4915204
  142.4 30.8 %copy-start.9 = (f32[12800]{0:T(1024)S(1)}, f32[12800]{0:T(1024)}, u32[]{:S(2)}) copy-start(f32[12800]{0:T(1024)} %gain_ref.3) | copy-start | bytes 153604
  142.4 30.8 %copy-start.12 = (f32[32,128]{1,0:T(8,128)S(1)}, f32[32,128]{1,0:T(8,128)}, u32[]{:S(2)}) copy-start(f32[32,128]{1,0:T(8,128)} %get-tuple-element.45.before_ref.hat_ref.inv_ref) | copy-start | bytes 49156
  142.4 30.8 %all-to-all-start.2 = ((bf16[16,32,1664]{2,1,0:T(8,128)(2,1)}), bf16[16,32,1664]{2,1,0:T(8,128)(2,1)S(1)}, u32[]{:S(2)}, u32[]{:S(2)}) async-start(bf16[16,32,1664]{2,1,0:T(8,128)(2,1)} %join.1), calls=%async_computation.2 | async-start | bytes 3407872 | tf_op jit(solution)/shard_map/all_to_all | solution.py:499
  148.6 0.9 copy-start.5
  149.5 0.9 copy-start.7

commit v6 on v5

--- a/solution.py
+++ b/solution.py
@@ -114,8 +114,7 @@
             out_ref[side * half + j] = (main_ref[j] + product).astype(BF)
 
 
-def prepare_kernel(before_ref, text_ref, cot_ref, gain_ref, upstream_ref, stat_ref):
-    del before_ref
+def prepare_kernel(text_ref, cot_ref, gain_ref, upstream_ref, stat_ref):
     upstream_ref[...] = cot_ref[...].astype(F32) * gain_ref[...]
     text = text_ref[...].astype(F32)
     square = jnp.sum(text * text, axis=1, keepdims=True)
@@ -124,24 +123,29 @@
 
 
 def slots_kernel(
-    place_ref, pick_ref, hat_ref, parts_ref, upstream_ref, text_stat_ref, feature_ref, slope_ref, stat_ref
+    place_ref, parts_ref, upstream_ref, text_stat_ref, feature_ref, slope_ref, grad_ref, stat_ref, held, sem
 ):
-    del pick_ref, hat_ref
-    lane = lax.broadcasted_iota(jnp.int32, (UNIT, LANES), 1)
-    stats = []
-    for s in range(feature_ref.shape[0] // UNIT):
+    copy = pltpu.make_async_copy(upstream_ref, held, sem)
+    copy.start()
+    runs = feature_ref.shape[0] // UNIT
+    for s in range(runs):
         rows = slice(s * UNIT, (s + 1) * UNIT)
         projected = parts_ref[0, rows].astype(F32)
         for k in range(1, parts_ref.shape[0]):
             projected = projected + parts_ref[k, rows].astype(F32)
         gate = 0.5 * (1.0 + lax.erf(projected * HALF_ROOT))
-        feature = (projected * gate).astype(BF)
-        feature_ref[rows] = feature
+        feature_ref[rows] = (projected * gate).astype(BF)
         slope_ref[rows] = gate + projected * jnp.exp(-0.5 * projected * projected) * INV_ROOT_TWO_PI
-        wide = feature.astype(F32)
+    copy.wait()
+    lane = lax.broadcasted_iota(jnp.int32, (UNIT, LANES), 1)
+    stats = []
+    for s in range(runs):
+        rows = slice(s * UNIT, (s + 1) * UNIT)
         at = pl.ds(pl.multiple_of(place_ref[s] * UNIT, UNIT), UNIT)
+        wide, upstream = feature_ref[rows].astype(F32), held[at]
+        grad_ref[rows] = upstream
         square = jnp.sum(wide * wide, axis=1, keepdims=True)
-        cross = jnp.sum(upstream_ref[at] * wide, axis=1, keepdims=True)
+        cross = jnp.sum(upstream * wide, axis=1, keepdims=True)
         stats.append(jnp.where(lane == 0, square, cross))
     stat = jnp.transpose(jnp.concatenate(stats, axis=0))[: stat_ref.shape[0]]
     row = lax.broadcasted_iota(jnp.int32, stat.shape, 0)
@@ -155,7 +159,7 @@
 
 
 def grad_kernel(
-    width, place_ref, live_ref, feature_ref, slope_ref, upstream_ref, *refs
+    width, live_ref, feature_ref, slope_ref, upstream_ref, *refs
 ):
     stat_refs, grad_ref = refs[:-1], refs[-1]
     stat = row_scales(stat_refs, width)
@@ -163,8 +167,7 @@
         rows = slice(s * UNIT, (s + 1) * UNIT)
         inv, cross = lax.rsqrt(stat[rows, 0:1] + EPSILON), stat[rows, 1:2]
         wide = feature_ref[rows].astype(F32)
-        at = pl.ds(pl.multiple_of(place_ref[s] * UNIT, UNIT), UNIT)
-        hidden_grad = (inv * (upstream_ref[at] - wide * inv * inv * cross)).astype(BF)
+        hidden_grad = (inv * (upstream_ref[rows] - wide * inv * inv * cross)).astype(BF)
         grad = (hidden_grad.astype(F32) * slope_ref[rows]).astype(BF)
         grad = jnp.where(live_ref[s] > 0, grad, jnp.zeros_like(grad))
         grad_ref[s] = grad
@@ -236,8 +239,14 @@
     groups = lax.axis_size("dp")
     me = lax.axis_index("dp")
     height = block.shape[0]
-    up = [(i, (i + 1) % groups) for i in range(groups)]
-    down = [(i, (i - 1) % groups) for i in range(groups)]
+    turn = 1 - 2 * lax.axis_index("core")
+    ring = ("dp", "core")
+    up = [
+        (i * 2 + core, (i + 1 - 2 * core) % groups * 2 + core)
+        for i in range(groups)
+        for core in range(2)
+    ]
+    down = [(target, source) for source, target in up]
     out = jnp.zeros((rows, block.shape[1]), block.dtype)
 
     def put(out, piece, owner):
@@ -246,16 +255,20 @@
     out = put(out, block, me)
     rising = falling = block
     for hop in range(1, (groups - 1) // 2 + 1):
-        rising = lax.ppermute(rising, "dp", up)
-        falling = lax.ppermute(falling, "dp", down)
+        rising = lax.ppermute(rising, ring, up)
+        falling = lax.ppermute(falling, ring, down)
         out, rising, falling = lax.optimization_barrier((out, rising, falling))
         if hop == 1:
             rising, falling, beside = lax.optimization_barrier((rising, falling, beside))
-        out = put(out, rising, me - hop + groups)
-        out = put(out, falling, me + hop)
-    last = lax.ppermute(rising, "dp", up)
+        out = put(out, rising, me - hop * turn + groups)
+        out = put(out, falling, me + hop * turn + groups)
+    last = lax.ppermute(rising, ring, up)
     owner = (me + groups // 2) % groups
     return out, last, owner * height, rising, falling, beside
+
+
+def after(value, *marks):
+    return lax.optimization_barrier((value, marks))[0]
 
 
 def fill_places(wanted, alive, places):
@@ -401,26 +414,28 @@
     )((tensor * share).reshape(1).astype(jnp.int32), table, vision_rows)
     upstream, text_stat = pl.pallas_call(
         prepare_kernel,
-        out_shape=(shape((slots, columns), F32), shape((8, LANES), F32)),
-        in_specs=[ANY] + [VMEM] * 3,
+        out_shape=(pltpu.HBM((slots, columns), F32), shape((8, LANES), F32)),
+        in_specs=[VMEM] * 3,
         out_specs=(VMEM, VMEM),
         compiler_params=PARAMS,
         cost_estimate=FREE,
         name="prepare",
-    )(hat_inv, text_rows, out_cotangent, text_gain_row)
-    feature, slope, stat = pl.pallas_call(
+    )(text_rows, out_cotangent, after(text_gain_row, hat_inv))
+    feature, slope, run_upstream, stat = pl.pallas_call(
         slots_kernel,
         out_shape=(
             shape((slots, columns), BF),
             shape((slots, columns), F32),
+            shape((slots, columns), F32),
             shape((8, LANES), F32),
         ),
-        in_specs=[SMEM, ANY, ANY, VMEM, VMEM, VMEM],
-        out_specs=(VMEM, VMEM, VMEM),
+        in_specs=[SMEM, VMEM, pl.BlockSpec(memory_space=pltpu.HBM), VMEM],
+        out_specs=(VMEM,) * 4,
+        scratch_shapes=[pltpu.VMEM((slots, columns), F32), pltpu.SemaphoreType.DMA],
         compiler_params=PARAMS,
         cost_estimate=FREE,
         name="slots",
-    )(where, pick, hat_inv, partial, upstream, text_stat)
+    )(after(where, pick, hat_inv), partial, upstream, text_stat)
     stats = [stat] + [
         lax.ppermute(stat, ("y_hi", "core"), [(i, i ^ turn) for i in range(tensors)])
         for turn in range(1, tensors)
@@ -428,12 +443,12 @@
     grads = pl.pallas_call(
         functools.partial(grad_kernel, width),
         out_shape=shape((sections, UNIT, columns), BF),
-        in_specs=[SMEM, SMEM] + [VMEM] * (3 + tensors),
+        in_specs=[SMEM] + [VMEM] * (3 + tensors),
         out_specs=VMEM,
         compiler_params=PARAMS,
         cost_estimate=FREE,
         name="grads",
-    )(where, has, feature, slope, upstream, *stats)
+    )(has, feature, slope, run_upstream, *stats)
     def turn(block, dx, dy=0):
         moves = [
             (i, (i // along ^ dy) * along + (i + dx) % along) for i in range(sections)

time: 176 us -> 174 us (0.989)
  local copies, waits for them, and re-layouts: 16.7 us -> 13.4 us
  waiting for transfers between devices: 76.2 us -> 78.3 us
    unnamed x36 -> x28, local copies, waits for them, and re-layouts: 8.54 us -> 5.27 us
  transfers between devices with their start and end apart: 23 -> 23, of which waited for: 15 -> 17; matrix products, arithmetic and copies ran while one was open for 5% -> 5% of each run, Pallas kernels for 11% -> 12%
where the time goes in v6:
time: 174 us; the launch traced here: 173 us
  waiting for transfers between devices  78.3 us (45%)
  starting transfers between devices  46.8 us (27%)
  Pallas kernels  32.6 us (19%)
  local copies, waits for them, and re-layouts  13.4 us (8%)
    all_to_all x1, waiting for transfers between devices, shards(): partial = lax.all_to_all(partial, along_first, 0, 0, tiled=True)  21.8 us
    all_to_all x1, waiting for transfers between devices, shards(): back = lax.all_to_all(total, ('x', 'y_hi', 'y_lo'), 0, 0, tiled=True)  20.8 us
    ppermute x3, waiting for transfers between devices, ring_gather(): rising = lax.ppermute(rising, ring, up)  18.5 us
    ppermute x7, waiting for transfers between devices, turn(): return lax.ppermute(block, ('y_lo', 'x'), moves)  11.9 us
    ppermute x7, starting transfers between devices, turn(): return lax.ppermute(block, ('y_lo', 'x'), moves)  11.3 us
    ppermute x3, starting transfers between devices, ring_gather(): falling = lax.ppermute(falling, ring, down)  11 us
    pallas_call x2, Pallas kernels, forward(): pl.pallas_call(forward_kernel, out_shape=(shape((half, sections * UNIT, c...  6.85 us
    dynamic_update_slice x7, local copies, waits for them, and re-layouts, put(): lax.dynamic_update_slice_in_dim(out, piece, owner % groups * height, 0)  6.23 us
  transfers between devices with their start and end apart: 23, of which 17 were waited for; matrix products, arithmetic and copies ran while one was open for 5% of the time, Pallas kernels for 12%

profile of v6, /device:TPU:8, one launch (start us, length us, event | category | flops | bytes accessed | tf_op | source)
XLA Modules:
  0.0 173.1 jit_solution(13311410402288503021)
XLA Ops:
  0.6 2.0 %collective-permute-start = (bf16[200,1024]{1,0:T(8,128)(2,1)}, bf16[200,1024]{1,0:T(8,128)(2,1)}, u32[]{:S(2)}, u32[]{:S(2)}) collective-permute-start(bf16[200,1024]{1,0:T(8,128)(2,1)} %param.13), channel_id=1, source_target_pairs={{0,4},{1,29},{4,8},{5,1},{8,12},{9,5},{12,16},{13,9},{16,20},{17,1... | collective-permute-start | bytes 1228808 | tf_op jit(solution)/shard_map/ppermute | solution.py:258
  2.6 4.0 %collective-permute-start.1 = (bf16[200,1024]{1,0:T(8,128)(2,1)}, bf16[200,1024]{1,0:T(8,128)(2,1)}, u32[]{:S(2)}, u32[]{:S(2)}) collective-permute-start(bf16[200,1024]{1,0:T(8,128)(2,1)} %param.13), channel_id=1, source_target_pairs={{4,0},{29,1},{8,4},{1,5},{12,8},{5,9},{16,12},{9,13},{20,16},{13,1... | collective-permute-start | bytes 1228808 | tf_op jit(solution)/shard_map/ppermute | solution.py:259
  6.7 5.6 %vision_norm.1 = bf16[8,64,1664]{2,1,0:T(8,128)(2,1)} custom-call(s32[128]{0:T(128)} %slot_ref.1, s32[1]{0:T(128)} %bitcast.1.core_ref, bf16[128,12800]{1,0:T(8,128)(2,1)} %rows_ref.3, f32[12800]{0:T(1024)} %gain_ref.3, f32[12800]{0:T(1024)} %bias_ref.1), custom_call_target="tpu_custom_call" | custom-call | tf_op jit(solution)/shard_map/vision_norm/pallas_call | solution.py:313
  12.3 0.4 broadcast_in_dim.45
  12.8 2.5 %collective-permute-done = bf16[200,1024]{1,0:T(8,128)(2,1)} collective-permute-done((bf16[200,1024]{1,0:T(8,128)(2,1)}, bf16[200,1024]{1,0:T(8,128)(2,1)}, u32[]{:S(2)}, u32[]{:S(2)}) %collective-permute-start) | collective-permute-done | bytes 409632 | tf_op jit(solution)/shard_map/ppermute | solution.py:258
  15.3 0.3 collective-permute-done.1
  15.6 5.8 %all-to-all-start = ((bf16[8,64,1664]{2,1,0:T(8,128)(2,1)}), bf16[8,64,1664]{2,1,0:T(8,128)(2,1)}, u32[]{:S(2)}, u32[]{:S(2)}) async-start(bf16[8,64,1664]{2,1,0:T(8,128)(2,1)} %vision_norm.1), calls=%async_computation | async-start | bytes 3407872 | tf_op jit(solution)/shard_map/all_to_all | solution.py:324
  21.4 3.7 %collective-permute-start.3 = (bf16[200,1024]{1,0:T(8,128)(2,1)}, bf16[200,1024]{1,0:T(8,128)(2,1)}, u32[]{:S(2)}, u32[]{:S(2)}) collective-permute-start(bf16[200,1024]{1,0:T(8,128)(2,1)} %collective-permute-done.1), channel_id=1, source_target_pairs={{4,0},{29,1},{8,4},{1,5},{12,8},{5,9},{16,12},{9,13},{20,16},{13,1... | collective-permute-start | bytes 1228808 | tf_op jit(solution)/shard_map/ppermute | solution.py:259
  25.1 1.0 constant_dynamic-update-slice_fusion.7
  26.1 1.0 constant_dynamic-update-slice_fusion.6
  27.1 7.9 %collective-permute-done.2 = bf16[200,1024]{1,0:T(8,128)(2,1)} collective-permute-done((bf16[200,1024]{1,0:T(8,128)(2,1)}, bf16[200,1024]{1,0:T(8,128)(2,1)}, u32[]{:S(2)}, u32[]{:S(2)}) %collective-permute-start.2) | collective-permute-done | bytes 409632 | tf_op jit(solution)/shard_map/ppermute | solution.py:258
  35.0 3.2 %collective-permute-start.5 = (bf16[200,1024]{1,0:T(8,128)(2,1)}, bf16[200,1024]{1,0:T(8,128)(2,1)}, u32[]{:S(2)}, u32[]{:S(2)}) collective-permute-start(bf16[200,1024]{1,0:T(8,128)(2,1)} %collective-permute-done.3), channel_id=1, source_target_pairs={{4,0},{29,1},{8,4},{1,5},{12,8},{5,9},{16,12},{9,13},{20,16},{13,1... | collective-permute-start | bytes 1228808 | tf_op jit(solution)/shard_map/ppermute | solution.py:259
  38.2 1.0 constant_dynamic-update-slice_fusion.5
  39.3 1.0 constant_dynamic-update-slice_fusion.4
  40.3 8.1 %collective-permute-done.4 = bf16[200,1024]{1,0:T(8,128)(2,1)} collective-permute-done((bf16[200,1024]{1,0:T(8,128)(2,1)}, bf16[200,1024]{1,0:T(8,128)(2,1)}, u32[]{:S(2)}, u32[]{:S(2)}) %collective-permute-start.4) | collective-permute-done | bytes 409632 | tf_op jit(solution)/shard_map/ppermute | solution.py:258
  49.0 1.0 constant_dynamic-update-slice_fusion.3
  50.0 1.0 constant_dynamic-update-slice_fusion.2.weight_ref
  51.0 3.4 %forward_own.1 = (f32[4,128,1024]{2,1,0:T(8,128)S(1)}, bf16[4,128,384]{2,1,0:T(8,128)(2,1)S(1)}, f32[4,8,128]{2,1,0:T(8,128)S(1)}) custom-call(s32[1]{0:T(128)} %bitcast.tile_ref, bf16[8,64,1664]{2,1,0:T(8,128)(2,1)} %all-to-all-done.rows_ref, bf16[1664,1024]{1,0:T(8,128)(2,1)S(1)} %constant_dynamic-update-slice_fusion.2.weight_ref), custom_call_target="tpu_custom_call" | custom-call | tf_op jit(solution)/shard_map/forward_own/pallas_call | solution.py:334
  54.5 3.4 %forward_other.1 = (f32[4,128,1024]{2,1,0:T(8,128)S(1)}, bf16[4,128,384]{2,1,0:T(8,128)(2,1)S(1)}, f32[4,8,128]{2,1,0:T(8,128)S(1)}) custom-call(s32[1]{0:T(128)} %bitcast.tile_ref, bf16[8,64,1664]{2,1,0:T(8,128)(2,1)} %collective-permute-done.6.rows_ref, bf16[1664,1024]{1,0:T(8,128)(2,1)S(1)} %constant_dynamic-update-slice_fusion.2.weight_ref), custom_call_target="tpu_custom_call" | custom-call | tf_op jit(solution)/shard_map/forward_other/pallas_call | solution.py:334
  57.9 0.3 collective-permute-done.7
  58.4 2.6 %tail.1 = bf16[8,128,1024]{2,1,0:T(8,128)(2,1)} custom-call(s32[1]{0:T(128)} %bitcast.1.core_ref, bf16[4,128,384]{2,1,0:T(8,128)(2,1)S(1)} %get-tuple-element.50.own_window_ref, bf16[4,128,384]{2,1,0:T(8,128)(2,1)S(1)} %get-tuple-element.51.other_window_ref, bf16[384,1024]{1,0:T(8,128)(2,1)S(1)} %get-tuple-element.65.weight_ref, ...), custom_call_target="tpu_custom_call" | custom-call | tf_op jit(solution)/shard_map/tail/pallas_call | solution.py:364
  61.0 6.1 %all-to-all-start.1 = ((bf16[8,128,1024]{2,1,0:T(8,128)(2,1)}), bf16[8,128,1024]{2,1,0:T(8,128)(2,1)}, u32[]{:S(2)}, u32[]{:S(2)}) async-start(bf16[8,128,1024]{2,1,0:T(8,128)(2,1)} %tail.1), calls=%async_computation.1 | async-start | bytes 4194304 | tf_op jit(solution)/shard_map/all_to_all | solution.py:373
  67.2 0.2 slice_reduce_fusion
  67.4 0.4 copy-done.11
  67.8 2.8 %vision_hat.1 = (f32[32,12800]{1,0:T(8,128)}, f32[32,128]{1,0:T(8,128)}) custom-call(s32[1]{0:T(128)} %bitcast.9.first_ref, s32[8,8,3]{2,1,0:T(8,128)} %bitcast.25, bf16[128,12800]{1,0:T(8,128)(2,1)} %rows_ref.3), custom_call_target="tpu_custom_call" | custom-call | tf_op jit(solution)/shard_map/vision_hat/pallas_call | solution.py:399
  70.6 0.2 select_reduce_fusion
  70.9 0.8 constant_dynamic-slice_fusion
  71.9 0.2 reduce-window.16
  72.3 0.2 select_reduce_fusion.1
  72.5 0.9 copy-done.1
  73.5 0.9 copy-done.6
  74.4 0.9 prepare.1
  75.4 21.8 %all-to-all-done.1.parts_ref = bf16[8,128,1024]{2,1,0:T(8,128)(2,1)} async-done(((bf16[8,128,1024]{2,1,0:T(8,128)(2,1)}), bf16[8,128,1024]{2,1,0:T(8,128)(2,1)}, u32[]{:S(2)}, u32[]{:S(2)}) %all-to-all-start.1) | async-done | bytes 2097184 | tf_op jit(solution)/shard_map/all_to_all | solution.py:373
  97.2 1.0 copy-done.5
  98.2 2.3 %slots.1 = (bf16[128,1024]{1,0:T(8,128)(2,1)S(1)}, f32[128,1024]{1,0:T(8,128)S(1)}, f32[128,1024]{1,0:T(8,128)S(1)}, f32[8,128]{1,0:T(8,128)S(1)}) custom-call(s32[8]{0:T(128)S(1)} %fusion.9.place_ref, bf16[8,128,1024]{2,1,0:T(8,128)(2,1)} %all-to-all-done.1.parts_ref, f32[128,1024]{1,0:T(8,128)S(1)} %copy-done.5, f32[8,128]{1,0:T(8,128)S(1)} %get-tuple-element.56.text_stat_ref), custom_call_target="tpu_custom_call" | custom-call | tf_op jit(solution)/shard_map/slots/pallas_call | solution.py:424
  100.6 0.9 collective-permute-start.10
  101.5 1.5 collective-permute-start.8
  103.1 1.3 collective-permute-start.9
  104.3 0.9 collective-permute-done.10.refs_3_
  105.2 3.0 %collective-permute-done.9.refs_2_ = f32[8,128]{1,0:T(8,128)S(1)} collective-permute-done((f32[8,128]{1,0:T(8,128)S(1)}, f32[8,128]{1,0:T(8,128)S(1)}, u32[]{:S(2)}, u32[]{:S(2)}) %collective-permute-start.9) | collective-permute-done | bytes 4128 | tf_op jit(solution)/shard_map/ppermute | solution.py:440
  108.2 0.9 grads.1.refs_0_
  109.0 2.3 %collective-permute-start.11 = (bf16[8,16,1024]{2,1,0:T(8,128)(2,1)S(1)}, bf16[8,16,1024]{2,1,0:T(8,128)(2,1)S(1)}, u32[]{:S(2)}, u32[]{:S(2)}) collective-permute-start(bf16[8,16,1024]{2,1,0:T(8,128)(2,1)S(1)} %grads.1.refs_0_), channel_id=1, source_target_pairs={{0,128},{32,160},{64,192},{96,224},{128,0},{160,32},{192,64},{224,... | collective-permute-start | bytes 786440 | tf_op jit(solution)/shard_map/ppermute | solution.py:456
  111.4 3.2 %collective-permute-start.13 = (bf16[8,16,1024]{2,1,0:T(8,128)(2,1)S(1)}, bf16[8,16,1024]{2,1,0:T(8,128)(2,1)S(1)}, u32[]{:S(2)}, u32[]{:S(2)}) collective-permute-start(bf16[8,16,1024]{2,1,0:T(8,128)(2,1)S(1)} %grads.1.refs_0_), channel_id=1, source_target_pairs={{0,96},{32,0},{64,32},{96,64},{128,224},{160,128},{192,160},{224,1... | collective-permute-start | bytes 786440 | tf_op jit(solution)/shard_map/ppermute | solution.py:456
  114.6 2.1 %collective-permute-done.11.refs_1_ = bf16[8,16,1024]{2,1,0:T(8,128)(2,1)S(1)} collective-permute-done((bf16[8,16,1024]{2,1,0:T(8,128)(2,1)S(1)}, bf16[8,16,1024]{2,1,0:T(8,128)(2,1)S(1)}, u32[]{:S(2)}, u32[]{:S(2)}) %collective-permute-start.11) | collective-permute-done | bytes 262176 | tf_op jit(solution)/shard_map/ppermute | solution.py:456
  116.8 2.5 %collective-permute-done.12.refs_2_ = bf16[8,16,1024]{2,1,0:T(8,128)(2,1)S(1)} collective-permute-done((bf16[8,16,1024]{2,1,0:T(8,128)(2,1)S(1)}, bf16[8,16,1024]{2,1,0:T(8,128)(2,1)S(1)}, u32[]{:S(2)}, u32[]{:S(2)}) %collective-permute-start.12) | collective-permute-done | bytes 262176 | tf_op jit(solution)/shard_map/ppermute | solution.py:456
  119.4 2.0 %collective-permute-done.13.refs_4_ = bf16[8,16,1024]{2,1,0:T(8,128)(2,1)S(1)} collective-permute-done((bf16[8,16,1024]{2,1,0:T(8,128)(2,1)S(1)}, bf16[8,16,1024]{2,1,0:T(8,128)(2,1)S(1)}, u32[]{:S(2)}, u32[]{:S(2)}) %collective-permute-start.13) | collective-permute-done | bytes 262176 | tf_op jit(solution)/shard_map/ppermute | solution.py:456
  121.4 1.9 %collective-permute-start.14 = (bf16[8,16,1024]{2,1,0:T(8,128)(2,1)S(1)}, bf16[8,16,1024]{2,1,0:T(8,128)(2,1)S(1)}, u32[]{:S(2)}, u32[]{:S(2)}) collective-permute-start(bf16[8,16,1024]{2,1,0:T(8,128)(2,1)S(1)} %collective-permute-done.11.refs_1_), channel_id=1, source_target_pairs={{0,32},{32,64},{64,96},{96,0},{128,160},{160,192},{192,224},{224,1... | collective-permute-start | bytes 786440 | tf_op jit(solution)/shard_map/ppermute | solution.py:456
  123.2 1.0 collective-permute-done.15.refs_5_
  124.2 3.7 %collective-permute-start.17 = (bf16[8,16,1024]{2,1,0:T(8,128)(2,1)S(1)}, bf16[8,16,1024]{2,1,0:T(8,128)(2,1)S(1)}, u32[]{:S(2)}, u32[]{:S(2)}) collective-permute-start(bf16[8,16,1024]{2,1,0:T(8,128)(2,1)S(1)} %collective-permute-done.15.refs_5_), channel_id=1, source_target_pairs={{0,96},{32,0},{64,32},{96,64},{128,224},{160,128},{192,160},{224,1... | collective-permute-start | bytes 786440 | tf_op jit(solution)/shard_map/ppermute | solution.py:456
  127.9 1.5 collective-permute-done.16.refs_6_
  129.4 2.8 %collective-permute-done.14.refs_3_ = bf16[8,16,1024]{2,1,0:T(8,128)(2,1)S(1)} collective-permute-done((bf16[8,16,1024]{2,1,0:T(8,128)(2,1)S(1)}, bf16[8,16,1024]{2,1,0:T(8,128)(2,1)S(1)}, u32[]{:S(2)}, u32[]{:S(2)}) %collective-permute-start.14) | collective-permute-done | bytes 262176 | tf_op jit(solution)/shard_map/ppermute | solution.py:456
  132.2 0.7 arrange.1.grads_ref
  132.9 1.1 give1.1
  134.1 1.1 give0.1
  135.3 0.5 collective-permute-start.18
  135.8 2.3 %keep.1.own_ref = f32[512,1664]{1,0:T(8,128)S(1)} custom-call(bf16[64,16,1024]{2,1,0:T(8,128)(2,1)S(1)} %arrange.1.grads_ref, bf16[1664,1024]{1,0:T(8,128)(2,1)S(1)} %get-tuple-element.64.weight_ref), custom_call_target="tpu_custom_call" | custom-call | tf_op jit(solution)/shard_map/keep/pallas_call | solution.py:486
  138.2 0.8 collective-permute-done.18.low_ref
  138.9 1.4 join.1
  140.3 6.2 %all-to-all-start.2 = ((bf16[16,32,1664]{2,1,0:T(8,128)(2,1)}), bf16[16,32,1664]{2,1,0:T(8,128)(2,1)S(1)}, u32[]{:S(2)}, u32[]{:S(2)}) async-start(bf16[16,32,1664]{2,1,0:T(8,128)(2,1)} %join.1), calls=%async_computation.2 | async-start | bytes 3407872 | tf_op jit(solution)/shard_map/all_to_all | solution.py:514
  146.5 0.9 copy-done.2
  147.5 0.9 copy-done.4
  148.4 1.9 %normed.1 = bf16[128,1024]{1,0:T(8,128)(2,1)} custom-call(s32[8]{0:T(128)S(1)} %fusion.9.place_ref, s32[8]{0:T(128)S(1)} %get-tuple-element.66.live_ref, bf16[128,1024]{1,0:T(8,128)(2,1)S(1)} %copy-done.2, bf16[128,1024]{1,0:T(8,128)(2,1)S(1)} %copy-done.4, f32[1,1024]{1,0:T(1,128)S(1)} %bitcast.23, f32[8,128]{1,0:T(8,128)S(1)} %get-tuple-element.58.refs_0_, ...), custom_call_target="tpu_custom_call" | custom-call | tf_op jit(solution)/shard_map/normed/pallas_call | solution.py:472
  150.3 20.8 %all-to-all-done.2.parts_ref = bf16[16,32,1664]{2,1,0:T(8,128)(2,1)S(1)} async-done(((bf16[16,32,1664]{2,1,0:T(8,128)(2,1)}), bf16[16,32,1664]{2,1,0:T(8,128)(2,1)S(1)}, u32[]{:S(2)}, u32[]{:S(2)}) %all-to-all-start.2) | async-done | bytes 1703968 | tf_op jit(solution)/shard_map/all_to_all | solution.py:514
  171.1 2.0 %vision_back.1 = bf16[32,12800]{1,0:T(8,128)(2,1)} custom-call(bf16[16,32,1664]{2,1,0:T(8,128)(2,1)S(1)} %all-to-all-done.2.parts_ref, f32[32,12800]{1,0:T(8,128)S(1)} %copy-done, f32[32,128]{1,0:T(8,128)S(1)} %copy-done.8, f32[12800]{0:T(1024)S(1)} %copy-done.7), custom_call_target="tpu_custom_call" | custom-call | tf_op jit(solution)/shard_map/vision_back/pallas_call | solution.py:519
  (60 shorter events, 1.7 us)
Async XLA Ops:
  0.6 14.7 %collective-permute-start = (bf16[200,1024]{1,0:T(8,128)(2,1)}, bf16[200,1024]{1,0:T(8,128)(2,1)}, u32[]{:S(2)}, u32[]{:S(2)}) collective-permute-start(bf16[200,1024]{1,0:T(8,128)(2,1)} %param.13), channel_id=1, source_target_pairs={{0,4},{1,29},{4,8},{5,1},{8,12},{9,5},{12,16},{13,9},{16,20},{17,1... | collective-permute-start | bytes 1228808 | tf_op jit(solution)/shard_map/ppermute | solution.py:258
  2.6 13.0 %collective-permute-start.1 = (bf16[200,1024]{1,0:T(8,128)(2,1)}, bf16[200,1024]{1,0:T(8,128)(2,1)}, u32[]{:S(2)}, u32[]{:S(2)}) collective-permute-start(bf16[200,1024]{1,0:T(8,128)(2,1)} %param.13), channel_id=1, source_target_pairs={{4,0},{29,1},{8,4},{1,5},{12,8},{5,9},{16,12},{9,13},{20,16},{13,1... | collective-permute-start | bytes 1228808 | tf_op jit(solution)/shard_map/ppermute | solution.py:259
  6.7 6.1 %copy-start.10 = (bf16[200,1024]{1,0:T(8,128)(2,1)S(1)}, bf16[200,1024]{1,0:T(8,128)(2,1)}, u32[]{:S(2)}) copy-start(bf16[200,1024]{1,0:T(8,128)(2,1)} %param.13) | copy-start | bytes 1228804
  12.8 36.0 %copy-start.12 = (s32[8]{0:T(128)S(1)}, s32[8]{0:T(128)}, u32[]{:S(2)}) copy-start(s32[8]{0:T(128)} %constant.182.clone) | copy-start | bytes 100
  12.8 36.0 %copy-start.13 = (s32[8]{0:T(128)S(1)}, s32[8]{0:T(128)}, u32[]{:S(2)}) copy-start(s32[8]{0:T(128)} %constant.184) | copy-start | bytes 100
  15.6 32.9 %all-to-all-start = ((bf16[8,64,1664]{2,1,0:T(8,128)(2,1)}), bf16[8,64,1664]{2,1,0:T(8,128)(2,1)}, u32[]{:S(2)}, u32[]{:S(2)}) async-start(bf16[8,64,1664]{2,1,0:T(8,128)(2,1)} %vision_norm.1), calls=%async_computation | async-start | bytes 3407872 | tf_op jit(solution)/shard_map/all_to_all | solution.py:324
  21.4 13.6 %collective-permute-start.2 = (bf16[200,1024]{1,0:T(8,128)(2,1)}, bf16[200,1024]{1,0:T(8,128)(2,1)}, u32[]{:S(2)}, u32[]{:S(2)}) collective-permute-start(bf16[200,1024]{1,0:T(8,128)(2,1)} %collective-permute-done), channel_id=1, source_target_pairs={{0,4},{1,29},{4,8},{5,1},{8,12},{9,5},{12,16},{13,9},{16,20},{17,1... | collective-permute-start | bytes 1228808 | tf_op jit(solution)/shard_map/ppermute | solution.py:258
  21.4 13.6 %collective-permute-start.3 = (bf16[200,1024]{1,0:T(8,128)(2,1)}, bf16[200,1024]{1,0:T(8,128)(2,1)}, u32[]{:S(2)}, u32[]{:S(2)}) collective-permute-start(bf16[200,1024]{1,0:T(8,128)(2,1)} %collective-permute-done.1), channel_id=1, source_target_pairs={{4,0},{29,1},{8,4},{1,5},{12,8},{5,9},{16,12},{9,13},{20,16},{13,1... | collective-permute-start | bytes 1228808 | tf_op jit(solution)/shard_map/ppermute | solution.py:259
  35.0 13.4 %collective-permute-start.4 = (bf16[200,1024]{1,0:T(8,128)(2,1)}, bf16[200,1024]{1,0:T(8,128)(2,1)}, u32[]{:S(2)}, u32[]{:S(2)}) collective-permute-start(bf16[200,1024]{1,0:T(8,128)(2,1)} %collective-permute-done.2), channel_id=1, source_target_pairs={{0,4},{1,29},{4,8},{5,1},{8,12},{9,5},{12,16},{13,9},{16,20},{17,1... | collective-permute-start | bytes 1228808 | tf_op jit(solution)/shard_map/ppermute | solution.py:258
  35.0 13.4 %collective-permute-start.5 = (bf16[200,1024]{1,0:T(8,128)(2,1)}, bf16[200,1024]{1,0:T(8,128)(2,1)}, u32[]{:S(2)}, u32[]{:S(2)}) collective-permute-start(bf16[200,1024]{1,0:T(8,128)(2,1)} %collective-permute-done.3), channel_id=1, source_target_pairs={{4,0},{29,1},{8,4},{1,5},{12,8},{5,9},{16,12},{9,13},{20,16},{13,1... | collective-permute-start | bytes 1228808 | tf_op jit(solution)/shard_map/ppermute | solution.py:259
  48.5 6.0 %collective-permute-start.6 = (bf16[8,64,1664]{2,1,0:T(8,128)(2,1)}, bf16[8,64,1664]{2,1,0:T(8,128)(2,1)}, u32[]{:S(2)}, u32[]{:S(2)}) collective-permute-start(bf16[8,64,1664]{2,1,0:T(8,128)(2,1)} %all-to-all-done.rows_ref), channel_id=1, source_target_pairs={{0,1},{1,0},{2,3},{3,2},{4,5},{5,4},{6,7},{7,6},{8,9},{9,8},{10,11... | collective-permute-start | bytes 5111816 | tf_op jit(solution)/shard_map/ppermute | solution.py:326
  48.8 9.5 %collective-permute-start.7 = (bf16[200,1024]{1,0:T(8,128)(2,1)}, bf16[200,1024]{1,0:T(8,128)(2,1)S(1)}, u32[]{:S(2)}, u32[]{:S(2)}) collective-permute-start(bf16[200,1024]{1,0:T(8,128)(2,1)} %collective-permute-done.4), channel_id=1, source_target_pairs={{0,4},{1,29},{4,8},{5,1},{8,12},{9,5},{12,16},{13,9},{16,20},{17,1... | collective-permute-start | bytes 1228808 | tf_op jit(solution)/shard_map/ppermute | solution.py:265
  61.0 11.5 %copy-start.9 = (f32[1024]{0:T(1024)S(1)}, f32[1024]{0:T(1024)}, u32[]{:S(2)}) copy-start(f32[1024]{0:T(1024)} %param.15) | copy-start | bytes 12292
  61.0 36.2 %all-to-all-start.1 = ((bf16[8,128,1024]{2,1,0:T(8,128)(2,1)}), bf16[8,128,1024]{2,1,0:T(8,128)(2,1)}, u32[]{:S(2)}, u32[]{:S(2)}) async-start(bf16[8,128,1024]{2,1,0:T(8,128)(2,1)} %tail.1), calls=%async_computation.1 | async-start | bytes 4194304 | tf_op jit(solution)/shard_map/all_to_all | solution.py:373
  67.2 0.6 copy-start.11
  72.5 1.0 copy-start.1
  73.5 0.9 copy-start.6
  97.2 1.0 copy-start.5
  100.6 33.5 %copy-start.3 = (bf16[128,1024]{1,0:T(8,128)(2,1)}, bf16[128,1024]{1,0:T(8,128)(2,1)S(1)}, u32[]{:S(2)}) copy-start(bf16[128,1024]{1,0:T(8,128)(2,1)S(1)} %get-tuple-element.57.feature_ref) | copy-start | bytes 786436
  100.6 4.6 %collective-permute-start.10 = (f32[8,128]{1,0:T(8,128)S(1)}, f32[8,128]{1,0:T(8,128)S(1)}, u32[]{:S(2)}, u32[]{:S(2)}) collective-permute-start(f32[8,128]{1,0:T(8,128)S(1)} %get-tuple-element.58.refs_0_), channel_id=1, source_target_pairs={{0,3},{1,2},{2,1},{3,0},{4,7},{5,6},{6,5},{7,4},{8,11},{9,10},{10,... | collective-permute-start | bytes 12296 | tf_op jit(solution)/shard_map/ppermute | solution.py:440
  101.5 3.7 %collective-permute-start.8 = (f32[8,128]{1,0:T(8,128)S(1)}, f32[8,128]{1,0:T(8,128)S(1)}, u32[]{:S(2)}, u32[]{:S(2)}) collective-permute-start(f32[8,128]{1,0:T(8,128)S(1)} %get-tuple-element.58.refs_0_), channel_id=1, source_target_pairs={{0,1},{1,0},{2,3},{3,2},{4,5},{5,4},{6,7},{7,6},{8,9},{9,8},{10,11... | collective-permute-start | bytes 12296 | tf_op jit(solution)/shard_map/ppermute | solution.py:440
  103.1 5.1 %collective-permute-start.9 = (f32[8,128]{1,0:T(8,128)S(1)}, f32[8,128]{1,0:T(8,128)S(1)}, u32[]{:S(2)}, u32[]{:S(2)}) collective-permute-start(f32[8,128]{1,0:T(8,128)S(1)} %get-tuple-element.58.refs_0_), channel_id=1, source_target_pairs={{0,2},{1,3},{2,0},{3,1},{4,6},{5,7},{6,4},{7,5},{8,10},{9,11},{10,... | collective-permute-start | bytes 12296 | tf_op jit(solution)/shard_map/ppermute | solution.py:440
  109.0 7.7 %collective-permute-start.11 = (bf16[8,16,1024]{2,1,0:T(8,128)(2,1)S(1)}, bf16[8,16,1024]{2,1,0:T(8,128)(2,1)S(1)}, u32[]{:S(2)}, u32[]{:S(2)}) collective-permute-start(bf16[8,16,1024]{2,1,0:T(8,128)(2,1)S(1)} %grads.1.refs_0_), channel_id=1, source_target_pairs={{0,128},{32,160},{64,192},{96,224},{128,0},{160,32},{192,64},{224,... | collective-permute-start | bytes 786440 | tf_op jit(solution)/shard_map/ppermute | solution.py:456
  111.4 8.0 %collective-permute-start.12 = (bf16[8,16,1024]{2,1,0:T(8,128)(2,1)S(1)}, bf16[8,16,1024]{2,1,0:T(8,128)(2,1)S(1)}, u32[]{:S(2)}, u32[]{:S(2)}) collective-permute-start(bf16[8,16,1024]{2,1,0:T(8,128)(2,1)S(1)} %grads.1.refs_0_), channel_id=1, source_target_pairs={{0,32},{32,64},{64,96},{96,0},{128,160},{160,192},{192,224},{224,1... | collective-permute-start | bytes 786440 | tf_op jit(solution)/shard_map/ppermute | solution.py:456
  111.4 10.0 %collective-permute-start.13 = (bf16[8,16,1024]{2,1,0:T(8,128)(2,1)S(1)}, bf16[8,16,1024]{2,1,0:T(8,128)(2,1)S(1)}, u32[]{:S(2)}, u32[]{:S(2)}) collective-permute-start(bf16[8,16,1024]{2,1,0:T(8,128)(2,1)S(1)} %grads.1.refs_0_), channel_id=1, source_target_pairs={{0,96},{32,0},{64,32},{96,64},{128,224},{160,128},{192,160},{224,1... | collective-permute-start | bytes 786440 | tf_op jit(solution)/shard_map/ppermute | solution.py:456
  116.7 7.6 %collective-permute-start.15 = (bf16[8,16,1024]{2,1,0:T(8,128)(2,1)S(1)}, bf16[8,16,1024]{2,1,0:T(8,128)(2,1)S(1)}, u32[]{:S(2)}, u32[]{:S(2)}) collective-permute-start(bf16[8,16,1024]{2,1,0:T(8,128)(2,1)S(1)} %collective-permute-done.11.refs_1_), channel_id=1, source_target_pairs={{0,96},{32,0},{64,32},{96,64},{128,224},{160,128},{192,160},{224,1... | collective-permute-start | bytes 786440 | tf_op jit(solution)/shard_map/ppermute | solution.py:456
  121.4 8.0 %collective-permute-start.16 = (bf16[8,16,1024]{2,1,0:T(8,128)(2,1)S(1)}, bf16[8,16,1024]{2,1,0:T(8,128)(2,1)S(1)}, u32[]{:S(2)}, u32[]{:S(2)}) collective-permute-start(bf16[8,16,1024]{2,1,0:T(8,128)(2,1)S(1)} %collective-permute-done.12.refs_2_), channel_id=1, source_target_pairs={{0,32},{32,64},{64,96},{96,0},{128,160},{160,192},{192,224},{224,1... | collective-permute-start | bytes 786440 | tf_op jit(solution)/shard_map/ppermute | solution.py:456
  121.4 10.8 %collective-permute-start.14 = (bf16[8,16,1024]{2,1,0:T(8,128)(2,1)S(1)}, bf16[8,16,1024]{2,1,0:T(8,128)(2,1)S(1)}, u32[]{:S(2)}, u32[]{:S(2)}) collective-permute-start(bf16[8,16,1024]{2,1,0:T(8,128)(2,1)S(1)} %collective-permute-done.11.refs_1_), channel_id=1, source_target_pairs={{0,32},{32,64},{64,96},{96,0},{128,160},{160,192},{192,224},{224,1... | collective-permute-start | bytes 786440 | tf_op jit(solution)/shard_map/ppermute | solution.py:456
  124.2 8.0 %collective-permute-start.17 = (bf16[8,16,1024]{2,1,0:T(8,128)(2,1)S(1)}, bf16[8,16,1024]{2,1,0:T(8,128)(2,1)S(1)}, u32[]{:S(2)}, u32[]{:S(2)}) collective-permute-start(bf16[8,16,1024]{2,1,0:T(8,128)(2,1)S(1)} %collective-permute-done.15.refs_5_), channel_id=1, source_target_pairs={{0,96},{32,0},{64,32},{96,64},{128,224},{160,128},{192,160},{224,1... | collective-permute-start | bytes 786440 | tf_op jit(solution)/shard_map/ppermute | solution.py:456
  135.2 2.9 %collective-permute-start.19 = (bf16[256,1664]{1,0:T(8,128)(2,1)S(1)}, bf16[256,1664]{1,0:T(8,128)(2,1)S(1)}, u32[]{:S(2)}, u32[]{:S(2)}) collective-permute-start(bf16[256,1664]{1,0:T(8,128)(2,1)S(1)} %give1.1), channel_id=1, source_target_pairs={{0,1},{1,0},{2,3},{3,2},{4,5},{5,4},{6,7},{7,6},{8,9},{9,8},{10,11... | collective-permute-start | bytes 2555912 | tf_op jit(solution)/shard_map/ppermute | solution.py:501
  135.3 3.6 %collective-permute-start.18 = (bf16[256,1664]{1,0:T(8,128)(2,1)S(1)}, bf16[256,1664]{1,0:T(8,128)(2,1)S(1)}, u32[]{:S(2)}, u32[]{:S(2)}) collective-permute-start(bf16[256,1664]{1,0:T(8,128)(2,1)S(1)} %give0.1), channel_id=1, source_target_pairs={{0,1},{1,0},{2,3},{3,2},{4,5},{5,4},{6,7},{7,6},{8,9},{9,8},{10,11... | collective-permute-start | bytes 2555912 | tf_op jit(solution)/shard_map/ppermute | solution.py:501
  140.3 30.8 %copy-start = (f32[32,12800]{1,0:T(8,128)S(1)}, f32[32,12800]{1,0:T(8,128)}, u32[]{:S(2)}) copy-start(f32[32,12800]{1,0:T(8,128)} %get-tuple-element.63.hat_ref) | copy-start | bytes 4915204
  140.3 30.8 %copy-start.7 = (f32[12800]{0:T(1024)S(1)}, f32[12800]{0:T(1024)}, u32[]{:S(2)}) copy-start(f32[12800]{0:T(1024)} %gain_ref.3) | copy-start | bytes 153604
  140.3 30.8 %copy-start.8 = (f32[32,128]{1,0:T(8,128)S(1)}, f32[32,128]{1,0:T(8,128)}, u32[]{:S(2)}) copy-start(f32[32,128]{1,0:T(8,128)} %get-tuple-element.48.inv_ref) | copy-start | bytes 49156
  140.3 30.8 %all-to-all-start.2 = ((bf16[16,32,1664]{2,1,0:T(8,128)(2,1)}), bf16[16,32,1664]{2,1,0:T(8,128)(2,1)S(1)}, u32[]{:S(2)}, u32[]{:S(2)}) async-start(bf16[16,32,1664]{2,1,0:T(8,128)(2,1)} %join.1), calls=%async_computation.2 | async-start | bytes 3407872 | tf_op jit(solution)/shard_map/all_to_all | solution.py:514
  146.5 0.9 copy-start.2
  147.5 0.9 copy-start.4

commit v7 on v6

--- a/solution.py
+++ b/solution.py
@@ -53,7 +53,7 @@
 
 
 def norm_kernel(
-    chunk, own_slots, section_slots, along, slot_ref, core_ref, rows_ref, gain_ref, bias_ref, out_ref, held, sems
+    chunk, own_slots, section_slots, along, slot_ref, core_ref, rows_ref, gain_ref, bias_ref, out_ref, held, made, sems, out_sems
 ):
     parts, high, padded = out_ref.shape
     half = high // UNIT
@@ -85,9 +85,12 @@
         note = jnp.where(lane == 0, run, jnp.where(lane == 1, live, spot)).astype(F32).astype(BF)
         for k in range(parts):
             at = (k % 2 * (parts // 2) + k // 2) * chunk
-            out_ref[k, i * UNIT : (i + 1) * UNIT] = jnp.concatenate(
-                [normed[:, at : at + chunk], note], axis=1
-            )
+            made[i, k] = jnp.concatenate([normed[:, at : at + chunk], note], axis=1)
+        target = out_ref.at[:, pl.ds(i * UNIT, UNIT)]
+        copies.append(pltpu.make_async_copy(made.at[i], target, out_sems.at[i]))
+        copies[-1].start()
+    for copy in copies[half:]:
+        copy.wait()
 
 
 def forward_kernel(tile_ref, rows_ref, weight_ref, out_ref, window_ref, note_ref):
@@ -105,13 +108,22 @@
         note_ref[j] = jnp.concatenate([head.astype(F32) for head in heads], axis=0)
 
 
-def tail_kernel(core_ref, own_window_ref, other_window_ref, weight_ref, own_ref, other_ref, out_ref):
+def tail_kernel(
+    core_ref, own_window_ref, other_window_ref, weight_ref, own_ref, other_ref, out_ref, made, sems
+):
     half = own_ref.shape[0]
     halves = ((core_ref[0], own_window_ref, own_ref), (1 - core_ref[0], other_window_ref, other_ref))
+    copies = []
     for side, window_ref, main_ref in halves:
         for j in range(half):
+            n = len(copies)
             product = jnp.dot(window_ref[j], weight_ref[...], preferred_element_type=F32)
-            out_ref[side * half + j] = (main_ref[j] + product).astype(BF)
+            made[n] = (main_ref[j] + product).astype(BF)
+            target = out_ref.at[side * half + j]
+            copies.append(pltpu.make_async_copy(made.at[n], target, sems.at[n]))
+            copies[n].start()
+    for copy in copies:
+        copy.wait()
 
 
 def prepare_kernel(text_ref, cot_ref, gain_ref, upstream_ref, stat_ref):
@@ -314,8 +326,13 @@
         functools.partial(norm_kernel, chunk, slots, slots * groups, along),
         out_shape=pltpu.HBM((sections, half * UNIT, padded), BF),
         in_specs=[SMEM, SMEM, ANY, VMEM, VMEM],
-        out_specs=VMEM,
-        scratch_shapes=[pltpu.VMEM((half, UNIT, depth), BF), pltpu.SemaphoreType.DMA((half,))],
+        out_specs=ANY,
+        scratch_shapes=[
+            pltpu.VMEM((half, UNIT, depth), BF),
+            pltpu.VMEM((half, sections, UNIT, padded), BF),
+            pltpu.SemaphoreType.DMA((half,)),
+            pltpu.SemaphoreType.DMA((half,)),
+        ],
         compiler_params=WIDE,
         cost_estimate=FREE,
         name="vision_norm",
@@ -365,7 +382,11 @@
         tail_kernel,
         out_shape=pltpu.HBM((units, sections * UNIT, columns), BF),
         in_specs=[SMEM] + [VMEM] * 5,
-        out_specs=VMEM,
+        out_specs=ANY,
+        scratch_shapes=[
+            pltpu.VMEM((units, sections * UNIT, columns), BF),
+            pltpu.SemaphoreType.DMA((units,)),
+        ],
         compiler_params=PARAMS,
         cost_estimate=FREE,
         name="tail",

time: 174 us -> 173 us (level)
  transfers between devices with their start and end apart: 23 -> 23, of which waited for: 17 -> 17; matrix products, arithmetic and copies ran while one was open for 5% -> 5% of each run, Pallas kernels for 12% -> 11%
where the time goes in v7:
time: 173 us; the launch traced here: 172 us
  waiting for transfers between devices  78.9 us (46%)
  starting transfers between devices  46.7 us (27%)
  Pallas kernels  31.4 us (18%)
  local copies, waits for them, and re-layouts  13.4 us (8%)
    all_to_all x1, waiting for transfers between devices, shards(): partial = lax.all_to_all(partial, along_first, 0, 0, tiled=True)  21.8 us
    all_to_all x1, waiting for transfers between devices, shards(): back = lax.all_to_all(total, ('x', 'y_hi', 'y_lo'), 0, 0, tiled=True)  21.1 us
    ppermute x3, waiting for transfers between devices, ring_gather(): rising = lax.ppermute(rising, ring, up)  18.8 us
    ppermute x7, waiting for transfers between devices, turn(): return lax.ppermute(block, ('y_lo', 'x'), moves)  11.9 us
    ppermute x7, starting transfers between devices, turn(): return lax.ppermute(block, ('y_lo', 'x'), moves)  11.3 us
    ppermute x3, starting transfers between devices, ring_gather(): falling = lax.ppermute(falling, ring, down)  11 us
    pallas_call x2, Pallas kernels, forward(): pl.pallas_call(forward_kernel, out_shape=(shape((half, sections * UNIT, c...  6.85 us
    dynamic_update_slice x7, local copies, waits for them, and re-layouts, put(): lax.dynamic_update_slice_in_dim(out, piece, owner % groups * height, 0)  6.23 us
  transfers between devices with their start and end apart: 23, of which 17 were waited for; matrix products, arithmetic and copies ran while one was open for 5% of the time, Pallas kernels for 11%

profile of v7, /device:TPU:8, one launch (start us, length us, event | category | flops | bytes accessed | tf_op | source)
XLA Modules:
  0.0 172.5 jit_solution(12713685562742764453)
XLA Ops:
  0.6 2.0 %collective-permute-start = (bf16[200,1024]{1,0:T(8,128)(2,1)}, bf16[200,1024]{1,0:T(8,128)(2,1)}, u32[]{:S(2)}, u32[]{:S(2)}) collective-permute-start(bf16[200,1024]{1,0:T(8,128)(2,1)} %param.13), channel_id=1, source_target_pairs={{0,4},{1,29},{4,8},{5,1},{8,12},{9,5},{12,16},{13,9},{16,20},{17,1... | collective-permute-start | bytes 1228808 | tf_op jit(solution)/shard_map/ppermute | solution.py:270
  2.6 4.0 %collective-permute-start.1 = (bf16[200,1024]{1,0:T(8,128)(2,1)}, bf16[200,1024]{1,0:T(8,128)(2,1)}, u32[]{:S(2)}, u32[]{:S(2)}) collective-permute-start(bf16[200,1024]{1,0:T(8,128)(2,1)} %param.13), channel_id=1, source_target_pairs={{4,0},{29,1},{8,4},{1,5},{12,8},{5,9},{16,12},{9,13},{20,16},{13,1... | collective-permute-start | bytes 1228808 | tf_op jit(solution)/shard_map/ppermute | solution.py:271
  6.7 5.3 %vision_norm.1 = bf16[8,64,1664]{2,1,0:T(8,128)(2,1)} custom-call(s32[128]{0:T(128)} %slot_ref.1, s32[1]{0:T(128)} %bitcast.1.core_ref, bf16[128,12800]{1,0:T(8,128)(2,1)} %rows_ref.3, f32[12800]{0:T(1024)} %gain_ref.3, f32[12800]{0:T(1024)} %bias_ref.1), custom_call_target="tpu_custom_call" | custom-call | tf_op jit(solution)/shard_map/vision_norm/pallas_call | solution.py:325
  11.9 0.4 broadcast_in_dim.45
  12.4 2.9 %collective-permute-done = bf16[200,1024]{1,0:T(8,128)(2,1)} collective-permute-done((bf16[200,1024]{1,0:T(8,128)(2,1)}, bf16[200,1024]{1,0:T(8,128)(2,1)}, u32[]{:S(2)}, u32[]{:S(2)}) %collective-permute-start) | collective-permute-done | bytes 409632 | tf_op jit(solution)/shard_map/ppermute | solution.py:270
  15.3 0.3 collective-permute-done.1
  15.6 5.8 %all-to-all-start = ((bf16[8,64,1664]{2,1,0:T(8,128)(2,1)}), bf16[8,64,1664]{2,1,0:T(8,128)(2,1)}, u32[]{:S(2)}, u32[]{:S(2)}) async-start(bf16[8,64,1664]{2,1,0:T(8,128)(2,1)} %vision_norm.1), calls=%async_computation | async-start | bytes 3407872 | tf_op jit(solution)/shard_map/all_to_all | solution.py:341
  21.4 3.7 %collective-permute-start.3 = (bf16[200,1024]{1,0:T(8,128)(2,1)}, bf16[200,1024]{1,0:T(8,128)(2,1)}, u32[]{:S(2)}, u32[]{:S(2)}) collective-permute-start(bf16[200,1024]{1,0:T(8,128)(2,1)} %collective-permute-done.1), channel_id=1, source_target_pairs={{4,0},{29,1},{8,4},{1,5},{12,8},{5,9},{16,12},{9,13},{20,16},{13,1... | collective-permute-start | bytes 1228808 | tf_op jit(solution)/shard_map/ppermute | solution.py:271
  25.1 1.0 constant_dynamic-update-slice_fusion.7
  26.1 1.0 constant_dynamic-update-slice_fusion.6
  27.1 7.9 %collective-permute-done.2 = bf16[200,1024]{1,0:T(8,128)(2,1)} collective-permute-done((bf16[200,1024]{1,0:T(8,128)(2,1)}, bf16[200,1024]{1,0:T(8,128)(2,1)}, u32[]{:S(2)}, u32[]{:S(2)}) %collective-permute-start.2) | collective-permute-done | bytes 409632 | tf_op jit(solution)/shard_map/ppermute | solution.py:270
  35.0 3.2 %collective-permute-start.5 = (bf16[200,1024]{1,0:T(8,128)(2,1)}, bf16[200,1024]{1,0:T(8,128)(2,1)}, u32[]{:S(2)}, u32[]{:S(2)}) collective-permute-start(bf16[200,1024]{1,0:T(8,128)(2,1)} %collective-permute-done.3), channel_id=1, source_target_pairs={{4,0},{29,1},{8,4},{1,5},{12,8},{5,9},{16,12},{9,13},{20,16},{13,1... | collective-permute-start | bytes 1228808 | tf_op jit(solution)/shard_map/ppermute | solution.py:271
  38.2 1.0 constant_dynamic-update-slice_fusion.5
  39.3 1.0 constant_dynamic-update-slice_fusion.4
  40.3 8.1 %collective-permute-done.4 = bf16[200,1024]{1,0:T(8,128)(2,1)} collective-permute-done((bf16[200,1024]{1,0:T(8,128)(2,1)}, bf16[200,1024]{1,0:T(8,128)(2,1)}, u32[]{:S(2)}, u32[]{:S(2)}) %collective-permute-start.4) | collective-permute-done | bytes 409632 | tf_op jit(solution)/shard_map/ppermute | solution.py:270
  49.0 1.0 constant_dynamic-update-slice_fusion.3
  50.0 1.0 constant_dynamic-update-slice_fusion.2.weight_ref
  51.0 3.4 %forward_own.1 = (f32[4,128,1024]{2,1,0:T(8,128)S(1)}, bf16[4,128,384]{2,1,0:T(8,128)(2,1)S(1)}, f32[4,8,128]{2,1,0:T(8,128)S(1)}) custom-call(s32[1]{0:T(128)} %bitcast.tile_ref, bf16[8,64,1664]{2,1,0:T(8,128)(2,1)} %all-to-all-done.rows_ref, bf16[1664,1024]{1,0:T(8,128)(2,1)S(1)} %constant_dynamic-update-slice_fusion.2.weight_ref), custom_call_target="tpu_custom_call" | custom-call | tf_op jit(solution)/shard_map/forward_own/pallas_call | solution.py:351
  54.5 3.4 %forward_other.1 = (f32[4,128,1024]{2,1,0:T(8,128)S(1)}, bf16[4,128,384]{2,1,0:T(8,128)(2,1)S(1)}, f32[4,8,128]{2,1,0:T(8,128)S(1)}) custom-call(s32[1]{0:T(128)} %bitcast.tile_ref, bf16[8,64,1664]{2,1,0:T(8,128)(2,1)} %collective-permute-done.6.rows_ref, bf16[1664,1024]{1,0:T(8,128)(2,1)S(1)} %constant_dynamic-update-slice_fusion.2.weight_ref), custom_call_target="tpu_custom_call" | custom-call | tf_op jit(solution)/shard_map/forward_other/pallas_call | solution.py:351
  57.9 0.3 collective-permute-done.7
  58.4 2.0 %tail.1 = bf16[8,128,1024]{2,1,0:T(8,128)(2,1)} custom-call(s32[1]{0:T(128)} %bitcast.1.core_ref, bf16[4,128,384]{2,1,0:T(8,128)(2,1)S(1)} %get-tuple-element.50.own_window_ref, bf16[4,128,384]{2,1,0:T(8,128)(2,1)S(1)} %get-tuple-element.51.other_window_ref, bf16[384,1024]{1,0:T(8,128)(2,1)S(1)} %get-tuple-element.65.weight_ref, ...), custom_call_target="tpu_custom_call" | custom-call | tf_op jit(solution)/shard_map/tail/pallas_call | solution.py:381
  60.5 6.0 %all-to-all-start.1 = ((bf16[8,128,1024]{2,1,0:T(8,128)(2,1)}), bf16[8,128,1024]{2,1,0:T(8,128)(2,1)}, u32[]{:S(2)}, u32[]{:S(2)}) async-start(bf16[8,128,1024]{2,1,0:T(8,128)(2,1)} %tail.1), calls=%async_computation.1 | async-start | bytes 4194304 | tf_op jit(solution)/shard_map/all_to_all | solution.py:394
  66.6 0.2 slice_reduce_fusion
  66.8 0.4 copy-done.11
  67.2 2.8 %vision_hat.1 = (f32[32,12800]{1,0:T(8,128)}, f32[32,128]{1,0:T(8,128)}) custom-call(s32[1]{0:T(128)} %bitcast.9.first_ref, s32[8,8,3]{2,1,0:T(8,128)} %bitcast.25, bf16[128,12800]{1,0:T(8,128)(2,1)} %rows_ref.3), custom_call_target="tpu_custom_call" | custom-call | tf_op jit(solution)/shard_map/vision_hat/pallas_call | solution.py:420
  70.0 0.2 select_reduce_fusion
  70.3 0.8 constant_dynamic-slice_fusion
  71.3 0.2 reduce-window.16
  71.7 0.2 select_reduce_fusion.1
  71.9 0.9 copy-done.1
  72.8 0.9 copy-done.6
  73.8 0.9 prepare.1
  74.7 21.8 %all-to-all-done.1.parts_ref = bf16[8,128,1024]{2,1,0:T(8,128)(2,1)} async-done(((bf16[8,128,1024]{2,1,0:T(8,128)(2,1)}), bf16[8,128,1024]{2,1,0:T(8,128)(2,1)}, u32[]{:S(2)}, u32[]{:S(2)}) %all-to-all-start.1) | async-done | bytes 2097184 | tf_op jit(solution)/shard_map/all_to_all | solution.py:394
  96.5 1.0 copy-done.5
  97.5 2.3 %slots.1 = (bf16[128,1024]{1,0:T(8,128)(2,1)S(1)}, f32[128,1024]{1,0:T(8,128)S(1)}, f32[128,1024]{1,0:T(8,128)S(1)}, f32[8,128]{1,0:T(8,128)S(1)}) custom-call(s32[8]{0:T(128)S(1)} %fusion.9.place_ref, bf16[8,128,1024]{2,1,0:T(8,128)(2,1)} %all-to-all-done.1.parts_ref, f32[128,1024]{1,0:T(8,128)S(1)} %copy-done.5, f32[8,128]{1,0:T(8,128)S(1)} %get-tuple-element.56.text_stat_ref), custom_call_target="tpu_custom_call" | custom-call | tf_op jit(solution)/shard_map/slots/pallas_call | solution.py:445
  99.9 1.0 collective-permute-start.10
  100.9 1.5 collective-permute-start.8
  102.4 1.2 collective-permute-start.9
  103.6 0.9 collective-permute-done.10.refs_3_
  104.5 3.0 %collective-permute-done.9.refs_2_ = f32[8,128]{1,0:T(8,128)S(1)} collective-permute-done((f32[8,128]{1,0:T(8,128)S(1)}, f32[8,128]{1,0:T(8,128)S(1)}, u32[]{:S(2)}, u32[]{:S(2)}) %collective-permute-start.9) | collective-permute-done | bytes 4128 | tf_op jit(solution)/shard_map/ppermute | solution.py:461
  107.5 0.9 grads.1.refs_0_
  108.4 2.3 %collective-permute-start.11 = (bf16[8,16,1024]{2,1,0:T(8,128)(2,1)S(1)}, bf16[8,16,1024]{2,1,0:T(8,128)(2,1)S(1)}, u32[]{:S(2)}, u32[]{:S(2)}) collective-permute-start(bf16[8,16,1024]{2,1,0:T(8,128)(2,1)S(1)} %grads.1.refs_0_), channel_id=1, source_target_pairs={{0,128},{32,160},{64,192},{96,224},{128,0},{160,32},{192,64},{224,... | collective-permute-start | bytes 786440 | tf_op jit(solution)/shard_map/ppermute | solution.py:477
  110.7 3.2 %collective-permute-start.13 = (bf16[8,16,1024]{2,1,0:T(8,128)(2,1)S(1)}, bf16[8,16,1024]{2,1,0:T(8,128)(2,1)S(1)}, u32[]{:S(2)}, u32[]{:S(2)}) collective-permute-start(bf16[8,16,1024]{2,1,0:T(8,128)(2,1)S(1)} %grads.1.refs_0_), channel_id=1, source_target_pairs={{0,96},{32,0},{64,32},{96,64},{128,224},{160,128},{192,160},{224,1... | collective-permute-start | bytes 786440 | tf_op jit(solution)/shard_map/ppermute | solution.py:477
  114.0 2.1 %collective-permute-done.11.refs_1_ = bf16[8,16,1024]{2,1,0:T(8,128)(2,1)S(1)} collective-permute-done((bf16[8,16,1024]{2,1,0:T(8,128)(2,1)S(1)}, bf16[8,16,1024]{2,1,0:T(8,128)(2,1)S(1)}, u32[]{:S(2)}, u32[]{:S(2)}) %collective-permute-start.11) | collective-permute-done | bytes 262176 | tf_op jit(solution)/shard_map/ppermute | solution.py:477
  116.2 2.5 %collective-permute-done.12.refs_2_ = bf16[8,16,1024]{2,1,0:T(8,128)(2,1)S(1)} collective-permute-done((bf16[8,16,1024]{2,1,0:T(8,128)(2,1)S(1)}, bf16[8,16,1024]{2,1,0:T(8,128)(2,1)S(1)}, u32[]{:S(2)}, u32[]{:S(2)}) %collective-permute-start.12) | collective-permute-done | bytes 262176 | tf_op jit(solution)/shard_map/ppermute | solution.py:477
  118.7 2.0 %collective-permute-done.13.refs_4_ = bf16[8,16,1024]{2,1,0:T(8,128)(2,1)S(1)} collective-permute-done((bf16[8,16,1024]{2,1,0:T(8,128)(2,1)S(1)}, bf16[8,16,1024]{2,1,0:T(8,128)(2,1)S(1)}, u32[]{:S(2)}, u32[]{:S(2)}) %collective-permute-start.13) | collective-permute-done | bytes 262176 | tf_op jit(solution)/shard_map/ppermute | solution.py:477
  120.7 1.9 %collective-permute-start.14 = (bf16[8,16,1024]{2,1,0:T(8,128)(2,1)S(1)}, bf16[8,16,1024]{2,1,0:T(8,128)(2,1)S(1)}, u32[]{:S(2)}, u32[]{:S(2)}) collective-permute-start(bf16[8,16,1024]{2,1,0:T(8,128)(2,1)S(1)} %collective-permute-done.11.refs_1_), channel_id=1, source_target_pairs={{0,32},{32,64},{64,96},{96,0},{128,160},{160,192},{192,224},{224,1... | collective-permute-start | bytes 786440 | tf_op jit(solution)/shard_map/ppermute | solution.py:477
  122.6 1.0 collective-permute-done.15.refs_5_
  123.6 3.7 %collective-permute-start.17 = (bf16[8,16,1024]{2,1,0:T(8,128)(2,1)S(1)}, bf16[8,16,1024]{2,1,0:T(8,128)(2,1)S(1)}, u32[]{:S(2)}, u32[]{:S(2)}) collective-permute-start(bf16[8,16,1024]{2,1,0:T(8,128)(2,1)S(1)} %collective-permute-done.15.refs_5_), channel_id=1, source_target_pairs={{0,96},{32,0},{64,32},{96,64},{128,224},{160,128},{192,160},{224,1... | collective-permute-start | bytes 786440 | tf_op jit(solution)/shard_map/ppermute | solution.py:477
  127.3 1.5 collective-permute-done.16.refs_6_
  128.8 2.8 %collective-permute-done.14.refs_3_ = bf16[8,16,1024]{2,1,0:T(8,128)(2,1)S(1)} collective-permute-done((bf16[8,16,1024]{2,1,0:T(8,128)(2,1)S(1)}, bf16[8,16,1024]{2,1,0:T(8,128)(2,1)S(1)}, u32[]{:S(2)}, u32[]{:S(2)}) %collective-permute-start.14) | collective-permute-done | bytes 262176 | tf_op jit(solution)/shard_map/ppermute | solution.py:477
  131.6 0.7 arrange.1.grads_ref
  132.3 1.1 give1.1
  133.4 1.1 give0.1
  134.7 0.5 collective-permute-start.18
  135.2 2.3 %keep.1.own_ref = f32[512,1664]{1,0:T(8,128)S(1)} custom-call(bf16[64,16,1024]{2,1,0:T(8,128)(2,1)S(1)} %arrange.1.grads_ref, bf16[1664,1024]{1,0:T(8,128)(2,1)S(1)} %get-tuple-element.64.weight_ref), custom_call_target="tpu_custom_call" | custom-call | tf_op jit(solution)/shard_map/keep/pallas_call | solution.py:507
  137.5 0.8 collective-permute-done.18.low_ref
  138.3 1.4 join.1
  139.7 6.2 %all-to-all-start.2 = ((bf16[16,32,1664]{2,1,0:T(8,128)(2,1)}), bf16[16,32,1664]{2,1,0:T(8,128)(2,1)S(1)}, u32[]{:S(2)}, u32[]{:S(2)}) async-start(bf16[16,32,1664]{2,1,0:T(8,128)(2,1)} %join.1), calls=%async_computation.2 | async-start | bytes 3407872 | tf_op jit(solution)/shard_map/all_to_all | solution.py:535
  145.9 0.9 copy-done.2
  146.8 0.9 copy-done.4
  147.8 1.6 normed.1
  149.4 21.1 %all-to-all-done.2.parts_ref = bf16[16,32,1664]{2,1,0:T(8,128)(2,1)S(1)} async-done(((bf16[16,32,1664]{2,1,0:T(8,128)(2,1)}), bf16[16,32,1664]{2,1,0:T(8,128)(2,1)S(1)}, u32[]{:S(2)}, u32[]{:S(2)}) %all-to-all-start.2) | async-done | bytes 1703968 | tf_op jit(solution)/shard_map/all_to_all | solution.py:535
  170.5 2.0 %vision_back.1 = bf16[32,12800]{1,0:T(8,128)(2,1)} custom-call(bf16[16,32,1664]{2,1,0:T(8,128)(2,1)S(1)} %all-to-all-done.2.parts_ref, f32[32,12800]{1,0:T(8,128)S(1)} %copy-done, f32[32,128]{1,0:T(8,128)S(1)} %copy-done.8, f32[12800]{0:T(1024)S(1)} %copy-done.7), custom_call_target="tpu_custom_call" | custom-call | tf_op jit(solution)/shard_map/vision_back/pallas_call | solution.py:540
  (60 shorter events, 1.7 us)
Async XLA Ops:
  0.6 14.7 %collective-permute-start = (bf16[200,1024]{1,0:T(8,128)(2,1)}, bf16[200,1024]{1,0:T(8,128)(2,1)}, u32[]{:S(2)}, u32[]{:S(2)}) collective-permute-start(bf16[200,1024]{1,0:T(8,128)(2,1)} %param.13), channel_id=1, source_target_pairs={{0,4},{1,29},{4,8},{5,1},{8,12},{9,5},{12,16},{13,9},{16,20},{17,1... | collective-permute-start | bytes 1228808 | tf_op jit(solution)/shard_map/ppermute | solution.py:270
  2.6 13.0 %collective-permute-start.1 = (bf16[200,1024]{1,0:T(8,128)(2,1)}, bf16[200,1024]{1,0:T(8,128)(2,1)}, u32[]{:S(2)}, u32[]{:S(2)}) collective-permute-start(bf16[200,1024]{1,0:T(8,128)(2,1)} %param.13), channel_id=1, source_target_pairs={{4,0},{29,1},{8,4},{1,5},{12,8},{5,9},{16,12},{9,13},{20,16},{13,1... | collective-permute-start | bytes 1228808 | tf_op jit(solution)/shard_map/ppermute | solution.py:271
  6.7 5.7 %copy-start.10 = (bf16[200,1024]{1,0:T(8,128)(2,1)S(1)}, bf16[200,1024]{1,0:T(8,128)(2,1)}, u32[]{:S(2)}) copy-start(bf16[200,1024]{1,0:T(8,128)(2,1)} %param.13) | copy-start | bytes 1228804
  12.4 36.4 %copy-start.12 = (s32[8]{0:T(128)S(1)}, s32[8]{0:T(128)}, u32[]{:S(2)}) copy-start(s32[8]{0:T(128)} %constant.182.clone) | copy-start | bytes 100
  12.4 36.3 %copy-start.13 = (s32[8]{0:T(128)S(1)}, s32[8]{0:T(128)}, u32[]{:S(2)}) copy-start(s32[8]{0:T(128)} %constant.184) | copy-start | bytes 100
  15.6 32.9 %all-to-all-start = ((bf16[8,64,1664]{2,1,0:T(8,128)(2,1)}), bf16[8,64,1664]{2,1,0:T(8,128)(2,1)}, u32[]{:S(2)}, u32[]{:S(2)}) async-start(bf16[8,64,1664]{2,1,0:T(8,128)(2,1)} %vision_norm.1), calls=%async_computation | async-start | bytes 3407872 | tf_op jit(solution)/shard_map/all_to_all | solution.py:341
  21.4 13.6 %collective-permute-start.2 = (bf16[200,1024]{1,0:T(8,128)(2,1)}, bf16[200,1024]{1,0:T(8,128)(2,1)}, u32[]{:S(2)}, u32[]{:S(2)}) collective-permute-start(bf16[200,1024]{1,0:T(8,128)(2,1)} %collective-permute-done), channel_id=1, source_target_pairs={{0,4},{1,29},{4,8},{5,1},{8,12},{9,5},{12,16},{13,9},{16,20},{17,1... | collective-permute-start | bytes 1228808 | tf_op jit(solution)/shard_map/ppermute | solution.py:270
  21.4 13.6 %collective-permute-start.3 = (bf16[200,1024]{1,0:T(8,128)(2,1)}, bf16[200,1024]{1,0:T(8,128)(2,1)}, u32[]{:S(2)}, u32[]{:S(2)}) collective-permute-start(bf16[200,1024]{1,0:T(8,128)(2,1)} %collective-permute-done.1), channel_id=1, source_target_pairs={{4,0},{29,1},{8,4},{1,5},{12,8},{5,9},{16,12},{9,13},{20,16},{13,1... | collective-permute-start | bytes 1228808 | tf_op jit(solution)/shard_map/ppermute | solution.py:271
  35.0 13.4 %collective-permute-start.4 = (bf16[200,1024]{1,0:T(8,128)(2,1)}, bf16[200,1024]{1,0:T(8,128)(2,1)}, u32[]{:S(2)}, u32[]{:S(2)}) collective-permute-start(bf16[200,1024]{1,0:T(8,128)(2,1)} %collective-permute-done.2), channel_id=1, source_target_pairs={{0,4},{1,29},{4,8},{5,1},{8,12},{9,5},{12,16},{13,9},{16,20},{17,1... | collective-permute-start | bytes 1228808 | tf_op jit(solution)/shard_map/ppermute | solution.py:270
  35.0 13.4 %collective-permute-start.5 = (bf16[200,1024]{1,0:T(8,128)(2,1)}, bf16[200,1024]{1,0:T(8,128)(2,1)}, u32[]{:S(2)}, u32[]{:S(2)}) collective-permute-start(bf16[200,1024]{1,0:T(8,128)(2,1)} %collective-permute-done.3), channel_id=1, source_target_pairs={{4,0},{29,1},{8,4},{1,5},{12,8},{5,9},{16,12},{9,13},{20,16},{13,1... | collective-permute-start | bytes 1228808 | tf_op jit(solution)/shard_map/ppermute | solution.py:271
  48.5 6.0 %collective-permute-start.6 = (bf16[8,64,1664]{2,1,0:T(8,128)(2,1)}, bf16[8,64,1664]{2,1,0:T(8,128)(2,1)}, u32[]{:S(2)}, u32[]{:S(2)}) collective-permute-start(bf16[8,64,1664]{2,1,0:T(8,128)(2,1)} %all-to-all-done.rows_ref), channel_id=1, source_target_pairs={{0,1},{1,0},{2,3},{3,2},{4,5},{5,4},{6,7},{7,6},{8,9},{9,8},{10,11... | collective-permute-start | bytes 5111816 | tf_op jit(solution)/shard_map/ppermute | solution.py:343
  48.8 9.5 %collective-permute-start.7 = (bf16[200,1024]{1,0:T(8,128)(2,1)}, bf16[200,1024]{1,0:T(8,128)(2,1)S(1)}, u32[]{:S(2)}, u32[]{:S(2)}) collective-permute-start(bf16[200,1024]{1,0:T(8,128)(2,1)} %collective-permute-done.4), channel_id=1, source_target_pairs={{0,4},{1,29},{4,8},{5,1},{8,12},{9,5},{12,16},{13,9},{16,20},{17,1... | collective-permute-start | bytes 1228808 | tf_op jit(solution)/shard_map/ppermute | solution.py:277
  60.5 11.4 %copy-start.9 = (f32[1024]{0:T(1024)S(1)}, f32[1024]{0:T(1024)}, u32[]{:S(2)}) copy-start(f32[1024]{0:T(1024)} %param.15) | copy-start | bytes 12292
  60.5 36.0 %all-to-all-start.1 = ((bf16[8,128,1024]{2,1,0:T(8,128)(2,1)}), bf16[8,128,1024]{2,1,0:T(8,128)(2,1)}, u32[]{:S(2)}, u32[]{:S(2)}) async-start(bf16[8,128,1024]{2,1,0:T(8,128)(2,1)} %tail.1), calls=%async_computation.1 | async-start | bytes 4194304 | tf_op jit(solution)/shard_map/all_to_all | solution.py:394
  66.6 0.6 copy-start.11
  71.9 1.0 copy-start.1
  72.8 0.9 copy-start.6
  96.5 1.0 copy-start.5
  99.9 33.6 %copy-start.3 = (bf16[128,1024]{1,0:T(8,128)(2,1)}, bf16[128,1024]{1,0:T(8,128)(2,1)S(1)}, u32[]{:S(2)}) copy-start(bf16[128,1024]{1,0:T(8,128)(2,1)S(1)} %get-tuple-element.57.feature_ref) | copy-start | bytes 786436
  99.9 4.6 %collective-permute-start.10 = (f32[8,128]{1,0:T(8,128)S(1)}, f32[8,128]{1,0:T(8,128)S(1)}, u32[]{:S(2)}, u32[]{:S(2)}) collective-permute-start(f32[8,128]{1,0:T(8,128)S(1)} %get-tuple-element.58.refs_0_), channel_id=1, source_target_pairs={{0,3},{1,2},{2,1},{3,0},{4,7},{5,6},{6,5},{7,4},{8,11},{9,10},{10,... | collective-permute-start | bytes 12296 | tf_op jit(solution)/shard_map/ppermute | solution.py:461
  100.9 3.6 %collective-permute-start.8 = (f32[8,128]{1,0:T(8,128)S(1)}, f32[8,128]{1,0:T(8,128)S(1)}, u32[]{:S(2)}, u32[]{:S(2)}) collective-permute-start(f32[8,128]{1,0:T(8,128)S(1)} %get-tuple-element.58.refs_0_), channel_id=1, source_target_pairs={{0,1},{1,0},{2,3},{3,2},{4,5},{5,4},{6,7},{7,6},{8,9},{9,8},{10,11... | collective-permute-start | bytes 12296 | tf_op jit(solution)/shard_map/ppermute | solution.py:461
  102.4 5.1 %collective-permute-start.9 = (f32[8,128]{1,0:T(8,128)S(1)}, f32[8,128]{1,0:T(8,128)S(1)}, u32[]{:S(2)}, u32[]{:S(2)}) collective-permute-start(f32[8,128]{1,0:T(8,128)S(1)} %get-tuple-element.58.refs_0_), channel_id=1, source_target_pairs={{0,2},{1,3},{2,0},{3,1},{4,6},{5,7},{6,4},{7,5},{8,10},{9,11},{10,... | collective-permute-start | bytes 12296 | tf_op jit(solution)/shard_map/ppermute | solution.py:461
  108.4 7.7 %collective-permute-start.11 = (bf16[8,16,1024]{2,1,0:T(8,128)(2,1)S(1)}, bf16[8,16,1024]{2,1,0:T(8,128)(2,1)S(1)}, u32[]{:S(2)}, u32[]{:S(2)}) collective-permute-start(bf16[8,16,1024]{2,1,0:T(8,128)(2,1)S(1)} %grads.1.refs_0_), channel_id=1, source_target_pairs={{0,128},{32,160},{64,192},{96,224},{128,0},{160,32},{192,64},{224,... | collective-permute-start | bytes 786440 | tf_op jit(solution)/shard_map/ppermute | solution.py:477
  110.7 8.0 %collective-permute-start.12 = (bf16[8,16,1024]{2,1,0:T(8,128)(2,1)S(1)}, bf16[8,16,1024]{2,1,0:T(8,128)(2,1)S(1)}, u32[]{:S(2)}, u32[]{:S(2)}) collective-permute-start(bf16[8,16,1024]{2,1,0:T(8,128)(2,1)S(1)} %grads.1.refs_0_), channel_id=1, source_target_pairs={{0,32},{32,64},{64,96},{96,0},{128,160},{160,192},{192,224},{224,1... | collective-permute-start | bytes 786440 | tf_op jit(solution)/shard_map/ppermute | solution.py:477
  110.7 10.0 %collective-permute-start.13 = (bf16[8,16,1024]{2,1,0:T(8,128)(2,1)S(1)}, bf16[8,16,1024]{2,1,0:T(8,128)(2,1)S(1)}, u32[]{:S(2)}, u32[]{:S(2)}) collective-permute-start(bf16[8,16,1024]{2,1,0:T(8,128)(2,1)S(1)} %grads.1.refs_0_), channel_id=1, source_target_pairs={{0,96},{32,0},{64,32},{96,64},{128,224},{160,128},{192,160},{224,1... | collective-permute-start | bytes 786440 | tf_op jit(solution)/shard_map/ppermute | solution.py:477
  116.1 7.6 %collective-permute-start.15 = (bf16[8,16,1024]{2,1,0:T(8,128)(2,1)S(1)}, bf16[8,16,1024]{2,1,0:T(8,128)(2,1)S(1)}, u32[]{:S(2)}, u32[]{:S(2)}) collective-permute-start(bf16[8,16,1024]{2,1,0:T(8,128)(2,1)S(1)} %collective-permute-done.11.refs_1_), channel_id=1, source_target_pairs={{0,96},{32,0},{64,32},{96,64},{128,224},{160,128},{192,160},{224,1... | collective-permute-start | bytes 786440 | tf_op jit(solution)/shard_map/ppermute | solution.py:477
  120.7 8.0 %collective-permute-start.16 = (bf16[8,16,1024]{2,1,0:T(8,128)(2,1)S(1)}, bf16[8,16,1024]{2,1,0:T(8,128)(2,1)S(1)}, u32[]{:S(2)}, u32[]{:S(2)}) collective-permute-start(bf16[8,16,1024]{2,1,0:T(8,128)(2,1)S(1)} %collective-permute-done.12.refs_2_), channel_id=1, source_target_pairs={{0,32},{32,64},{64,96},{96,0},{128,160},{160,192},{192,224},{224,1... | collective-permute-start | bytes 786440 | tf_op jit(solution)/shard_map/ppermute | solution.py:477
  120.7 10.8 %collective-permute-start.14 = (bf16[8,16,1024]{2,1,0:T(8,128)(2,1)S(1)}, bf16[8,16,1024]{2,1,0:T(8,128)(2,1)S(1)}, u32[]{:S(2)}, u32[]{:S(2)}) collective-permute-start(bf16[8,16,1024]{2,1,0:T(8,128)(2,1)S(1)} %collective-permute-done.11.refs_1_), channel_id=1, source_target_pairs={{0,32},{32,64},{64,96},{96,0},{128,160},{160,192},{192,224},{224,1... | collective-permute-start | bytes 786440 | tf_op jit(solution)/shard_map/ppermute | solution.py:477
  123.6 8.0 %collective-permute-start.17 = (bf16[8,16,1024]{2,1,0:T(8,128)(2,1)S(1)}, bf16[8,16,1024]{2,1,0:T(8,128)(2,1)S(1)}, u32[]{:S(2)}, u32[]{:S(2)}) collective-permute-start(bf16[8,16,1024]{2,1,0:T(8,128)(2,1)S(1)} %collective-permute-done.15.refs_5_), channel_id=1, source_target_pairs={{0,96},{32,0},{64,32},{96,64},{128,224},{160,128},{192,160},{224,1... | collective-permute-start | bytes 786440 | tf_op jit(solution)/shard_map/ppermute | solution.py:477
  134.6 2.9 %collective-permute-start.19 = (bf16[256,1664]{1,0:T(8,128)(2,1)S(1)}, bf16[256,1664]{1,0:T(8,128)(2,1)S(1)}, u32[]{:S(2)}, u32[]{:S(2)}) collective-permute-start(bf16[256,1664]{1,0:T(8,128)(2,1)S(1)} %give1.1), channel_id=1, source_target_pairs={{0,1},{1,0},{2,3},{3,2},{4,5},{5,4},{6,7},{7,6},{8,9},{9,8},{10,11... | collective-permute-start | bytes 2555912 | tf_op jit(solution)/shard_map/ppermute | solution.py:522
  134.7 3.6 %collective-permute-start.18 = (bf16[256,1664]{1,0:T(8,128)(2,1)S(1)}, bf16[256,1664]{1,0:T(8,128)(2,1)S(1)}, u32[]{:S(2)}, u32[]{:S(2)}) collective-permute-start(bf16[256,1664]{1,0:T(8,128)(2,1)S(1)} %give0.1), channel_id=1, source_target_pairs={{0,1},{1,0},{2,3},{3,2},{4,5},{5,4},{6,7},{7,6},{8,9},{9,8},{10,11... | collective-permute-start | bytes 2555912 | tf_op jit(solution)/shard_map/ppermute | solution.py:522
  139.7 30.8 %copy-start = (f32[32,12800]{1,0:T(8,128)S(1)}, f32[32,12800]{1,0:T(8,128)}, u32[]{:S(2)}) copy-start(f32[32,12800]{1,0:T(8,128)} %get-tuple-element.63.hat_ref) | copy-start | bytes 4915204
  139.7 30.8 %copy-start.7 = (f32[12800]{0:T(1024)S(1)}, f32[12800]{0:T(1024)}, u32[]{:S(2)}) copy-start(f32[12800]{0:T(1024)} %gain_ref.3) | copy-start | bytes 153604
  139.7 30.8 %copy-start.8 = (f32[32,128]{1,0:T(8,128)S(1)}, f32[32,128]{1,0:T(8,128)}, u32[]{:S(2)}) copy-start(f32[32,128]{1,0:T(8,128)} %get-tuple-element.48.inv_ref) | copy-start | bytes 49156
  139.7 30.8 %all-to-all-start.2 = ((bf16[16,32,1664]{2,1,0:T(8,128)(2,1)}), bf16[16,32,1664]{2,1,0:T(8,128)(2,1)S(1)}, u32[]{:S(2)}, u32[]{:S(2)}) async-start(bf16[16,32,1664]{2,1,0:T(8,128)(2,1)} %join.1), calls=%async_computation.2 | async-start | bytes 3407872 | tf_op jit(solution)/shard_map/all_to_all | solution.py:535
  145.9 0.9 copy-start.2
  146.8 0.9 copy-start.4

commit v8 on v7

--- a/solution.py
+++ b/solution.py
@@ -477,7 +477,8 @@
         return lax.ppermute(block, ("y_lo", "x"), moves)
 
     across = turn(grads, 0, 1)
-    left, right = lax.optimization_barrier((turn(grads, 1), turn(grads, -1)))
+    left, right = turn(grads, 1), turn(grads, -1)
+    across, right = lax.optimization_barrier((across, right))
     left_across, right_across = turn(across, 1), turn(across, -1)
     opposite, opposite_across = turn(left, 1), turn(right_across, -1)
     blocks = [grads, across, left, left_across, right, right_across, opposite, opposite_across]

time: 173 us -> 173 us (level)
  starting transfers between devices: 46.7 us -> 42.8 us
  waiting for transfers between devices: 78.9 us -> 81.8 us
    ppermute x7, waiting for transfers between devices: 11.9 us -> 15 us  [turn(): return lax.ppermute(block, ('y_lo', 'x'), moves)]
    ppermute x7, starting transfers between devices: 11.3 us -> 8.28 us  [turn(): return lax.ppermute(block, ('y_lo', 'x'), moves)]
  transfers between devices with their start and end apart: 23 -> 23, of which waited for: 17 -> 16; matrix products, arithmetic and copies ran while one was open for 5% -> 5% of each run, Pallas kernels for 11% -> 12%
where the time goes in v8:
time: 173 us; the launch traced here: 172 us
  waiting for transfers between devices  81.8 us (47%)
  starting transfers between devices  42.8 us (25%)
  Pallas kernels  31.7 us (18%)
  local copies, waits for them, and re-layouts  13.4 us (8%)
    all_to_all x1, waiting for transfers between devices, shards(): partial = lax.all_to_all(partial, along_first, 0, 0, tiled=True)  21.8 us
    all_to_all x1, waiting for transfers between devices, shards(): back = lax.all_to_all(total, ('x', 'y_hi', 'y_lo'), 0, 0, tiled=True)  20.8 us
    ppermute x3, waiting for transfers between devices, ring_gather(): rising = lax.ppermute(rising, ring, up)  18.8 us
    ppermute x7, waiting for transfers between devices, turn(): return lax.ppermute(block, ('y_lo', 'x'), moves)  15 us
    ppermute x3, starting transfers between devices, ring_gather(): falling = lax.ppermute(falling, ring, down)  11 us
    ppermute x7, starting transfers between devices, turn(): return lax.ppermute(block, ('y_lo', 'x'), moves)  8.28 us
    pallas_call x2, Pallas kernels, forward(): pl.pallas_call(forward_kernel, out_shape=(shape((half, sections * UNIT, c...  6.85 us
    dynamic_update_slice x7, local copies, waits for them, and re-layouts, put(): lax.dynamic_update_slice_in_dim(out, piece, owner % groups * height, 0)  6.23 us
  transfers between devices with their start and end apart: 23, of which 16 were waited for; matrix products, arithmetic and copies ran while one was open for 5% of the time, Pallas kernels for 12%

profile of v8, /device:TPU:8, one launch (start us, length us, event | category | flops | bytes accessed | tf_op | source)
XLA Modules:
  0.0 171.8 jit_solution(11392470812665660386)
XLA Ops:
  0.6 2.0 %collective-permute-start = (bf16[200,1024]{1,0:T(8,128)(2,1)}, bf16[200,1024]{1,0:T(8,128)(2,1)}, u32[]{:S(2)}, u32[]{:S(2)}) collective-permute-start(bf16[200,1024]{1,0:T(8,128)(2,1)} %param.13), channel_id=1, source_target_pairs={{0,4},{1,29},{4,8},{5,1},{8,12},{9,5},{12,16},{13,9},{16,20},{17,1... | collective-permute-start | bytes 1228808 | tf_op jit(solution)/shard_map/ppermute | solution.py:270
  2.6 4.0 %collective-permute-start.1 = (bf16[200,1024]{1,0:T(8,128)(2,1)}, bf16[200,1024]{1,0:T(8,128)(2,1)}, u32[]{:S(2)}, u32[]{:S(2)}) collective-permute-start(bf16[200,1024]{1,0:T(8,128)(2,1)} %param.13), channel_id=1, source_target_pairs={{4,0},{29,1},{8,4},{1,5},{12,8},{5,9},{16,12},{9,13},{20,16},{13,1... | collective-permute-start | bytes 1228808 | tf_op jit(solution)/shard_map/ppermute | solution.py:271
  6.7 5.3 %vision_norm.1 = bf16[8,64,1664]{2,1,0:T(8,128)(2,1)} custom-call(s32[128]{0:T(128)} %slot_ref.1, s32[1]{0:T(128)} %bitcast.1.core_ref, bf16[128,12800]{1,0:T(8,128)(2,1)} %rows_ref.3, f32[12800]{0:T(1024)} %gain_ref.3, f32[12800]{0:T(1024)} %bias_ref.1), custom_call_target="tpu_custom_call" | custom-call | tf_op jit(solution)/shard_map/vision_norm/pallas_call | solution.py:325
  11.9 0.4 broadcast_in_dim.45
  12.4 2.9 %collective-permute-done = bf16[200,1024]{1,0:T(8,128)(2,1)} collective-permute-done((bf16[200,1024]{1,0:T(8,128)(2,1)}, bf16[200,1024]{1,0:T(8,128)(2,1)}, u32[]{:S(2)}, u32[]{:S(2)}) %collective-permute-start) | collective-permute-done | bytes 409632 | tf_op jit(solution)/shard_map/ppermute | solution.py:270
  15.3 0.3 collective-permute-done.1
  15.6 5.8 %all-to-all-start = ((bf16[8,64,1664]{2,1,0:T(8,128)(2,1)}), bf16[8,64,1664]{2,1,0:T(8,128)(2,1)}, u32[]{:S(2)}, u32[]{:S(2)}) async-start(bf16[8,64,1664]{2,1,0:T(8,128)(2,1)} %vision_norm.1), calls=%async_computation | async-start | bytes 3407872 | tf_op jit(solution)/shard_map/all_to_all | solution.py:341
  21.4 3.7 %collective-permute-start.3 = (bf16[200,1024]{1,0:T(8,128)(2,1)}, bf16[200,1024]{1,0:T(8,128)(2,1)}, u32[]{:S(2)}, u32[]{:S(2)}) collective-permute-start(bf16[200,1024]{1,0:T(8,128)(2,1)} %collective-permute-done.1), channel_id=1, source_target_pairs={{4,0},{29,1},{8,4},{1,5},{12,8},{5,9},{16,12},{9,13},{20,16},{13,1... | collective-permute-start | bytes 1228808 | tf_op jit(solution)/shard_map/ppermute | solution.py:271
  25.1 1.0 constant_dynamic-update-slice_fusion.7
  26.1 1.0 constant_dynamic-update-slice_fusion.6
  27.1 7.9 %collective-permute-done.2 = bf16[200,1024]{1,0:T(8,128)(2,1)} collective-permute-done((bf16[200,1024]{1,0:T(8,128)(2,1)}, bf16[200,1024]{1,0:T(8,128)(2,1)}, u32[]{:S(2)}, u32[]{:S(2)}) %collective-permute-start.2) | collective-permute-done | bytes 409632 | tf_op jit(solution)/shard_map/ppermute | solution.py:270
  35.0 3.2 %collective-permute-start.5 = (bf16[200,1024]{1,0:T(8,128)(2,1)}, bf16[200,1024]{1,0:T(8,128)(2,1)}, u32[]{:S(2)}, u32[]{:S(2)}) collective-permute-start(bf16[200,1024]{1,0:T(8,128)(2,1)} %collective-permute-done.3), channel_id=1, source_target_pairs={{4,0},{29,1},{8,4},{1,5},{12,8},{5,9},{16,12},{9,13},{20,16},{13,1... | collective-permute-start | bytes 1228808 | tf_op jit(solution)/shard_map/ppermute | solution.py:271
  38.2 1.0 constant_dynamic-update-slice_fusion.5
  39.3 1.0 constant_dynamic-update-slice_fusion.4
  40.3 8.1 %collective-permute-done.4 = bf16[200,1024]{1,0:T(8,128)(2,1)} collective-permute-done((bf16[200,1024]{1,0:T(8,128)(2,1)}, bf16[200,1024]{1,0:T(8,128)(2,1)}, u32[]{:S(2)}, u32[]{:S(2)}) %collective-permute-start.4) | collective-permute-done | bytes 409632 | tf_op jit(solution)/shard_map/ppermute | solution.py:270
  49.0 1.0 constant_dynamic-update-slice_fusion.3
  50.0 1.0 constant_dynamic-update-slice_fusion.2.weight_ref
  51.0 3.4 %forward_own.1 = (f32[4,128,1024]{2,1,0:T(8,128)S(1)}, bf16[4,128,384]{2,1,0:T(8,128)(2,1)S(1)}, f32[4,8,128]{2,1,0:T(8,128)S(1)}) custom-call(s32[1]{0:T(128)} %bitcast.tile_ref, bf16[8,64,1664]{2,1,0:T(8,128)(2,1)} %all-to-all-done.rows_ref, bf16[1664,1024]{1,0:T(8,128)(2,1)S(1)} %constant_dynamic-update-slice_fusion.2.weight_ref), custom_call_target="tpu_custom_call" | custom-call | tf_op jit(solution)/shard_map/forward_own/pallas_call | solution.py:351
  54.5 3.4 %forward_other.1 = (f32[4,128,1024]{2,1,0:T(8,128)S(1)}, bf16[4,128,384]{2,1,0:T(8,128)(2,1)S(1)}, f32[4,8,128]{2,1,0:T(8,128)S(1)}) custom-call(s32[1]{0:T(128)} %bitcast.tile_ref, bf16[8,64,1664]{2,1,0:T(8,128)(2,1)} %collective-permute-done.6.rows_ref, bf16[1664,1024]{1,0:T(8,128)(2,1)S(1)} %constant_dynamic-update-slice_fusion.2.weight_ref), custom_call_target="tpu_custom_call" | custom-call | tf_op jit(solution)/shard_map/forward_other/pallas_call | solution.py:351
  57.9 0.3 collective-permute-done.7
  58.4 2.0 %tail.1 = bf16[8,128,1024]{2,1,0:T(8,128)(2,1)} custom-call(s32[1]{0:T(128)} %bitcast.1.core_ref, bf16[4,128,384]{2,1,0:T(8,128)(2,1)S(1)} %get-tuple-element.50.own_window_ref, bf16[4,128,384]{2,1,0:T(8,128)(2,1)S(1)} %get-tuple-element.51.other_window_ref, bf16[384,1024]{1,0:T(8,128)(2,1)S(1)} %get-tuple-element.65.weight_ref, ...), custom_call_target="tpu_custom_call" | custom-call | tf_op jit(solution)/shard_map/tail/pallas_call | solution.py:381
  60.5 6.0 %all-to-all-start.1 = ((bf16[8,128,1024]{2,1,0:T(8,128)(2,1)}), bf16[8,128,1024]{2,1,0:T(8,128)(2,1)}, u32[]{:S(2)}, u32[]{:S(2)}) async-start(bf16[8,128,1024]{2,1,0:T(8,128)(2,1)} %tail.1), calls=%async_computation.1 | async-start | bytes 4194304 | tf_op jit(solution)/shard_map/all_to_all | solution.py:394
  66.6 0.2 slice_reduce_fusion
  66.8 0.4 copy-done.11
  67.2 2.8 %vision_hat.1 = (f32[32,12800]{1,0:T(8,128)}, f32[32,128]{1,0:T(8,128)}) custom-call(s32[1]{0:T(128)} %bitcast.9.first_ref, s32[8,8,3]{2,1,0:T(8,128)} %bitcast.25, bf16[128,12800]{1,0:T(8,128)(2,1)} %rows_ref.3), custom_call_target="tpu_custom_call" | custom-call | tf_op jit(solution)/shard_map/vision_hat/pallas_call | solution.py:420
  70.0 0.2 select_reduce_fusion
  70.3 0.8 constant_dynamic-slice_fusion
  71.3 0.2 reduce-window.16
  71.7 0.2 select_reduce_fusion.1
  71.9 0.9 copy-done.1
  72.8 0.9 copy-done.6
  73.8 0.9 prepare.1
  74.7 21.8 %all-to-all-done.1.parts_ref = bf16[8,128,1024]{2,1,0:T(8,128)(2,1)} async-done(((bf16[8,128,1024]{2,1,0:T(8,128)(2,1)}), bf16[8,128,1024]{2,1,0:T(8,128)(2,1)}, u32[]{:S(2)}, u32[]{:S(2)}) %all-to-all-start.1) | async-done | bytes 2097184 | tf_op jit(solution)/shard_map/all_to_all | solution.py:394
  96.5 1.0 copy-done.5
  97.5 2.3 %slots.1 = (bf16[128,1024]{1,0:T(8,128)(2,1)S(1)}, f32[128,1024]{1,0:T(8,128)S(1)}, f32[128,1024]{1,0:T(8,128)S(1)}, f32[8,128]{1,0:T(8,128)S(1)}) custom-call(s32[8]{0:T(128)S(1)} %fusion.9.place_ref, bf16[8,128,1024]{2,1,0:T(8,128)(2,1)} %all-to-all-done.1.parts_ref, f32[128,1024]{1,0:T(8,128)S(1)} %copy-done.5, f32[8,128]{1,0:T(8,128)S(1)} %get-tuple-element.56.text_stat_ref), custom_call_target="tpu_custom_call" | custom-call | tf_op jit(solution)/shard_map/slots/pallas_call | solution.py:445
  99.9 1.0 collective-permute-start.10
  100.9 1.5 collective-permute-start.8
  102.4 1.2 collective-permute-start.9
  103.6 0.9 collective-permute-done.10.refs_3_
  104.5 3.0 %collective-permute-done.9.refs_2_ = f32[8,128]{1,0:T(8,128)S(1)} collective-permute-done((f32[8,128]{1,0:T(8,128)S(1)}, f32[8,128]{1,0:T(8,128)S(1)}, u32[]{:S(2)}, u32[]{:S(2)}) %collective-permute-start.9) | collective-permute-done | bytes 4128 | tf_op jit(solution)/shard_map/ppermute | solution.py:461
  107.5 0.9 grads.1.refs_0_
  108.4 2.3 %collective-permute-start.11 = (bf16[8,16,1024]{2,1,0:T(8,128)(2,1)S(1)}, bf16[8,16,1024]{2,1,0:T(8,128)(2,1)S(1)}, u32[]{:S(2)}, u32[]{:S(2)}) collective-permute-start(bf16[8,16,1024]{2,1,0:T(8,128)(2,1)S(1)} %grads.1.refs_0_), channel_id=1, source_target_pairs={{0,128},{32,160},{64,192},{96,224},{128,0},{160,32},{192,64},{224,... | collective-permute-start | bytes 786440 | tf_op jit(solution)/shard_map/ppermute | solution.py:477
  110.7 2.0 %collective-permute-start.13 = (bf16[8,16,1024]{2,1,0:T(8,128)(2,1)S(1)}, bf16[8,16,1024]{2,1,0:T(8,128)(2,1)S(1)}, u32[]{:S(2)}, u32[]{:S(2)}) collective-permute-start(bf16[8,16,1024]{2,1,0:T(8,128)(2,1)S(1)} %grads.1.refs_0_), channel_id=1, source_target_pairs={{0,32},{32,64},{64,96},{96,0},{128,160},{160,192},{192,224},{224,1... | collective-permute-start | bytes 786440 | tf_op jit(solution)/shard_map/ppermute | solution.py:477
  112.8 3.3 %collective-permute-done.11.refs_1_ = bf16[8,16,1024]{2,1,0:T(8,128)(2,1)S(1)} collective-permute-done((bf16[8,16,1024]{2,1,0:T(8,128)(2,1)S(1)}, bf16[8,16,1024]{2,1,0:T(8,128)(2,1)S(1)}, u32[]{:S(2)}, u32[]{:S(2)}) %collective-permute-start.11) | collective-permute-done | bytes 262176 | tf_op jit(solution)/shard_map/ppermute | solution.py:477
  116.1 1.5 collective-permute-done.12.refs_4_
  117.5 1.5 collective-permute-start.15
  119.0 0.5 collective-permute-start.14
  119.6 5.1 %collective-permute-done.15.refs_5_ = bf16[8,16,1024]{2,1,0:T(8,128)(2,1)S(1)} collective-permute-done((bf16[8,16,1024]{2,1,0:T(8,128)(2,1)S(1)}, bf16[8,16,1024]{2,1,0:T(8,128)(2,1)S(1)}, u32[]{:S(2)}, u32[]{:S(2)}) %collective-permute-start.15) | collective-permute-done | bytes 262176 | tf_op jit(solution)/shard_map/ppermute | solution.py:477
  124.7 1.9 %collective-permute-start.17 = (bf16[8,16,1024]{2,1,0:T(8,128)(2,1)S(1)}, bf16[8,16,1024]{2,1,0:T(8,128)(2,1)S(1)}, u32[]{:S(2)}, u32[]{:S(2)}) collective-permute-start(bf16[8,16,1024]{2,1,0:T(8,128)(2,1)S(1)} %collective-permute-done.15.refs_5_), channel_id=1, source_target_pairs={{0,96},{32,0},{64,32},{96,64},{128,224},{160,128},{192,160},{224,1... | collective-permute-start | bytes 786440 | tf_op jit(solution)/shard_map/ppermute | solution.py:477
  126.6 2.3 %collective-permute-done.14.refs_3_ = bf16[8,16,1024]{2,1,0:T(8,128)(2,1)S(1)} collective-permute-done((bf16[8,16,1024]{2,1,0:T(8,128)(2,1)S(1)}, bf16[8,16,1024]{2,1,0:T(8,128)(2,1)S(1)}, u32[]{:S(2)}, u32[]{:S(2)}) %collective-permute-start.14) | collective-permute-done | bytes 262176 | tf_op jit(solution)/shard_map/ppermute | solution.py:477
  128.9 2.8 %collective-permute-done.16.refs_6_ = bf16[8,16,1024]{2,1,0:T(8,128)(2,1)S(1)} collective-permute-done((bf16[8,16,1024]{2,1,0:T(8,128)(2,1)S(1)}, bf16[8,16,1024]{2,1,0:T(8,128)(2,1)S(1)}, u32[]{:S(2)}, u32[]{:S(2)}) %collective-permute-start.16) | collective-permute-done | bytes 262176 | tf_op jit(solution)/shard_map/ppermute | solution.py:477
  131.7 0.7 arrange.1.grads_ref
  132.4 1.1 give1.1
  133.6 1.1 give0.1
  134.8 0.5 collective-permute-start.18
  135.3 2.3 %keep.1.own_ref = f32[512,1664]{1,0:T(8,128)S(1)} custom-call(bf16[64,16,1024]{2,1,0:T(8,128)(2,1)S(1)} %arrange.1.grads_ref, bf16[1664,1024]{1,0:T(8,128)(2,1)S(1)} %get-tuple-element.64.weight_ref), custom_call_target="tpu_custom_call" | custom-call | tf_op jit(solution)/shard_map/keep/pallas_call | solution.py:508
  137.6 0.8 collective-permute-done.18.low_ref
  138.4 1.4 join.1
  139.8 5.4 %all-to-all-start.2 = ((bf16[16,32,1664]{2,1,0:T(8,128)(2,1)}), bf16[16,32,1664]{2,1,0:T(8,128)(2,1)S(1)}, u32[]{:S(2)}, u32[]{:S(2)}) async-start(bf16[16,32,1664]{2,1,0:T(8,128)(2,1)} %join.1), calls=%async_computation.2 | async-start | bytes 3407872 | tf_op jit(solution)/shard_map/all_to_all | solution.py:536
  145.2 0.9 copy-done.2
  146.1 0.9 copy-done.4
  147.1 1.9 %normed.1 = bf16[128,1024]{1,0:T(8,128)(2,1)} custom-call(s32[8]{0:T(128)S(1)} %fusion.9.place_ref, s32[8]{0:T(128)S(1)} %get-tuple-element.66.live_ref, bf16[128,1024]{1,0:T(8,128)(2,1)S(1)} %copy-done.2, bf16[128,1024]{1,0:T(8,128)(2,1)S(1)} %copy-done.4, f32[1,1024]{1,0:T(1,128)S(1)} %bitcast.23, f32[8,128]{1,0:T(8,128)S(1)} %get-tuple-element.58.refs_0_, ...), custom_call_target="tpu_custom_call" | custom-call | tf_op jit(solution)/shard_map/normed/pallas_call | solution.py:494
  149.0 20.8 %all-to-all-done.2.parts_ref = bf16[16,32,1664]{2,1,0:T(8,128)(2,1)S(1)} async-done(((bf16[16,32,1664]{2,1,0:T(8,128)(2,1)}), bf16[16,32,1664]{2,1,0:T(8,128)(2,1)S(1)}, u32[]{:S(2)}, u32[]{:S(2)}) %all-to-all-start.2) | async-done | bytes 1703968 | tf_op jit(solution)/shard_map/all_to_all | solution.py:536
  169.8 2.0 %vision_back.1 = bf16[32,12800]{1,0:T(8,128)(2,1)} custom-call(bf16[16,32,1664]{2,1,0:T(8,128)(2,1)S(1)} %all-to-all-done.2.parts_ref, f32[32,12800]{1,0:T(8,128)S(1)} %copy-done, f32[32,128]{1,0:T(8,128)S(1)} %copy-done.8, f32[12800]{0:T(1024)S(1)} %copy-done.7), custom_call_target="tpu_custom_call" | custom-call | tf_op jit(solution)/shard_map/vision_back/pallas_call | solution.py:541
  (60 shorter events, 1.5 us)
Async XLA Ops:
  0.6 14.7 %collective-permute-start = (bf16[200,1024]{1,0:T(8,128)(2,1)}, bf16[200,1024]{1,0:T(8,128)(2,1)}, u32[]{:S(2)}, u32[]{:S(2)}) collective-permute-start(bf16[200,1024]{1,0:T(8,128)(2,1)} %param.13), channel_id=1, source_target_pairs={{0,4},{1,29},{4,8},{5,1},{8,12},{9,5},{12,16},{13,9},{16,20},{17,1... | collective-permute-start | bytes 1228808 | tf_op jit(solution)/shard_map/ppermute | solution.py:270
  2.6 13.0 %collective-permute-start.1 = (bf16[200,1024]{1,0:T(8,128)(2,1)}, bf16[200,1024]{1,0:T(8,128)(2,1)}, u32[]{:S(2)}, u32[]{:S(2)}) collective-permute-start(bf16[200,1024]{1,0:T(8,128)(2,1)} %param.13), channel_id=1, source_target_pairs={{4,0},{29,1},{8,4},{1,5},{12,8},{5,9},{16,12},{9,13},{20,16},{13,1... | collective-permute-start | bytes 1228808 | tf_op jit(solution)/shard_map/ppermute | solution.py:271
  6.7 5.7 %copy-start.10 = (bf16[200,1024]{1,0:T(8,128)(2,1)S(1)}, bf16[200,1024]{1,0:T(8,128)(2,1)}, u32[]{:S(2)}) copy-start(bf16[200,1024]{1,0:T(8,128)(2,1)} %param.13) | copy-start | bytes 1228804
  12.4 36.4 %copy-start.12 = (s32[8]{0:T(128)S(1)}, s32[8]{0:T(128)}, u32[]{:S(2)}) copy-start(s32[8]{0:T(128)} %constant.182.clone) | copy-start | bytes 100
  12.4 36.3 %copy-start.13 = (s32[8]{0:T(128)S(1)}, s32[8]{0:T(128)}, u32[]{:S(2)}) copy-start(s32[8]{0:T(128)} %constant.184) | copy-start | bytes 100
  15.6 32.9 %all-to-all-start = ((bf16[8,64,1664]{2,1,0:T(8,128)(2,1)}), bf16[8,64,1664]{2,1,0:T(8,128)(2,1)}, u32[]{:S(2)}, u32[]{:S(2)}) async-start(bf16[8,64,1664]{2,1,0:T(8,128)(2,1)} %vision_norm.1), calls=%async_computation | async-start | bytes 3407872 | tf_op jit(solution)/shard_map/all_to_all | solution.py:341
  21.4 13.6 %collective-permute-start.2 = (bf16[200,1024]{1,0:T(8,128)(2,1)}, bf16[200,1024]{1,0:T(8,128)(2,1)}, u32[]{:S(2)}, u32[]{:S(2)}) collective-permute-start(bf16[200,1024]{1,0:T(8,128)(2,1)} %collective-permute-done), channel_id=1, source_target_pairs={{0,4},{1,29},{4,8},{5,1},{8,12},{9,5},{12,16},{13,9},{16,20},{17,1... | collective-permute-start | bytes 1228808 | tf_op jit(solution)/shard_map/ppermute | solution.py:270
  21.4 13.6 %collective-permute-start.3 = (bf16[200,1024]{1,0:T(8,128)(2,1)}, bf16[200,1024]{1,0:T(8,128)(2,1)}, u32[]{:S(2)}, u32[]{:S(2)}) collective-permute-start(bf16[200,1024]{1,0:T(8,128)(2,1)} %collective-permute-done.1), channel_id=1, source_target_pairs={{4,0},{29,1},{8,4},{1,5},{12,8},{5,9},{16,12},{9,13},{20,16},{13,1... | collective-permute-start | bytes 1228808 | tf_op jit(solution)/shard_map/ppermute | solution.py:271
  35.0 13.4 %collective-permute-start.4 = (bf16[200,1024]{1,0:T(8,128)(2,1)}, bf16[200,1024]{1,0:T(8,128)(2,1)}, u32[]{:S(2)}, u32[]{:S(2)}) collective-permute-start(bf16[200,1024]{1,0:T(8,128)(2,1)} %collective-permute-done.2), channel_id=1, source_target_pairs={{0,4},{1,29},{4,8},{5,1},{8,12},{9,5},{12,16},{13,9},{16,20},{17,1... | collective-permute-start | bytes 1228808 | tf_op jit(solution)/shard_map/ppermute | solution.py:270
  35.0 13.4 %collective-permute-start.5 = (bf16[200,1024]{1,0:T(8,128)(2,1)}, bf16[200,1024]{1,0:T(8,128)(2,1)}, u32[]{:S(2)}, u32[]{:S(2)}) collective-permute-start(bf16[200,1024]{1,0:T(8,128)(2,1)} %collective-permute-done.3), channel_id=1, source_target_pairs={{4,0},{29,1},{8,4},{1,5},{12,8},{5,9},{16,12},{9,13},{20,16},{13,1... | collective-permute-start | bytes 1228808 | tf_op jit(solution)/shard_map/ppermute | solution.py:271
  48.5 6.0 %collective-permute-start.6 = (bf16[8,64,1664]{2,1,0:T(8,128)(2,1)}, bf16[8,64,1664]{2,1,0:T(8,128)(2,1)}, u32[]{:S(2)}, u32[]{:S(2)}) collective-permute-start(bf16[8,64,1664]{2,1,0:T(8,128)(2,1)} %all-to-all-done.rows_ref), channel_id=1, source_target_pairs={{0,1},{1,0},{2,3},{3,2},{4,5},{5,4},{6,7},{7,6},{8,9},{9,8},{10,11... | collective-permute-start | bytes 5111816 | tf_op jit(solution)/shard_map/ppermute | solution.py:343
  48.8 9.5 %collective-permute-start.7 = (bf16[200,1024]{1,0:T(8,128)(2,1)}, bf16[200,1024]{1,0:T(8,128)(2,1)S(1)}, u32[]{:S(2)}, u32[]{:S(2)}) collective-permute-start(bf16[200,1024]{1,0:T(8,128)(2,1)} %collective-permute-done.4), channel_id=1, source_target_pairs={{0,4},{1,29},{4,8},{5,1},{8,12},{9,5},{12,16},{13,9},{16,20},{17,1... | collective-permute-start | bytes 1228808 | tf_op jit(solution)/shard_map/ppermute | solution.py:277
  60.5 11.4 %copy-start.9 = (f32[1024]{0:T(1024)S(1)}, f32[1024]{0:T(1024)}, u32[]{:S(2)}) copy-start(f32[1024]{0:T(1024)} %param.15) | copy-start | bytes 12292
  60.5 36.0 %all-to-all-start.1 = ((bf16[8,128,1024]{2,1,0:T(8,128)(2,1)}), bf16[8,128,1024]{2,1,0:T(8,128)(2,1)}, u32[]{:S(2)}, u32[]{:S(2)}) async-start(bf16[8,128,1024]{2,1,0:T(8,128)(2,1)} %tail.1), calls=%async_computation.1 | async-start | bytes 4194304 | tf_op jit(solution)/shard_map/all_to_all | solution.py:394
  66.6 0.6 copy-start.11
  71.9 1.0 copy-start.1
  72.8 0.9 copy-start.6
  96.5 1.0 copy-start.5
  99.9 33.7 %copy-start.3 = (bf16[128,1024]{1,0:T(8,128)(2,1)}, bf16[128,1024]{1,0:T(8,128)(2,1)S(1)}, u32[]{:S(2)}) copy-start(bf16[128,1024]{1,0:T(8,128)(2,1)S(1)} %get-tuple-element.57.feature_ref) | copy-start | bytes 786436
  99.9 4.6 %collective-permute-start.10 = (f32[8,128]{1,0:T(8,128)S(1)}, f32[8,128]{1,0:T(8,128)S(1)}, u32[]{:S(2)}, u32[]{:S(2)}) collective-permute-start(f32[8,128]{1,0:T(8,128)S(1)} %get-tuple-element.58.refs_0_), channel_id=1, source_target_pairs={{0,3},{1,2},{2,1},{3,0},{4,7},{5,6},{6,5},{7,4},{8,11},{9,10},{10,... | collective-permute-start | bytes 12296 | tf_op jit(solution)/shard_map/ppermute | solution.py:461
  100.9 3.6 %collective-permute-start.8 = (f32[8,128]{1,0:T(8,128)S(1)}, f32[8,128]{1,0:T(8,128)S(1)}, u32[]{:S(2)}, u32[]{:S(2)}) collective-permute-start(f32[8,128]{1,0:T(8,128)S(1)} %get-tuple-element.58.refs_0_), channel_id=1, source_target_pairs={{0,1},{1,0},{2,3},{3,2},{4,5},{5,4},{6,7},{7,6},{8,9},{9,8},{10,11... | collective-permute-start | bytes 12296 | tf_op jit(solution)/shard_map/ppermute | solution.py:461
  102.4 5.1 %collective-permute-start.9 = (f32[8,128]{1,0:T(8,128)S(1)}, f32[8,128]{1,0:T(8,128)S(1)}, u32[]{:S(2)}, u32[]{:S(2)}) collective-permute-start(f32[8,128]{1,0:T(8,128)S(1)} %get-tuple-element.58.refs_0_), channel_id=1, source_target_pairs={{0,2},{1,3},{2,0},{3,1},{4,6},{5,7},{6,4},{7,5},{8,10},{9,11},{10,... | collective-permute-start | bytes 12296 | tf_op jit(solution)/shard_map/ppermute | solution.py:461
  108.4 7.7 %collective-permute-start.11 = (bf16[8,16,1024]{2,1,0:T(8,128)(2,1)S(1)}, bf16[8,16,1024]{2,1,0:T(8,128)(2,1)S(1)}, u32[]{:S(2)}, u32[]{:S(2)}) collective-permute-start(bf16[8,16,1024]{2,1,0:T(8,128)(2,1)S(1)} %grads.1.refs_0_), channel_id=1, source_target_pairs={{0,128},{32,160},{64,192},{96,224},{128,0},{160,32},{192,64},{224,... | collective-permute-start | bytes 786440 | tf_op jit(solution)/shard_map/ppermute | solution.py:477
  110.7 6.8 %collective-permute-start.12 = (bf16[8,16,1024]{2,1,0:T(8,128)(2,1)S(1)}, bf16[8,16,1024]{2,1,0:T(8,128)(2,1)S(1)}, u32[]{:S(2)}, u32[]{:S(2)}) collective-permute-start(bf16[8,16,1024]{2,1,0:T(8,128)(2,1)S(1)} %grads.1.refs_0_), channel_id=1, source_target_pairs={{0,96},{32,0},{64,32},{96,64},{128,224},{160,128},{192,160},{224,1... | collective-permute-start | bytes 786440 | tf_op jit(solution)/shard_map/ppermute | solution.py:477
  110.7 8.8 %collective-permute-start.13 = (bf16[8,16,1024]{2,1,0:T(8,128)(2,1)S(1)}, bf16[8,16,1024]{2,1,0:T(8,128)(2,1)S(1)}, u32[]{:S(2)}, u32[]{:S(2)}) collective-permute-start(bf16[8,16,1024]{2,1,0:T(8,128)(2,1)S(1)} %grads.1.refs_0_), channel_id=1, source_target_pairs={{0,32},{32,64},{64,96},{96,0},{128,160},{160,192},{192,224},{224,1... | collective-permute-start | bytes 786440 | tf_op jit(solution)/shard_map/ppermute | solution.py:477
  117.5 7.2 %collective-permute-start.15 = (bf16[8,16,1024]{2,1,0:T(8,128)(2,1)S(1)}, bf16[8,16,1024]{2,1,0:T(8,128)(2,1)S(1)}, u32[]{:S(2)}, u32[]{:S(2)}) collective-permute-start(bf16[8,16,1024]{2,1,0:T(8,128)(2,1)S(1)} %collective-permute-done.11.refs_1_), channel_id=1, source_target_pairs={{0,96},{32,0},{64,32},{96,64},{128,224},{160,128},{192,160},{224,1... | collective-permute-start | bytes 786440 | tf_op jit(solution)/shard_map/ppermute | solution.py:477
  119.0 9.9 %collective-permute-start.14 = (bf16[8,16,1024]{2,1,0:T(8,128)(2,1)S(1)}, bf16[8,16,1024]{2,1,0:T(8,128)(2,1)S(1)}, u32[]{:S(2)}, u32[]{:S(2)}) collective-permute-start(bf16[8,16,1024]{2,1,0:T(8,128)(2,1)S(1)} %collective-permute-done.11.refs_1_), channel_id=1, source_target_pairs={{0,32},{32,64},{64,96},{96,0},{128,160},{160,192},{192,224},{224,1... | collective-permute-start | bytes 786440 | tf_op jit(solution)/shard_map/ppermute | solution.py:477
  119.6 12.2 %collective-permute-start.16 = (bf16[8,16,1024]{2,1,0:T(8,128)(2,1)S(1)}, bf16[8,16,1024]{2,1,0:T(8,128)(2,1)S(1)}, u32[]{:S(2)}, u32[]{:S(2)}) collective-permute-start(bf16[8,16,1024]{2,1,0:T(8,128)(2,1)S(1)} %collective-permute-done.13.refs_2_), channel_id=1, source_target_pairs={{0,32},{32,64},{64,96},{96,0},{128,160},{160,192},{192,224},{224,1... | collective-permute-start | bytes 786440 | tf_op jit(solution)/shard_map/ppermute | solution.py:477
  124.7 7.0 %collective-permute-start.17 = (bf16[8,16,1024]{2,1,0:T(8,128)(2,1)S(1)}, bf16[8,16,1024]{2,1,0:T(8,128)(2,1)S(1)}, u32[]{:S(2)}, u32[]{:S(2)}) collective-permute-start(bf16[8,16,1024]{2,1,0:T(8,128)(2,1)S(1)} %collective-permute-done.15.refs_5_), channel_id=1, source_target_pairs={{0,96},{32,0},{64,32},{96,64},{128,224},{160,128},{192,160},{224,1... | collective-permute-start | bytes 786440 | tf_op jit(solution)/shard_map/ppermute | solution.py:477
  134.7 2.9 %collective-permute-start.19 = (bf16[256,1664]{1,0:T(8,128)(2,1)S(1)}, bf16[256,1664]{1,0:T(8,128)(2,1)S(1)}, u32[]{:S(2)}, u32[]{:S(2)}) collective-permute-start(bf16[256,1664]{1,0:T(8,128)(2,1)S(1)} %give1.1), channel_id=1, source_target_pairs={{0,1},{1,0},{2,3},{3,2},{4,5},{5,4},{6,7},{7,6},{8,9},{9,8},{10,11... | collective-permute-start | bytes 2555912 | tf_op jit(solution)/shard_map/ppermute | solution.py:523
  134.8 3.6 %collective-permute-start.18 = (bf16[256,1664]{1,0:T(8,128)(2,1)S(1)}, bf16[256,1664]{1,0:T(8,128)(2,1)S(1)}, u32[]{:S(2)}, u32[]{:S(2)}) collective-permute-start(bf16[256,1664]{1,0:T(8,128)(2,1)S(1)} %give0.1), channel_id=1, source_target_pairs={{0,1},{1,0},{2,3},{3,2},{4,5},{5,4},{6,7},{7,6},{8,9},{9,8},{10,11... | collective-permute-start | bytes 2555912 | tf_op jit(solution)/shard_map/ppermute | solution.py:523
  139.8 30.0 %copy-start = (f32[32,12800]{1,0:T(8,128)S(1)}, f32[32,12800]{1,0:T(8,128)}, u32[]{:S(2)}) copy-start(f32[32,12800]{1,0:T(8,128)} %get-tuple-element.63.hat_ref) | copy-start | bytes 4915204
  139.8 30.0 %copy-start.7 = (f32[12800]{0:T(1024)S(1)}, f32[12800]{0:T(1024)}, u32[]{:S(2)}) copy-start(f32[12800]{0:T(1024)} %gain_ref.3) | copy-start | bytes 153604
  139.8 30.0 %copy-start.8 = (f32[32,128]{1,0:T(8,128)S(1)}, f32[32,128]{1,0:T(8,128)}, u32[]{:S(2)}) copy-start(f32[32,128]{1,0:T(8,128)} %get-tuple-element.48.inv_ref) | copy-start | bytes 49156
  139.8 30.0 %all-to-all-start.2 = ((bf16[16,32,1664]{2,1,0:T(8,128)(2,1)}), bf16[16,32,1664]{2,1,0:T(8,128)(2,1)S(1)}, u32[]{:S(2)}, u32[]{:S(2)}) async-start(bf16[16,32,1664]{2,1,0:T(8,128)(2,1)} %join.1), calls=%async_computation.2 | async-start | bytes 3407872 | tf_op jit(solution)/shard_map/all_to_all | solution.py:536
  145.2 0.9 copy-start.2
  146.1 0.9 copy-start.4
